TPU v7x, 512 devices: a whole 4x8x8 slice. The times are simulated.
512 devices in a mesh: lon: 32 (over x, y), lat: 16 (over z, core).
Axes of the slice: x: 4, y: 8, z: 8, core: 2. Of those that a mesh axis runs over, the one named last changes fastest.
Arguments:
- spectra: bfloat16 [2, 33, 128, 20480], P(None, None, 'lat', 'lon'), may hold values from 0.049804688 to 1
- supersat: bfloat16 [2, 128, 20480], P(None, 'lat', 'lon'), may hold values from -3 to 3
- cloud_flags: int32 [20480], P('lon'), may hold values from 0 to 1, as said below
- pair_kernel: bfloat16 [33, 33, 33], replicated, may hold values from -0.1875 to 0.1875
- rime_kernel: bfloat16 [33, 33, 33], replicated, may hold values from -0.1875 to 0.1875
- growth_matrix: bfloat16 [2, 33, 33], replicated, may hold values from -1 to 1
- fall_speed: float32 [2, 33], replicated, may hold values from 0.3 to 30
- density_factor: float32 [128], replicated, may hold values from 0.5 to 2
Outputs:
- tendency: bfloat16 [2, 33, 128, 20480], P(None, None, 'lat', 'lon')
Inputs may be any that keep to these rules, and one draw needn't show every extreme that they name: `cloud_flags`: 1 marks a column that takes part in collisions, 0 a clear one.
All inputs are finite; a program needn't handle non-finite values.
Results may differ from a plain program's by a relative error of at most 0.005.
Values may be sent and summed in bfloat16 or wider, within the bound.
No kernel may reach another device: no remote copies, remote signals or barrier semaphores. Data moves between devices by JAX's collectives and lax.ppermute only.
A program may use at most 128 MiB of HBM per device.

v0:
```python
import math

import jax
import jax.numpy as jnp
from jax import lax
from jax.sharding import PartitionSpec as P

ITERS = 2


time_step = 1.0


def settling_matrix(fall_speed, density_factor):
    courant = time_step * fall_speed.reshape(-1)[:, None] * density_factor[None, :]
    ratios = courant[:, :-1] / (1.0 + courant[:, 1:])
    log_sums = jnp.concatenate(
        [jnp.zeros((courant.shape[0], 1), jnp.float32), jnp.cumsum(jnp.log(ratios), axis=1)], axis=1
    )
    level_index = jnp.arange(courant.shape[1], dtype=jnp.int32)
    below_mask = level_index[:, None] >= level_index[None, :]
    spread = jnp.where(below_mask[None], log_sums[:, :, None] - log_sums[:, None, :], 0.0)
    return jnp.where(below_mask[None], jnp.exp(spread), 0.0) / (1.0 + courant[:, None, :])


def pair_gains(col_block, pair_kernel, rime_kernel):
    bin_count = pair_kernel.shape[0]
    flat_rows = col_block.reshape(2 * bin_count, -1)
    liquid = flat_rows[:bin_count]
    frozen = flat_rows[bin_count:]
    pair_terms = jnp.dot(
        pair_kernel.reshape(bin_count * bin_count, bin_count),
        liquid,
        preferred_element_type=jnp.float32,
    )
    pair_terms = pair_terms.astype(jnp.bfloat16).reshape(bin_count, bin_count, -1)
    rime_terms = jnp.dot(
        rime_kernel.reshape(bin_count * bin_count, bin_count),
        frozen,
        preferred_element_type=jnp.float32,
    )
    rime_terms = rime_terms.astype(jnp.bfloat16).reshape(bin_count, bin_count, -1)
    liquid_gain = jnp.einsum("kir,ir->kr", pair_terms, liquid, preferred_element_type=jnp.float32)
    frozen_gain = jnp.einsum("kir,ir->kr", rime_terms, liquid, preferred_element_type=jnp.float32)
    return jnp.concatenate([liquid_gain, frozen_gain], axis=0).reshape(col_block.shape)


def collide_packed(rounded, cloudy, pair_kernel, rime_kernel):
    channels, col_count, levels = rounded.shape
    flag_ints = (cloudy > 0.5).astype(jnp.int32)
    order = jnp.argsort(1 - flag_ints, stable=True)
    inverse = jnp.argsort(order, stable=True)
    cloudy_count = jnp.sum(flag_ints)
    packed = jnp.take(rounded, order, axis=1)
    packed_flags = jnp.take(cloudy, order, axis=0)
    block_width = math.gcd(col_count, max(8, 1024 // levels))
    block_count = col_count // block_width

    def one_block(block_index):
        first_col = block_index * block_width
        col_block = lax.dynamic_slice_in_dim(packed, first_col, block_width, 1)
        block_flags = lax.dynamic_slice_in_dim(packed_flags, first_col, block_width, 0)

        def collide():
            return pair_gains(col_block, pair_kernel, rime_kernel) * block_flags[None, :, None]

        def nothing():
            return jnp.zeros((channels, block_width, levels), jnp.float32)

        return lax.cond(first_col < cloudy_count, collide, nothing)

    gathered = lax.map(one_block, jnp.arange(block_count, dtype=jnp.int32))
    ordered = jnp.moveaxis(gathered, 0, 1).reshape(channels, col_count, levels)
    return jnp.take(ordered, inverse, axis=1)


def local(
    spectra,
    supersat,
    cloud_flags,
    pair_kernel,
    rime_kernel,
    growth_matrix,
    fall_speed,
    density_factor,
):
    species, bin_count, dyn_levels, dyn_cols = spectra.shape
    packed_state = spectra.reshape(species * bin_count, dyn_levels, dyn_cols)
    flag_plane = jnp.broadcast_to(
        cloud_flags.astype(jnp.bfloat16)[None, None, :], (1, dyn_levels, dyn_cols)
    )
    group_state, group_sat, group_flags = (
        lax.all_to_all(packed_state, "lat", split_axis=2, concat_axis=1, tiled=True),
        lax.all_to_all(supersat, "lat", split_axis=2, concat_axis=1, tiled=True),
        lax.all_to_all(flag_plane, "lat", split_axis=2, concat_axis=1, tiled=True),
    )
    channels, levels, col_count = group_state.shape
    initial = jnp.transpose(group_state, (0, 2, 1)).astype(jnp.float32)
    saturation = jnp.transpose(group_sat, (0, 2, 1)).astype(jnp.float32)
    flag_row = group_flags[0, 0, :]
    cloudy = flag_row.astype(jnp.float32)
    settle = settling_matrix(fall_speed, density_factor)
    spectrum = initial
    for substep in range(ITERS):
        rounded = spectrum.astype(jnp.bfloat16)
        collided = collide_packed(rounded, cloudy, pair_kernel, rime_kernel)
        growth = jnp.einsum(
            "skj,sjcl->skcl",
            growth_matrix,
            rounded.reshape(species, bin_count, col_count, levels),
            preferred_element_type=jnp.float32,
        )
        growth = growth * saturation[:, None]
        spectrum = spectrum + time_step * (collided + growth.reshape(channels, col_count, levels))
        spectrum = jnp.einsum("blm,bcm->bcl", settle, spectrum, precision=lax.Precision.HIGHEST)
    tendency = ((spectrum - initial) / (ITERS * time_step)).astype(jnp.bfloat16)
    level_major = jnp.transpose(tendency, (0, 2, 1))
    returned = lax.all_to_all(level_major, "lat", split_axis=1, concat_axis=2, tiled=True)
    return returned.reshape(species, bin_count, dyn_levels, dyn_cols)


def solution(mesh):
    return jax.shard_map(
        local,
        mesh=mesh,
        in_specs=(
            P(None, None, "lat", "lon"),
            P(None, "lat", "lon"),
            P("lon"),
            P(),
            P(),
            P(),
            P(),
            P(),
        ),
        out_specs=P(None, None, "lat", "lon"),
        check_vma=False,
    )
```

profile of v0, /device:TPU:1, one launch (start us, length us, event | category | flops | bytes accessed | tf_op | source)
XLA Modules:
  0.0 392.9 jit_solution(9734227957836375675)
XLA Ops:
  5.9 11.8 %all-to-all-start.1 = ((bf16[16,2,160]{2,1,0:T(2,128)(2,1)}), bf16[16,2,160]{2,1,0:T(2,128)(2,1)S(1)}, u32[]{:S(2)}, u32[]{:S(2)}) async-start(bf16[16,2,160]{2,1,0:T(2,128)(2,1)} %reshape.267), calls=%async_computation.1 | async-start | bytes 32768 | tf_op jit(solution)/shard_map/all_to_all | solution.py:95
  19.9 2.9 copy.137
  27.3 7.2 %all-to-all-start.2 = ((bf16[16,2,320]{2,1,0:T(2,128)(2,1)}), bf16[16,2,320]{2,1,0:T(2,128)(2,1)S(1)}, u32[]{:S(2)}, u32[]{:S(2)}) async-start(bf16[16,2,320]{2,1,0:T(2,128)(2,1)} %reshape.265), calls=%async_computation.2 | async-start | bytes 49152 | tf_op jit(solution)/shard_map/all_to_all | solution.py:94
  41.9 5.7 %all-to-all-start = ((bf16[66,8,640]{0,1,2:T(8,128)(2,1)}), bf16[66,8,640]{0,1,2:T(8,128)(2,1)S(1)}, u32[]{:S(2)}, u32[]{:S(2)}) async-start(bf16[66,8,640]{0,1,2:T(8,128)(2,1)} %copy.137), calls=%async_computation | async-start | bytes 2621440 | tf_op jit(solution)/shard_map/all_to_all | solution.py:93
  48.9 31.7 %all-to-all-done = bf16[66,8,640]{0,1,2:T(8,128)(2,1)S(1)} async-done(((bf16[66,8,640]{0,1,2:T(8,128)(2,1)}), bf16[66,8,640]{0,1,2:T(8,128)(2,1)S(1)}, u32[]{:S(2)}, u32[]{:S(2)}) %all-to-all-start) | async-done | bytes 675872 | tf_op jit(solution)/shard_map/all_to_all | solution.py:93
  86.1 91.3 %while.20 = (s32[]{:T(128)}, f32[5,66,8,128]{1,3,2,0:T(8,128)}, s32[5]{0:T(128)S(1)}, s32[]{:T(128)}, bf16[66,40,128]{2,1,0:T(8,128)(2,1)}, /*index=5*/bf16[33,3...) while((s32[]{:T(128)}, f32[5,66,8,128]{1,3,2,0:T(8,128)}, ...), condition=%wide.region_6.9_spmd, body=%wide.region_3.8_spmd.sunk | while | flops 156220416 | bytes 22618888 | solution.py:72
  87.9 19.5 %conditional.4 = (f32[1,66,8,128]{1,3,2,0:T(8,128)S(1)}) conditional(s32[]{:T(128)} %convert_element_type.125, () %tuple.85, (s32[]{:T(128)}, bf16[66,40,128]{2,1,0:T(8,128)(2,1)}, bf16[33,33,33]{1,0,2:T(8,128)(2,1)}, bf16[33,33,33]{1,0,2:T(8,128)(2,1)}, f32[40]{0:T(128)S(1)}) %tuple.86), branch_computations={%region_4.6_spmd, %region_5.7_spmd} | conditional | flops 156220416 | bytes 21823574 | solution.py:70
  92.5 3.4 reshape.172
  96.2 2.2 fusion.1
  98.4 4.5 %reshape.174 = bf16[33,33,1024]{2,1,0:T(8,128)(2,1)} reshape(bf16[1089,1024]{1,0:T(8,128)(2,1)} %fusion.1) | data formatting | bytes 4460544 | tf_op jit(solution)/shard_map/while/body/eval_jaxpr/cond/branch_1_fun/reshape | solution.py:42
  102.9 3.6 multiply_reduce_fusion.1
  110.1 19.5 %conditional.4 = (f32[1,66,8,128]{1,3,2,0:T(8,128)S(1)}) conditional(s32[]{:T(128)} %convert_element_type.125, () %tuple.85, (s32[]{:T(128)}, bf16[66,40,128]{2,1,0:T(8,128)(2,1)}, bf16[33,33,33]{1,0,2:T(8,128)(2,1)}, bf16[33,33,33]{1,0,2:T(8,128)(2,1)}, f32[40]{0:T(128)S(1)}) %tuple.86), branch_computations={%region_4.6_spmd, %region_5.7_spmd} | conditional | flops 156220416 | bytes 21823574 | solution.py:70
  114.6 3.4 reshape.172
  120.6 4.5 %reshape.174 = bf16[33,33,1024]{2,1,0:T(8,128)(2,1)} reshape(bf16[1089,1024]{1,0:T(8,128)(2,1)} %fusion.1) | data formatting | bytes 4460544 | tf_op jit(solution)/shard_map/while/body/eval_jaxpr/cond/branch_1_fun/reshape | solution.py:42
  125.1 3.6 multiply_reduce_fusion.1
  132.2 19.5 %conditional.4 = (f32[1,66,8,128]{1,3,2,0:T(8,128)S(1)}) conditional(s32[]{:T(128)} %convert_element_type.125, () %tuple.85, (s32[]{:T(128)}, bf16[66,40,128]{2,1,0:T(8,128)(2,1)}, bf16[33,33,33]{1,0,2:T(8,128)(2,1)}, bf16[33,33,33]{1,0,2:T(8,128)(2,1)}, f32[40]{0:T(128)S(1)}) %tuple.86), branch_computations={%region_4.6_spmd, %region_5.7_spmd} | conditional | flops 156220416 | bytes 21823574 | solution.py:70
  136.8 3.4 reshape.172
  142.7 4.5 %reshape.174 = bf16[33,33,1024]{2,1,0:T(8,128)(2,1)} reshape(bf16[1089,1024]{1,0:T(8,128)(2,1)} %fusion.1) | data formatting | bytes 4460544 | tf_op jit(solution)/shard_map/while/body/eval_jaxpr/cond/branch_1_fun/reshape | solution.py:42
  147.2 3.6 multiply_reduce_fusion.1
  154.3 19.5 %conditional.4 = (f32[1,66,8,128]{1,3,2,0:T(8,128)S(1)}) conditional(s32[]{:T(128)} %convert_element_type.125, () %tuple.85, (s32[]{:T(128)}, bf16[66,40,128]{2,1,0:T(8,128)(2,1)}, bf16[33,33,33]{1,0,2:T(8,128)(2,1)}, bf16[33,33,33]{1,0,2:T(8,128)(2,1)}, f32[40]{0:T(128)S(1)}) %tuple.86), branch_computations={%region_4.6_spmd, %region_5.7_spmd} | conditional | flops 156220416 | bytes 21823574 | solution.py:70
  158.9 3.4 reshape.172
  164.9 4.5 %reshape.174 = bf16[33,33,1024]{2,1,0:T(8,128)(2,1)} reshape(bf16[1089,1024]{1,0:T(8,128)(2,1)} %fusion.1) | data formatting | bytes 4460544 | tf_op jit(solution)/shard_map/while/body/eval_jaxpr/cond/branch_1_fun/reshape | solution.py:42
  169.4 3.6 multiply_reduce_fusion.1
  178.0 3.1 copy.147
  188.3 10.1 %fusion.32 = (bf16[66,40,128]{2,1,0:T(8,128)(2,1)S(1)}, f32[66,40,128]{2,1,0:T(8,128)}) fusion(f32[66,40,128]{2,1,0:T(8,128)S(1)} %fusion.20, f32[66,128]{1,0:T(8,128)S(1)} %copy-done.11, f32[66,128]{1,0:T(8,128)S(1)} %copy-done.13, pred[128,128]{1,0:T(8,128)(4,1)S(1)} %iota_compare_fusion), kind=kOutput, calls=%fused_computation.80 | convolution fusion | flops 523708416 | bytes 3463168 | tf_op jit(solution)/shard_map/blm,bcm->bcl/dot_general | solution.py:115
  202.9 91.3 %while.21 = (s32[]{:T(128)}, f32[5,66,8,128]{1,3,2,0:T(8,128)}, s32[5]{0:T(128)S(1)}, s32[]{:T(128)}, bf16[66,40,128]{2,1,0:T(8,128)(2,1)}, /*index=5*/bf16[33,3...) while((s32[]{:T(128)}, f32[5,66,8,128]{1,3,2,0:T(8,128)}, ...), condition=%wide.region_11.15_spmd, body=%wide.region_8.14_spmd.sunk | while | flops 156220416 | bytes 22618888 | solution.py:72
  204.7 19.5 %conditional.5 = (f32[1,66,8,128]{1,3,2,0:T(8,128)S(1)}) conditional(s32[]{:T(128)} %convert_element_type.126, () %tuple.88, (s32[]{:T(128)}, bf16[66,40,128]{2,1,0:T(8,128)(2,1)}, bf16[33,33,33]{1,0,2:T(8,128)(2,1)}, bf16[33,33,33]{1,0,2:T(8,128)(2,1)}, f32[40]{0:T(128)S(1)}) %tuple.89), branch_computations={%region_9.12_spmd, %region_10.13_spmd} | conditional | flops 156220416 | bytes 21823574 | solution.py:70
  209.2 3.4 reshape.177
  215.2 4.5 %reshape.179 = bf16[33,33,1024]{2,1,0:T(8,128)(2,1)} reshape(bf16[1089,1024]{1,0:T(8,128)(2,1)} %fusion.3) | data formatting | bytes 4460544 | tf_op jit(solution)/shard_map/while/body/eval_jaxpr/cond/branch_1_fun/reshape | solution.py:42
  219.7 3.6 multiply_reduce_fusion.3
  226.8 19.5 %conditional.5 = (f32[1,66,8,128]{1,3,2,0:T(8,128)S(1)}) conditional(s32[]{:T(128)} %convert_element_type.126, () %tuple.88, (s32[]{:T(128)}, bf16[66,40,128]{2,1,0:T(8,128)(2,1)}, bf16[33,33,33]{1,0,2:T(8,128)(2,1)}, bf16[33,33,33]{1,0,2:T(8,128)(2,1)}, f32[40]{0:T(128)S(1)}) %tuple.89), branch_computations={%region_9.12_spmd, %region_10.13_spmd} | conditional | flops 156220416 | bytes 21823574 | solution.py:70
  231.4 3.4 reshape.177
  237.4 4.5 %reshape.179 = bf16[33,33,1024]{2,1,0:T(8,128)(2,1)} reshape(bf16[1089,1024]{1,0:T(8,128)(2,1)} %fusion.3) | data formatting | bytes 4460544 | tf_op jit(solution)/shard_map/while/body/eval_jaxpr/cond/branch_1_fun/reshape | solution.py:42
  241.9 3.6 multiply_reduce_fusion.3
  249.0 19.5 %conditional.5 = (f32[1,66,8,128]{1,3,2,0:T(8,128)S(1)}) conditional(s32[]{:T(128)} %convert_element_type.126, () %tuple.88, (s32[]{:T(128)}, bf16[66,40,128]{2,1,0:T(8,128)(2,1)}, bf16[33,33,33]{1,0,2:T(8,128)(2,1)}, bf16[33,33,33]{1,0,2:T(8,128)(2,1)}, f32[40]{0:T(128)S(1)}) %tuple.89), branch_computations={%region_9.12_spmd, %region_10.13_spmd} | conditional | flops 156220416 | bytes 21823574 | solution.py:70
  253.5 3.4 reshape.177
  259.5 4.5 %reshape.179 = bf16[33,33,1024]{2,1,0:T(8,128)(2,1)} reshape(bf16[1089,1024]{1,0:T(8,128)(2,1)} %fusion.3) | data formatting | bytes 4460544 | tf_op jit(solution)/shard_map/while/body/eval_jaxpr/cond/branch_1_fun/reshape | solution.py:42
  264.0 3.6 multiply_reduce_fusion.3
  271.1 19.5 %conditional.5 = (f32[1,66,8,128]{1,3,2,0:T(8,128)S(1)}) conditional(s32[]{:T(128)} %convert_element_type.126, () %tuple.88, (s32[]{:T(128)}, bf16[66,40,128]{2,1,0:T(8,128)(2,1)}, bf16[33,33,33]{1,0,2:T(8,128)(2,1)}, bf16[33,33,33]{1,0,2:T(8,128)(2,1)}, f32[40]{0:T(128)S(1)}) %tuple.89), branch_computations={%region_9.12_spmd, %region_10.13_spmd} | conditional | flops 156220416 | bytes 21823574 | solution.py:70
  275.7 3.4 reshape.177
  279.4 2.2 fusion.3
  281.6 4.5 %reshape.179 = bf16[33,33,1024]{2,1,0:T(8,128)(2,1)} reshape(bf16[1089,1024]{1,0:T(8,128)(2,1)} %fusion.3) | data formatting | bytes 4460544 | tf_op jit(solution)/shard_map/while/body/eval_jaxpr/cond/branch_1_fun/reshape | solution.py:42
  286.1 3.6 multiply_reduce_fusion.3
  294.2 2.4 copy.159
  300.2 9.2 %fusion.18 = bf16[66,128,40]{1,2,0:T(8,128)(2,1)S(1)} fusion(f32[66,40,128]{2,1,0:T(8,128)S(1)} %fusion.19, f32[66,128]{1,0:T(8,128)S(1)} %copy-done.12, f32[66,128]{1,0:T(8,128)S(1)} %copy-done.14, pred[128,128]{1,0:T(8,128)(4,1)S(1)} %iota_compare_fusion, bf16[66,128,40]{1,2,0:T(8,128)(2,1)S(1)} %copy-done.5), kind=kOutput, calls=%fused_computation.46 | convolution fusion | flops 524722176 | bytes 2787328 | tf_op jit(solution)/shard_map/blm,bcm->bcl/dot_general | solution.py:115
  310.8 75.8 %all_to_all.60 = bf16[66,128,40]{0,2,1:T(8,128)(2,1)S(1)} all-to-all(bf16[66,128,40]{0,2,1:T(8,128)(2,1)S(1)} %copy.166), channel_id=1, replica_groups=mesh['lon'=32,'lat'=16] {'lat'}, dimensions={1} | all-to-all | bytes 1351680 | tf_op jit(solution)/shard_map/all_to_all | solution.py:118
  386.6 2.9 copy.167
  389.5 3.2 reshape.196
  (250 shorter events, 116.3 us)
Async XLA Ops:
  0.0 22.9 %copy-start.8 = (bf16[33,33,33]{2,1,0:T(8,128)(2,1)S(1)}, bf16[33,33,33]{2,1,0:T(8,128)(2,1)}, u32[]{:S(2)}) copy-start(bf16[33,33,33]{2,1,0:T(8,128)(2,1)} %param.25) | copy-start | bytes 215626
  0.0 24.0 %copy-start.9 = (bf16[33,33,33]{2,1,0:T(8,128)(2,1)S(1)}, bf16[33,33,33]{2,1,0:T(8,128)(2,1)}, u32[]{:S(2)}) copy-start(bf16[33,33,33]{2,1,0:T(8,128)(2,1)} %param.26) | copy-start | bytes 215626
  0.8 24.4 %copy-start.15 = (bf16[2,8,640]{2,1,0:T(8,128)(2,1)S(1)}, bf16[2,8,640]{2,1,0:T(8,128)(2,1)}, u32[]{:S(2)}) copy-start(bf16[2,8,640]{2,1,0:T(8,128)(2,1)} %param.23) | copy-start | bytes 61444
  5.9 21.4 %all-to-all-start.1 = ((bf16[16,2,160]{2,1,0:T(2,128)(2,1)}), bf16[16,2,160]{2,1,0:T(2,128)(2,1)S(1)}, u32[]{:S(2)}, u32[]{:S(2)}) async-start(bf16[16,2,160]{2,1,0:T(2,128)(2,1)} %reshape.267), calls=%async_computation.1 | async-start | bytes 32768 | tf_op jit(solution)/shard_map/all_to_all | solution.py:95
  27.3 14.6 %all-to-all-start.2 = ((bf16[16,2,320]{2,1,0:T(2,128)(2,1)}), bf16[16,2,320]{2,1,0:T(2,128)(2,1)S(1)}, u32[]{:S(2)}, u32[]{:S(2)}) async-start(bf16[16,2,320]{2,1,0:T(2,128)(2,1)} %reshape.265), calls=%async_computation.2 | async-start | bytes 49152 | tf_op jit(solution)/shard_map/all_to_all | solution.py:94
  41.9 38.8 %all-to-all-start = ((bf16[66,8,640]{0,1,2:T(8,128)(2,1)}), bf16[66,8,640]{0,1,2:T(8,128)(2,1)S(1)}, u32[]{:S(2)}, u32[]{:S(2)}) async-start(bf16[66,8,640]{0,1,2:T(8,128)(2,1)} %copy.137), calls=%async_computation | async-start | bytes 2621440 | tf_op jit(solution)/shard_map/all_to_all | solution.py:93
  80.9 2.4 copy-start.2
  92.5 3.5 copy-start
  114.6 3.5 copy-start
  136.8 3.5 copy-start
  158.9 3.5 copy-start
  177.4 0.6 copy-start.16
  177.4 3.7 copy-start.3
  178.0 4.7 %copy-start.10 = (bf16[2,33,33]{2,0,1:T(2,128)(2,1)S(1)}, bf16[2,33,33]{2,0,1:T(2,128)(2,1)}, u32[]{:S(2)}) copy-start(bf16[2,33,33]{2,0,1:T(2,128)(2,1)} %param.27) | copy-start | bytes 13072
  182.7 3.8 copy-start.4
  186.5 1.8 copy-start.11
  186.5 1.8 copy-start.13
  198.3 0.8 copy-start.6
  200.1 2.8 copy-start.17
  209.2 3.5 copy-start.1
  231.4 3.5 copy-start.1
  253.5 3.5 copy-start.1
  275.7 3.5 copy-start.1
  297.3 1.8 copy-start.7
  299.1 1.1 copy-start.5
  299.1 1.1 copy-start.12
  299.1 1.1 copy-start.14
where the time goes:
time: 401 us; the launch traced here: 393 us
  local copies, waits for them, and re-layouts  145 us (36%)
  blocking collectives  75.8 us (19%)
  matrix products  56.3 us (14%)
  other arithmetic  43.2 us (11%)
  waiting for transfers between devices  33.8 us (8%)
  starting transfers between devices  24.8 us (6%)
  loops' own time  13.1 us (3%)
    all_to_all x1, blocking collectives, local(): lax.all_to_all(level_major, 'lat', split_axis=1, concat_axis=2, tiled=True)  75.8 us
    reshape x8, local copies, waits for them, and re-layouts, pair_gains(): rime_terms.astype(jnp.bfloat16).reshape(bin_count, bin_count, -1)  36.1 us
    all_to_all x1, waiting for transfers between devices, local(): lax.all_to_all(packed_state, 'lat', split_axis=2, concat_axis=1, tiled=True)  31.7 us
    cond x16, other arithmetic  29.1 us
    reshape x8, local copies, waits for them, and re-layouts, pair_gains(): pair_terms.astype(jnp.bfloat16).reshape(bin_count, bin_count, -1)  27.5 us
    dot_general x2, matrix products, local(): jnp.einsum('blm,bcm->bcl', settle, spectrum, precision=lax.Precision.HIGH...  19.2 us
    dot_general x8, matrix products, pair_gains(): jnp.dot(rime_kernel.reshape(bin_count * bin_count, bin_count), frozen, pr...  17.7 us
    dot_general x8, matrix products, pair_gains(): jnp.dot(pair_kernel.reshape(bin_count * bin_count, bin_count), liquid, pr...  17.4 us
  transfers between devices with their start and end apart: 3, of which 2 were waited for; matrix products, arithmetic and copies ran while one was open for 4% of the time, Pallas kernels for 0%

commit v1 on v0

v1 whole, which is shorter than its diff:
```python
import functools

import jax
import jax.numpy as jnp
from jax import lax
from jax.experimental import pallas as pl
from jax.experimental.pallas import tpu as pltpu
from jax.sharding import PartitionSpec as P

BINS = 33
HALF = 40
ROWS = 2 * HALF
SLAB = 8
COLS = 640
LANES = 128
MINE = 3 * LANES
SENT = BINS + 1
UNITS = 5
CHIPS = 8
GROUP = 3
DEVS = 2 * CHIPS
FLAT = 168
DEPTH = 11
F32 = jnp.float32
BF16 = jnp.bfloat16

VMEM = pl.BlockSpec(memory_space=pltpu.VMEM)
SMEM = pl.BlockSpec(memory_space=pltpu.SMEM)
HBM = pl.BlockSpec(memory_space=pltpu.HBM)
PARAMS = pltpu.CompilerParams(vmem_limit_bytes=24 * 1024 * 1024)


def on_left():
    return lax.broadcasted_iota(jnp.int32, (1, LANES), 1) < LANES // 2


def turned(value):
    return pltpu.roll(value, LANES // 2, 1)


def padded(value, rows, lanes):
    have_rows, have_lanes = value.shape
    if lanes > have_lanes:
        value = jnp.concatenate([value, jnp.zeros((have_rows, lanes - have_lanes), value.dtype)], axis=1)
    if rows > have_rows:
        value = jnp.concatenate([value, jnp.zeros((rows - have_rows, lanes), value.dtype)], axis=0)
    return value


def fall_column(fall_ref):
    row = lax.broadcasted_iota(jnp.int32, (HALF, BINS), 0)
    lane = lax.broadcasted_iota(jnp.int32, (HALF, BINS), 1)
    parts = []
    for s in range(2):
        spread = jnp.broadcast_to(fall_ref[s : s + 1, :], (HALF, BINS))
        parts.append(jnp.sum(jnp.where(row == lane, spread, 0.0), axis=1, keepdims=True))
    return jnp.concatenate(parts, axis=0)


def lane_of(value, lane):
    return jnp.broadcast_to(value[:, lane : lane + 1], (ROWS, LANES))


def settle_tables(courant, chip, courant_ref, inverse_ref, lower_ref):
    own = pltpu.roll(courant, lax.rem(LANES - 2 * SLAB * chip, LANES), 1)
    left = on_left()
    lower = None
    for l in range(2 * SLAB):
        here = lane_of(own, l)
        inverse = 1.0 / (1.0 + here)
        lower = None if l < SLAB else inverse if l == SLAB else lower * last * inverse
        last = here
        courant_ref[l] = here
        inverse_ref[l] = inverse
        if l >= SLAB:
            at = l - SLAB
            courant_ref[l + SLAB] = jnp.where(left, courant_ref[at], here)
            inverse_ref[l + SLAB] = jnp.where(left, inverse_ref[at], inverse)
            lower_ref[at] = jnp.where(left, 0.0, lower)
    lower_ref[SLAB] = jnp.where(left, 0.0, lower * last)


def arrive_table(courant_ref, inverse_ref, arrive_ref):
    left = on_left()
    arrive = inverse_ref[0]
    for l in range(2 * SLAB):
        if l > 0:
            arrive = arrive * courant_ref[l - 1] * inverse_ref[l]
        arrive_ref[l] = arrive
        if l >= SLAB:
            arrive_ref[l + SLAB] = jnp.where(left, arrive_ref[l - SLAB], arrive)


def flat_of(a, b, packed):
    middle = jnp.where(on_left(), turned(packed[HALF:]), packed[:HALF])
    pieces = (a[:HALF], a[HALF:], b[:HALF], b[HALF:], middle)
    row = lax.broadcasted_iota(jnp.int32, (8, LANES), 0)
    rest = jnp.zeros((8, LANES), F32)
    for at, piece in enumerate(pieces):
        tail = piece[32:]
        rest = jnp.where(row == at, tail if at == 0 else pltpu.roll(tail, at, 0), rest)
    return jnp.concatenate([piece[:32] for piece in pieces] + [rest], axis=0)


def from_flat(flat):
    row = lax.broadcasted_iota(jnp.int32, (8, LANES), 0)
    rest = flat[160:]
    pieces = []
    for at in range(5):
        tail = rest if at == 0 else pltpu.roll(rest, 8 - at, 0)
        pieces.append(jnp.concatenate([flat[32 * at : 32 * (at + 1)], jnp.where(row == 0, tail, 0.0)], axis=0))
    return pieces


def scan_weights(courant, chip, factor_ref, weight_ref):
    ratio = courant / (1.0 + courant)
    for step in (1, 2, 4, 8):
        ratio = ratio * pltpu.roll(ratio, LANES - step, 1)
    for e in range(CHIPS):
        factor_ref[e] = lane_of(ratio, 2 * SLAB * e)
    one = jnp.ones((ROWS, LANES), F32)

    def product(first, end):
        return lax.fori_loop(first, end, lambda e, w: w * factor_ref[e], one)

    place = chip % GROUP
    first = chip - place
    size = jnp.minimum(GROUP, CHIPS - first)
    for r in range(GROUP):
        there = jnp.where(place >= r, place - r, place - r + size)
        fits = there >= 0
        if r > 0:
            w = jnp.where(fits & (there < place), product(first + there + 1, chip), 0.0)
            weight_ref[r - 1] = flat_of(w, w, w)
        w = jnp.where(fits, product(first + there + 1, first + size), 0.0)
        weight_ref[2 + r] = flat_of(w, w, w)
    for back in range(1, GROUP):
        start = first - GROUP * (back - 1)
        w = jnp.where(first >= GROUP * back, product(jnp.maximum(start, 0), chip), 0.0)
        weight_ref[4 + back] = flat_of(w, w, w)


def pack_weights(pair_ref, rime_ref, growth_ref, wide_ref, slim_ref, main_ref, rest_ref):
    for k in range(BINS):
        slim_ref[2 * k : 2 * k + 2, :] = padded(growth_ref[k].astype(F32), 2, LANES)
    for at, source in ((0, pair_ref), (1, rime_ref)):
        for k in range(BINS - 1):
            wide_ref[HALF * k : HALF * (k + 1), :] = padded(source[k].astype(F32), HALF, LANES)
        for i in range(BINS):
            main_ref[i, 32 * at : 32 * (at + 1), :] = wide_ref[pl.ds(i, 32, stride=HALF), :].astype(BF16)
        rest_ref[0, 48 * at : 48 * (at + 1), :] = padded(source[BINS - 1].astype(F32), 48, LANES).astype(BF16)
        grow = slim_ref[pl.ds(at, BINS, stride=2), :]
        rest_ref[1, 48 * at : 48 * (at + 1), :] = padded(grow, 48, LANES).astype(BF16)


def two_sided(block):
    half = block.shape[0] // 2
    empty = jnp.zeros((half, LANES), block.dtype)
    return jnp.concatenate(
        [
            jnp.concatenate([block[:half], empty], axis=1),
            jnp.concatenate([empty, block[half:]], axis=1),
        ],
        axis=0,
    )


def substep(round_ref, base_ref, state_ref, sat_ref, flag_ref, main_ref, rest_ref):
    steps = 2 * UNITS

    def place(step):
        block, first = step // 2, (step % 2) * 4
        return block, [(first + 2 * m, first + 2 * m + 1) for m in range(2)]

    def wide(ref, spot, rows, m):
        block, levels = spot
        return jnp.concatenate([ref[block, l, rows, :] for l in levels[m]], axis=1)

    def scoped(*accs):
        accs = (accs[: DEPTH + 2], accs[DEPTH + 2 :])

        def push(spot):
            empty = jnp.zeros((LANES - 48, 2 * LANES), BF16)
            for m in range(2):
                liquid = padded(wide(round_ref, spot, slice(0, HALF), m), 48, 2 * LANES).astype(BF16)
                frozen = padded(wide(round_ref, spot, slice(HALF, ROWS), m), 48, 2 * LANES).astype(BF16)
                pltpu.matmul_push_rhs(jnp.concatenate([liquid, empty, frozen, empty], axis=0), 0, m)

        def issue(j):
            lhs = two_sided(main_ref[j] if j < BINS else rest_ref[j - BINS])
            for m in range(2):
                acc = accs[m][j % DEPTH] if j < BINS else accs[m][DEPTH + j - BINS]
                pltpu.matmul_acc_lhs(acc, lhs, load_staged_rhs=0 if j == 0 else None)

        def body(step, carry):
            spot = place(step)
            block, levels = spot
            after = place(jnp.minimum(step + 1, steps - 1))
            sums = [jnp.zeros((64, 2 * LANES), F32) for m in range(2)]
            for i in range(BINS):
                if i == DEPTH - 1:
                    push(after)
                for m in range(2):
                    term = pltpu.matmul_pop(accs[m][i % DEPTH])
                    sums[m] = sums[m] + term * wide(round_ref, spot, slice(i, i + 1), m)
                if i + DEPTH < BINS:
                    issue(i + DEPTH)
                else:
                    if i + DEPTH == BINS:
                        issue(BINS)
                        issue(BINS + 1)
                    issue(i + DEPTH - BINS)
            flag = flag_ref[block]
            flag = jnp.concatenate([flag, flag], axis=1)
            for m in range(2):
                last = pltpu.matmul_pop(accs[m][DEPTH])
                grow = pltpu.matmul_pop(accs[m][DEPTH + 1])
                liquid = wide(round_ref, spot, slice(0, HALF), m)
                for s in range(2):
                    tail = jnp.sum(last[48 * s : 48 * s + HALF] * liquid, axis=0, keepdims=True)
                    tail = padded(tail, 8, 2 * LANES)
                    gain = jnp.concatenate([sums[m][32 * s : 32 * (s + 1)], tail], axis=0) * flag
                    sat = jnp.concatenate([sat_ref[block, s * SLAB + l] for l in levels[m]], axis=1)
                    gain = gain + grow[48 * s : 48 * s + HALF] * sat
                    for half, l in enumerate(levels[m]):
                        rows = slice(HALF * s, HALF * (s + 1))
                        part = gain[:, half * LANES : (half + 1) * LANES]
                        state_ref[block, l, rows, :] = base_ref[block, l, rows, :] + part
            return carry

        push(place(0))
        for j in range(DEPTH):
            issue(j)
        lax.fori_loop(0, steps, body, 0)
        for j in range(DEPTH):
            for m in range(2):
                pltpu.matmul_pop(accs[m][j])

    pl.run_scoped(scoped, *accumulators())


def settle(state_ref, courant_ref, inverse_ref, lower_ref, flux_ref):
    def column(units, first, levels):
        flux = None
        for at in range(levels):
            u, l = units[at // SLAB], at % SLAB
            state = state_ref[u, l] if flux is None else state_ref[u, l] + flux
            settled = state * inverse_ref[first + at]
            state_ref[u, l] = settled
            flux = courant_ref[first + at] * settled
        return flux

    a = column((0, 1), 0, 2 * SLAB)
    b = column((2, 3), 0, 2 * SLAB)
    packed = column((4,), 2 * SLAB, SLAB)
    upper = turned(packed)
    for l in range(SLAB):
        state_ref[4, l] = state_ref[4, l] + lower_ref[l] * upper
    packed = packed + lower_ref[SLAB] * upper
    flux_ref[...] = flat_of(a, b, packed).astype(BF16)


def arrivals(prefix_ref, far_ref, near_ref, weight_ref):
    flux = prefix_ref[...] + weight_ref[5] * near_ref[...].astype(F32) + weight_ref[6] * far_ref[...].astype(F32)
    pieces = from_flat(flux)
    middle = pieces[4]
    other = turned(middle)
    left = on_left()
    packed = [jnp.where(left, other, middle), jnp.where(left, middle, other)]
    return tuple(jnp.concatenate(x, axis=0) for x in (pieces[0:2], pieces[2:4], packed))


def with_arrivals(state_ref, arrive_ref, fluxes, put):
    for u in range(UNITS):
        for l in range(SLAB):
            level = (l, SLAB + l, l, SLAB + l, 2 * SLAB + l)[u]
            put(u, l, state_ref[u, l] + arrive_ref[level] * fluxes[u // 2])


def table_kernel(
    index_ref, pair_ref, rime_ref, growth_ref, fall_ref, dens_ref,
    main_ref, rest_ref, courant_ref, inverse_ref, lower_ref,
    wide_ref, slim_ref,
):
    chip = index_ref[0] // 2
    courant = fall_column(fall_ref) * dens_ref[...]
    settle_tables(courant, chip, courant_ref, inverse_ref, lower_ref)
    pack_weights(pair_ref, rime_ref, growth_ref, wide_ref, slim_ref, main_ref, rest_ref)


def weight_kernel(index_ref, fall_ref, dens_ref, courant_ref, inverse_ref, flux_ref, arrive_ref, weight_ref, factor_ref):
    courant = fall_column(fall_ref) * dens_ref[...]
    arrive_table(courant_ref, inverse_ref, arrive_ref)
    scan_weights(courant, index_ref[0] // 2, factor_ref, weight_ref)


def load_kernel(
    index_ref, spectra_hbm, sat_hbm, flag_hbm, pair_hbm, rime_hbm, growth_hbm, fall_hbm, dens_hbm,
    sent_ref, own_ref, flag_ref, pair_ref, rime_ref, growth_ref, fall_ref, dens_ref,
    sems,
):
    core = index_ref[0] % 2
    pieces = []
    for at, ref in ((1 - core, sent_ref), (core, own_ref)):
        cols = pl.ds(pl.multiple_of(at * 2 * LANES, LANES), MINE)
        pieces.append((spectra_hbm.at[:, :, :, cols], ref.at[:, pl.ds(0, BINS)]))
        pieces.append((sat_hbm.at[:, :, cols], ref.at[:, BINS]))
    pieces += [(fall_hbm, fall_ref), (dens_hbm, dens_ref), (pair_hbm, pair_ref), (rime_hbm, rime_ref)]
    pieces += [(growth_hbm, growth_ref), (flag_hbm, flag_ref)]
    copies = [pltpu.make_async_copy(a, b, sems.at[n]) for n, (a, b) in enumerate(pieces)]
    for copy in copies:
        copy.start()
    for copy in copies:
        copy.wait()


def first_kernel(
    index_ref, own_ref, flag_row_ref, other_ref,
    main_ref, rest_ref, courant_ref, inverse_ref, lower_ref,
    state_ref, flux_ref, initial_ref, sat_ref, flag_ref,
):
    core = index_ref[0] % 2
    for u in range(UNITS):
        for l in range(SLAB):
            for s in range(2):
                row = u * SLAB * ROWS + ROWS * l + HALF * s + 32
                initial_ref[row : row + 8, :] = jnp.zeros((8, LANES), F32)
    a, b, middle = (pl.ds(pl.multiple_of(at * LANES, LANES), LANES) for at in (core, core + 1, 2 - 2 * core))
    first = core == 0
    own_half = on_left() == first

    def in_units(s, n):
        units = []
        for cols in (a, b):
            own, other = own_ref[s, n, :, cols].astype(F32), other_ref[s, n, :, cols].astype(F32)
            units += [jnp.where(first, own, other), jnp.where(first, other, own)]
        own, other = own_ref[s, n, :, middle].astype(F32), other_ref[s, n, :, middle].astype(F32)
        return units + [jnp.where(own_half, own, turned(other))]

    flags = (flag_row_ref[...] != 0).astype(F32)
    row_a, row_b = (jnp.where(first, flags[i : i + 1], flags[i + 3 : i + 4]) for i in range(2))
    flag_units = row_a, row_a, row_b, row_b, jnp.where(own_half, flags, turned(flags))[2:3]
    for u in range(UNITS):
        flag_ref[u] = flag_units[u]
    for s in range(2):
        units = in_units(s, BINS)
        for u in range(UNITS):
            for l in range(SLAB):
                sat_ref[u, s * SLAB + l] = units[u][l : l + 1]
        for n in range(BINS):
            units = in_units(s, n)
            for u in range(UNITS):
                initial_ref[pl.ds(u * SLAB * ROWS + HALF * s + n, SLAB, stride=ROWS), :] = units[u]
    initial = initial_ref.reshape(UNITS, SLAB, ROWS, LANES)
    substep(initial, initial, state_ref, sat_ref, flag_ref, main_ref, rest_ref)
    settle(state_ref, courant_ref, inverse_ref, lower_ref, flux_ref)


def second_kernel(
    state_in, prefix_ref, far_ref, near_ref, weight_ref, sat_ref, flag_ref, main_ref, rest_ref,
    courant_ref, inverse_ref, arrive_ref, lower_ref,
    state_ref, flux_ref,
    round_ref,
):
    def put(u, l, state):
        state_ref[u, l] = state
        round_ref[u, l] = state.astype(BF16).astype(F32)

    with_arrivals(state_in, arrive_ref, arrivals(prefix_ref, far_ref, near_ref, weight_ref), put)
    substep(round_ref, state_ref, state_ref, sat_ref, flag_ref, main_ref, rest_ref)
    settle(state_ref, courant_ref, inverse_ref, lower_ref, flux_ref)


def group_kernel(flux_ref, got1_ref, got2_ref, weight_ref, prefix_ref, send_ref):
    got1, got2 = got1_ref[...].astype(F32), got2_ref[...].astype(F32)
    prefix_ref[...] = weight_ref[0] * got1 + weight_ref[1] * got2
    total = weight_ref[2] * flux_ref[...].astype(F32) + weight_ref[3] * got1 + weight_ref[4] * got2
    send_ref[...] = total.astype(BF16)


def last_kernel(
    of_own, index_ref, state_ref, initial_ref, prefix_ref, far_ref, near_ref, weight_ref, arrive_ref,
    part_ref,
    change_ref,
):
    core = index_ref[0] % 2
    slab = core if of_own else 1 - core
    fluxes = arrivals(prefix_ref, far_ref, near_ref, weight_ref)
    for k in range(3):
        u = 2 * k + slab if k < 2 else 4
        for l in range(SLAB):
            level = SLAB * slab + l if k < 2 else 2 * SLAB + l
            row = u * SLAB * ROWS + ROWS * l
            state = state_ref[u, l] + arrive_ref[level] * fluxes[k]
            start = initial_ref[pl.ds(pl.multiple_of(row, 8), ROWS), :]
            change_ref[(k * SLAB + l) * ROWS : (k * SLAB + l + 1) * ROWS, :] = (state - start) * 0.5
    spots = [pl.ds(pl.multiple_of(at * LANES, LANES), LANES) for at in (core, core + 1, 2 - 2 * core)]
    for s in range(2):
        for n in range(BINS):
            for k in range(3):
                rows = change_ref[pl.ds(k * SLAB * ROWS + HALF * s + n, SLAB, stride=ROWS), :]
                if k == 2 and not of_own:
                    rows = turned(rows)
                part_ref[s, n, :, spots[k]] = rows.astype(BF16)


def merge_kernel(index_ref, keep_ref, got_ref, out_hbm, middle_ref, sems):
    core = index_ref[0] % 2

    def merge(left_ref, right_ref):
        parts = [
            (left_ref.at[:, :, :, pl.ds(0, 2 * LANES)], out_hbm.at[:, :, :, pl.ds(0, 2 * LANES)]),
            (right_ref.at[:, :, :, pl.ds(LANES, 2 * LANES)], out_hbm.at[:, :, :, pl.ds(3 * LANES, 2 * LANES)]),
            (middle_ref, out_hbm.at[:, :, :, pl.ds(2 * LANES, LANES)]),
        ]
        copies = [pltpu.make_async_copy(x, y, sems.at[n]) for n, (x, y) in enumerate(parts)]
        copies[0].start()
        copies[1].start()
        side = lax.broadcasted_iota(jnp.int32, (2, BINS, SLAB, LANES), 3) < LANES // 2
        middle_ref[...] = jnp.where(
            side, left_ref[:, :, :, 2 * LANES :].astype(F32), right_ref[:, :, :, :LANES].astype(F32)
        ).astype(BF16)
        copies[2].start()
        for copy in copies:
            copy.wait()

    @pl.when(core == 0)
    def _():
        merge(keep_ref, got_ref)

    @pl.when(core == 1)
    def _():
        merge(got_ref, keep_ref)


def accumulators():
    kinds = []
    for m in range(2):
        kinds += [pltpu.ACC(m)((rows, 2 * LANES), F32) for rows in (64,) * DEPTH + (96, 96)]
    return kinds


def shaped(shape, dtype=F32):
    return jax.ShapeDtypeStruct(shape, dtype)


def local(spectra, supersat, cloud_flags, pair_kernel, rime_kernel, growth_matrix, fall_speed, density_factor):
    index = lax.axis_index("lat").astype(jnp.int32).reshape(1)
    swap = [(d, d ^ 1) for d in range(DEVS)]
    held = functools.partial(pltpu.with_memory_space_constraint, memory_space=pltpu.HBM)
    part = shaped((2, SENT, SLAB, MINE), BF16)
    tensor = shaped((BINS, BINS, BINS), BF16)
    sent, own, flag_rows, *parameters = pl.pallas_call(
        load_kernel,
        in_specs=[SMEM] + [HBM] * 8,
        out_specs=[VMEM] * 8,
        out_shape=[
            part,
            part,
            shaped((COLS // LANES, LANES), jnp.int32),
            tensor,
            tensor,
            shaped((BINS, 2, BINS), BF16),
            shaped((2, BINS)),
            shaped((1, LANES)),
        ],
        scratch_shapes=[pltpu.SemaphoreType.DMA((10,))],
        compiler_params=PARAMS,
        name="load_arguments",
    )(
        index, held(spectra), held(supersat), held(cloud_flags.reshape(COLS // LANES, LANES)), held(pair_kernel),
        held(rime_kernel), held(growth_matrix.transpose(1, 0, 2)), held(fall_speed), held(density_factor.reshape(1, LANES)),
    )
    other = lax.ppermute(sent, "lat", swap)

    state_shape = shaped((UNITS, SLAB, ROWS, LANES))
    flux_shape, flat_shape = shaped((FLAT, LANES), BF16), shaped((FLAT, LANES))
    level_shape = shaped((3 * SLAB, ROWS, LANES))
    cost = pl.CostEstimate(flops=2 * 2288 * 80 * SLAB * COLS, bytes_accessed=4_000_000, transcendentals=0)
    light = pl.CostEstimate(flops=1_000_000, bytes_accessed=8_000_000, transcendentals=0)

    main, rest, courant, inverse, lower = pl.pallas_call(
        table_kernel,
        in_specs=[SMEM] + [VMEM] * 5,
        out_specs=[VMEM] * 5,
        out_shape=[
            shaped((BINS, 64, LANES), BF16),
            shaped((2, 96, LANES), BF16),
            level_shape,
            level_shape,
            shaped((SLAB + 1, ROWS, LANES)),
        ],
        scratch_shapes=[
            pltpu.VMEM((HALF * (BINS - 1), LANES), F32),
            pltpu.VMEM((2 * BINS, LANES), F32),
        ],
        compiler_params=PARAMS,
        cost_estimate=light,
        name="tables",
    )(index, *parameters)

    state, flux, initial, sat, flags = pl.pallas_call(
        first_kernel,
        in_specs=[SMEM] + [VMEM] * 8,
        out_specs=[VMEM] * 5,
        out_shape=[
            state_shape,
            flux_shape,
            shaped((UNITS * SLAB * ROWS, LANES)),
            shaped((UNITS, 2 * SLAB, 1, LANES)),
            shaped((UNITS, 1, LANES)),
        ],
        compiler_params=PARAMS,
        cost_estimate=cost,
        name="first_substep",
    )(index, own, flag_rows, other, main, rest, courant, inverse, lower)

    arrive, weight = pl.pallas_call(
        weight_kernel,
        in_specs=[SMEM] + [VMEM] * 4 + [pl.BlockSpec(memory_space=pl.ANY)],
        out_specs=[VMEM] * 2,
        out_shape=[level_shape, shaped((7, FLAT, LANES))],
        scratch_shapes=[pltpu.VMEM((CHIPS, ROWS, LANES), F32)],
        compiler_params=PARAMS,
        cost_estimate=light,
        name="scan_weights",
    )(index, *parameters[3:], courant, inverse, flux)

    def between(pairs):
        return [(2 * a + c, 2 * b + c) for a, b in pairs for c in range(2)]

    around = []
    for r in range(1, GROUP):
        pairs = []
        for first in range(0, CHIPS, GROUP):
            size = min(GROUP, CHIPS - first)
            pairs += [(first + p, first + (p + r) % size) for p in range(size) if r < size]
        around.append(between([(a, b) for a, b in pairs if b not in (3, 6)]))
    near = between([(0, 3), (1, 4), (2, 5), (4, 6), (5, 7)])
    far = between([(0, 6), (1, 7)])

    def scan(flux):
        got = [lax.ppermute(flux, "lat", pairs) for pairs in around]
        prefix, send = pl.pallas_call(
            group_kernel,
            in_specs=[VMEM] * 4,
            out_specs=[VMEM] * 2,
            out_shape=[flat_shape, flux_shape],
            compiler_params=PARAMS,
            name="scan_group",
        )(flux, *got, weight)
        return prefix, lax.ppermute(send, "lat", far), lax.ppermute(send, "lat", near)

    state, flux = pl.pallas_call(
        second_kernel,
        in_specs=[VMEM] * 13,
        out_specs=[VMEM] * 2,
        out_shape=[state_shape, flux_shape],
        scratch_shapes=[pltpu.VMEM((UNITS, SLAB, ROWS, LANES), F32)],
        compiler_params=PARAMS,
        cost_estimate=cost,
        name="second_substep",
    )(state, *scan(flux), weight, sat, flags, main, rest, courant, inverse, arrive, lower)

    arrived = scan(flux)

    def tendencies(of_own, name):
        return pl.pallas_call(
            functools.partial(last_kernel, of_own),
            in_specs=[SMEM] + [VMEM] * 7,
            out_specs=VMEM,
            out_shape=shaped((2, BINS, SLAB, MINE), BF16),
            scratch_shapes=[pltpu.VMEM((3 * SLAB * ROWS, LANES), F32)],
            compiler_params=PARAMS,
            cost_estimate=light,
            name=name,
        )(index, state, initial, *arrived, weight, arrive)

    send = tendencies(False, "tendencies_sent")
    keep = tendencies(True, "tendencies_kept")

    got = lax.ppermute(send, "lat", swap)
    return pl.pallas_call(
        merge_kernel,
        in_specs=[SMEM] + [VMEM] * 2,
        out_specs=HBM,
        out_shape=shaped(spectra.shape, BF16),
        scratch_shapes=[pltpu.VMEM((2, BINS, SLAB, LANES), BF16), pltpu.SemaphoreType.DMA((3,))],
        compiler_params=PARAMS,
        cost_estimate=light,
        name="merge_slabs",
    )(index, keep, got)


def solution(mesh):
    return jax.shard_map(
        local,
        mesh=mesh,
        in_specs=(
            P(None, None, "lat", "lon"),
            P(None, "lat", "lon"),
            P("lon"),
            P(),
            P(),
            P(),
            P(),
            P(),
        ),
        out_specs=P(None, None, "lat", "lon"),
        check_vma=False,
    )
```

time: 401 us -> 64 us (0.16); the launches traced: 393 us -> 63.3 us
  local copies, waits for them, and re-layouts: 145 us -> 0 us
  blocking collectives: 75.8 us -> 0 us
  matrix products: 56.3 us -> 0 us
  other arithmetic: 43.2 us -> 0 us
  waiting for transfers between devices: 33.8 us -> 8.42 us
  Pallas kernels: 0 us -> 19.6 us
  loops' own time: 13.1 us -> 0 us
  starting transfers between devices: 24.8 us -> 35.2 us
    reshape x34 -> x0, local copies, waits for them, and re-layouts: 81.7 us -> none  [the longest x8 36.1 us: pair_gains(): rime_terms.astype(jnp.bfloat16).reshape(bin_count, bin_count, -1)]
    all_to_all x1 -> x0, blocking collectives: 75.8 us -> none  [local(): lax.all_to_all(level_major, 'lat', split_axis=1, concat_axis=2, tiled=True)]
    dot_general x20 -> x0, matrix products: 56.3 us -> none  [the longest x2 19.2 us: local(): jnp.einsum('blm,bcm->bcl', settle, spectrum, precision=lax.Precision.HIGH...]
    ppermute x0 -> x10, starting transfers between devices: none -> 35.2 us  [the longest x4 12.2 us: scan(): got = [lax.ppermute(flux, 'lat', pairs) for pairs in around]]
    all_to_all x3 -> x0, waiting for transfers between devices: 33.8 us -> none  [the longest x1 31.7 us: local(): lax.all_to_all(packed_state, 'lat', split_axis=2, concat_axis=1, tiled=True)]
    cond x16 -> x0, other arithmetic: 29.1 us -> none
    all_to_all x3 -> x0, starting transfers between devices: 24.8 us -> none  [the longest x1 11.8 us: local(): lax.all_to_all(flag_plane, 'lat', split_axis=2, concat_axis=1, tiled=True)]
    pallas_call x0 -> x10, Pallas kernels: none -> 19.6 us  [the longest x1 7.17 us: local(): pl.pallas_call(first_kernel, in_specs=[SMEM] + [VMEM] * 8, out_specs=[VME...]
  transfers between devices with their start and end apart: 3 -> 10, of which waited for: 2 -> 6; matrix products, arithmetic and copies ran while one was open for 4% -> 0% of each run, Pallas kernels for 0% -> 4%
where the time goes in v1:
time: 64 us; the launch traced here: 63.3 us
  starting transfers between devices  35.2 us (55%)
  Pallas kernels  19.6 us (31%)
  waiting for transfers between devices  8.42 us (13%)
    ppermute x4, starting transfers between devices, scan(): got = [lax.ppermute(flux, 'lat', pairs) for pairs in around]  12.2 us
    ppermute x1, starting transfers between devices, local(): other = lax.ppermute(sent, 'lat', swap)  8.79 us
    ppermute x2, starting transfers between devices, scan(): lax.ppermute(send, 'lat', near)  7.47 us
    pallas_call x1, Pallas kernels, local(): pl.pallas_call(first_kernel, in_specs=[SMEM] + [VMEM] * 8, out_specs=[VME...  7.17 us
    pallas_call x1, Pallas kernels, local(): pl.pallas_call(second_kernel, in_specs=[VMEM] * 13, out_specs=[VMEM] * 2,...  6.92 us
    ppermute x4, waiting for transfers between devices, scan(): got = [lax.ppermute(flux, 'lat', pairs) for pairs in around]  4.81 us
    ppermute x1, starting transfers between devices, local(): got = lax.ppermute(send, 'lat', swap)  4.16 us
    ppermute x2, starting transfers between devices, scan(): lax.ppermute(send, 'lat', far)  2.58 us
  transfers between devices with their start and end apart: 10, of which 6 were waited for; matrix products, arithmetic and copies ran while one was open for 0% of the time, Pallas kernels for 4%

profile of v1, /device:TPU:1, one launch (start us, length us, event | category | flops | bytes accessed | tf_op | source)
XLA Modules:
  0.0 63.3 jit_solution(6831446371356337194)
XLA Ops:
  0.0 1.5 %load_arguments.1 = (bf16[2,34,8,384]{3,2,1,0:T(8,128)(2,1)S(1)}, bf16[2,34,8,384]{3,2,1,0:T(8,128)(2,1)S(1)}, s32[5,128]{1,0:T(8,128)S(1)}, bf16[33,33,33]{2,1,...) custom-call(s32[1]{0:T(128)} %bitcast.index_ref, ...), custom_call_target="tpu_custom_call" | custom-call | tf_op jit(solution)/shard_map/load_arguments/pallas_call | solution.py:453
  1.5 8.8 %collective-permute-start = (bf16[2,34,8,384]{3,2,1,0:T(8,128)(2,1)S(1)}, bf16[2,34,8,384]{3,2,1,0:T(8,128)(2,1)S(1)}, u32[]{:S(2)}, u32[]{:S(2)}) collective-permute-start(bf16[2,34,8,384]{3,2,1,0:T(8,128)(2,1)S(1)} %get-tuple-element.33), channel_id=1, source_target_pairs={{0,1},{1,0},{2,3},{3,2},{4,5},{5,4},{6,7},{7,6},{8,9},{9,8},{10,11... | collective-permute-start | bytes 1253384 | tf_op jit(solution)/shard_map/ppermute | solution.py:474
  10.3 0.8 %tables.1 = (bf16[33,64,128]{2,1,0:T(8,128)(2,1)S(1)}, bf16[2,96,128]{2,1,0:T(8,128)(2,1)S(1)}, f32[24,80,128]{2,1,0:T(8,128)S(1)}, f32[24,80,128]{2,1,0:T(8,128)S(1)}, f32[9,80,128]{2,1,0:T(8,128)S(1)}) custom-call(s32[1]{0:T(128)} %bitcast.index_ref, bf16[33,33,33]{2,1,0:T(8,128)(2,1)S(1)} %get-tuple-element.34.pair_ref, ...), custom_call_target="tpu_custom_call" | custom-call | flops 1000000 | bytes 8000000 | tf_op jit(solution)/shard_map/tables/pallas_call | solution.py:482
  11.1 0.6 collective-permute-done.other_ref
  11.7 7.2 %first_substep.1 = (f32[5,8,80,128]{3,2,1,0:T(8,128)S(1)}, bf16[168,128]{1,0:T(8,128)(2,1)S(1)}, f32[3200,128]{1,0:T(8,128)S(1)}, f32[5,16,1,128]{3,2,1,0:T(1,128)S(1)}, f32[5,1,128]{2,1,0:T(1,128)S(1)}) custom-call(s32[1]{0:T(128)} %bitcast.index_ref, bf16[2,34,8,384]{3,2,1,0:T(8,128)(2,1)S(1)} %get-tuple-element.31.own_ref, ...), custom_call_target="tpu_custom_call" | custom-call | flops 1874329600 | bytes 4000000 | tf_op jit(solution)/shard_map/first_substep/pallas_call | solution.py:502
  18.8 1.9 %collective-permute-start.2 = (bf16[168,128]{1,0:T(8,128)(2,1)S(1)}, bf16[168,128]{1,0:T(8,128)(2,1)S(1)}, u32[]{:S(2)}, u32[]{:S(2)}) collective-permute-start(bf16[168,128]{1,0:T(8,128)(2,1)S(1)} %get-tuple-element.45.flux_ref), channel_id=1, source_target_pairs={{0,4},{1,5},{2,0},{3,1},{4,2},{5,3},{6,10},{7,11},{10,8},{11,9},{1... | collective-permute-start | bytes 129032 | tf_op jit(solution)/shard_map/ppermute | solution.py:543
  20.8 3.4 %collective-permute-start.1 = (bf16[168,128]{1,0:T(8,128)(2,1)S(1)}, bf16[168,128]{1,0:T(8,128)(2,1)S(1)}, u32[]{:S(2)}, u32[]{:S(2)}) collective-permute-start(bf16[168,128]{1,0:T(8,128)(2,1)S(1)} %get-tuple-element.45.flux_ref), channel_id=1, source_target_pairs={{0,2},{1,3},{2,4},{3,5},{4,0},{5,1},{6,8},{7,9},{8,10},{9,11},{12,... | collective-permute-start | bytes 129032 | tf_op jit(solution)/shard_map/ppermute | solution.py:543
  24.1 1.2 %scan_weights.1 = (f32[24,80,128]{2,1,0:T(8,128)S(1)}, f32[7,168,128]{2,1,0:T(8,128)S(1)}) custom-call(s32[1]{0:T(128)} %bitcast.index_ref, f32[2,33]{1,0:T(2,128)S(1)} %get-tuple-element.37.fall_ref, f32[1,128]{1,0:T(1,128)S(1)} %get-tuple-element.38.dens_ref, f32[24,80,128]{2,1,0:T(8,128)S(1)} %get-tuple-element.41.courant_ref, ...), custom_call_target="tpu_custom_call" | custom-call | flops 1000000 | bytes 8000000 | tf_op jit(solution)/shard_map/scan_weights/pallas_call | solution.py:518
  25.3 0.0 collective-permute-done.2.got2_ref
  25.3 1.1 %collective-permute-done.1.got1_ref = bf16[168,128]{1,0:T(8,128)(2,1)S(1)} collective-permute-done((bf16[168,128]{1,0:T(8,128)(2,1)S(1)}, bf16[168,128]{1,0:T(8,128)(2,1)S(1)}, u32[]{:S(2)}, u32[]{:S(2)}) %collective-permute-start.1) | collective-permute-done | bytes 43040 | tf_op jit(solution)/shard_map/ppermute | solution.py:543
  26.5 3.3 %collective-permute-start.4 = (bf16[168,128]{1,0:T(8,128)(2,1)S(1)}, bf16[168,128]{1,0:T(8,128)(2,1)S(1)}, u32[]{:S(2)}, u32[]{:S(2)}) collective-permute-start(bf16[168,128]{1,0:T(8,128)(2,1)S(1)} %get-tuple-element.48), channel_id=1, source_target_pairs={{0,6},{1,7},{2,8},{3,9},{4,10},{5,11},{8,12},{9,13},{10,14},{11,15... | collective-permute-start | bytes 129032 | tf_op jit(solution)/shard_map/ppermute | solution.py:552
  29.8 1.3 %collective-permute-start.3 = (bf16[168,128]{1,0:T(8,128)(2,1)S(1)}, bf16[168,128]{1,0:T(8,128)(2,1)S(1)}, u32[]{:S(2)}, u32[]{:S(2)}) collective-permute-start(bf16[168,128]{1,0:T(8,128)(2,1)S(1)} %get-tuple-element.48), channel_id=1, source_target_pairs={{0,12},{1,13},{2,14},{3,15},{16,28},{17,29},{18,30},{19,31},{32,44... | collective-permute-start | bytes 129032 | tf_op jit(solution)/shard_map/ppermute | solution.py:552
  31.1 0.0 collective-permute-done.4.near_ref
  31.1 1.1 %collective-permute-done.3.far_ref = bf16[168,128]{1,0:T(8,128)(2,1)S(1)} collective-permute-done((bf16[168,128]{1,0:T(8,128)(2,1)S(1)}, bf16[168,128]{1,0:T(8,128)(2,1)S(1)}, u32[]{:S(2)}, u32[]{:S(2)}) %collective-permute-start.3) | collective-permute-done | bytes 43040 | tf_op jit(solution)/shard_map/ppermute | solution.py:552
  32.2 6.9 %second_substep.1 = (f32[5,8,80,128]{3,2,1,0:T(8,128)S(1)}, bf16[168,128]{1,0:T(8,128)(2,1)S(1)}) custom-call(f32[5,8,80,128]{3,2,1,0:T(8,128)S(1)} %get-tuple-element.44.state_in, f32[168,128]{1,0:T(8,128)S(1)} %get-tuple-element.47.prefix_ref, bf16[168,128]{1,0:T(8,128)(2,1)S(1)} %collective-permute-done.3.far_ref, ...), custom_call_target="tpu_custom_call" | custom-call | flops 1874329600 | bytes 4000000 | tf_op jit(solution)/shard_map/second_substep/pallas_call | solution.py:554
  39.1 5.0 %collective-permute-start.6 = (bf16[168,128]{1,0:T(8,128)(2,1)S(1)}, bf16[168,128]{1,0:T(8,128)(2,1)S(1)}, u32[]{:S(2)}, u32[]{:S(2)}) collective-permute-start(bf16[168,128]{1,0:T(8,128)(2,1)S(1)} %get-tuple-element.54.flux_ref), channel_id=1, source_target_pairs={{0,4},{1,5},{2,0},{3,1},{4,2},{5,3},{6,10},{7,11},{10,8},{11,9},{1... | collective-permute-start | bytes 129032 | tf_op jit(solution)/shard_map/ppermute | solution.py:543
  44.1 1.9 %collective-permute-start.5 = (bf16[168,128]{1,0:T(8,128)(2,1)S(1)}, bf16[168,128]{1,0:T(8,128)(2,1)S(1)}, u32[]{:S(2)}, u32[]{:S(2)}) collective-permute-start(bf16[168,128]{1,0:T(8,128)(2,1)S(1)} %get-tuple-element.54.flux_ref), channel_id=1, source_target_pairs={{0,2},{1,3},{2,4},{3,5},{4,0},{5,1},{6,8},{7,9},{8,10},{9,11},{12,... | collective-permute-start | bytes 129032 | tf_op jit(solution)/shard_map/ppermute | solution.py:543
  46.1 0.0 collective-permute-done.6.got2_ref
  46.1 3.7 %collective-permute-done.5.got1_ref = bf16[168,128]{1,0:T(8,128)(2,1)S(1)} collective-permute-done((bf16[168,128]{1,0:T(8,128)(2,1)S(1)}, bf16[168,128]{1,0:T(8,128)(2,1)S(1)}, u32[]{:S(2)}, u32[]{:S(2)}) %collective-permute-start.5) | collective-permute-done | bytes 43040 | tf_op jit(solution)/shard_map/ppermute | solution.py:543
  49.8 4.2 %collective-permute-start.8 = (bf16[168,128]{1,0:T(8,128)(2,1)S(1)}, bf16[168,128]{1,0:T(8,128)(2,1)S(1)}, u32[]{:S(2)}, u32[]{:S(2)}) collective-permute-start(bf16[168,128]{1,0:T(8,128)(2,1)S(1)} %get-tuple-element.56), channel_id=1, source_target_pairs={{0,6},{1,7},{2,8},{3,9},{4,10},{5,11},{8,12},{9,13},{10,14},{11,15... | collective-permute-start | bytes 129032 | tf_op jit(solution)/shard_map/ppermute | solution.py:552
  54.0 1.3 %collective-permute-start.7 = (bf16[168,128]{1,0:T(8,128)(2,1)S(1)}, bf16[168,128]{1,0:T(8,128)(2,1)S(1)}, u32[]{:S(2)}, u32[]{:S(2)}) collective-permute-start(bf16[168,128]{1,0:T(8,128)(2,1)S(1)} %get-tuple-element.56), channel_id=1, source_target_pairs={{0,12},{1,13},{2,14},{3,15},{16,28},{17,29},{18,30},{19,31},{32,44... | collective-permute-start | bytes 129032 | tf_op jit(solution)/shard_map/ppermute | solution.py:552
  55.3 0.0 collective-permute-done.8.near_ref
  55.3 1.1 %collective-permute-done.7.far_ref = bf16[168,128]{1,0:T(8,128)(2,1)S(1)} collective-permute-done((bf16[168,128]{1,0:T(8,128)(2,1)S(1)}, bf16[168,128]{1,0:T(8,128)(2,1)S(1)}, u32[]{:S(2)}, u32[]{:S(2)}) %collective-permute-start.7) | collective-permute-done | bytes 43040 | tf_op jit(solution)/shard_map/ppermute | solution.py:552
  56.4 0.6 tendencies_sent.1
  57.0 4.2 %collective-permute-start.9 = (bf16[2,33,8,384]{3,2,1,0:T(8,128)(2,1)S(1)}, bf16[2,33,8,384]{3,2,1,0:T(8,128)(2,1)S(1)}, u32[]{:S(2)}, u32[]{:S(2)}) collective-permute-start(bf16[2,33,8,384]{3,2,1,0:T(8,128)(2,1)S(1)} %tendencies_sent.1), channel_id=1, source_target_pairs={{0,1},{1,0},{2,3},{3,2},{4,5},{5,4},{6,7},{7,6},{8,9},{9,8},{10,11... | collective-permute-start | bytes 1216520 | tf_op jit(solution)/shard_map/ppermute | solution.py:582
  61.1 0.5 tendencies_kept.1.keep_ref
  61.6 0.9 %collective-permute-done.9.got_ref = bf16[2,33,8,384]{3,2,1,0:T(8,128)(2,1)S(1)} collective-permute-done((bf16[2,33,8,384]{3,2,1,0:T(8,128)(2,1)S(1)}, bf16[2,33,8,384]{3,2,1,0:T(8,128)(2,1)S(1)}, u32[]{:S(2)}, u32[]{:S(2)}) %collective-permute-start.9) | collective-permute-done | bytes 405536 | tf_op jit(solution)/shard_map/ppermute | solution.py:582
  62.5 0.9 %merge_slabs.1 = bf16[2,33,8,640]{3,2,1,0:T(8,128)(2,1)} custom-call(s32[1]{0:T(128)} %bitcast.index_ref, bf16[2,33,8,384]{3,2,1,0:T(8,128)(2,1)S(1)} %tendencies_kept.1.keep_ref, bf16[2,33,8,384]{3,2,1,0:T(8,128)(2,1)S(1)} %collective-permute-done.9.got_ref), custom_call_target="tpu_custom_call" | custom-call | flops 1000000 | bytes 8000000 | tf_op jit(solution)/shard_map/merge_slabs/pallas_call | solution.py:583
  (2 shorter events, 0.1 us)
Async XLA Ops:
  1.5 10.2 %collective-permute-start = (bf16[2,34,8,384]{3,2,1,0:T(8,128)(2,1)S(1)}, bf16[2,34,8,384]{3,2,1,0:T(8,128)(2,1)S(1)}, u32[]{:S(2)}, u32[]{:S(2)}) collective-permute-start(bf16[2,34,8,384]{3,2,1,0:T(8,128)(2,1)S(1)} %get-tuple-element.33), channel_id=1, source_target_pairs={{0,1},{1,0},{2,3},{3,2},{4,5},{5,4},{6,7},{7,6},{8,9},{9,8},{10,11... | collective-permute-start | bytes 1253384 | tf_op jit(solution)/shard_map/ppermute | solution.py:474
  18.8 6.5 %collective-permute-start.2 = (bf16[168,128]{1,0:T(8,128)(2,1)S(1)}, bf16[168,128]{1,0:T(8,128)(2,1)S(1)}, u32[]{:S(2)}, u32[]{:S(2)}) collective-permute-start(bf16[168,128]{1,0:T(8,128)(2,1)S(1)} %get-tuple-element.45.flux_ref), channel_id=1, source_target_pairs={{0,4},{1,5},{2,0},{3,1},{4,2},{5,3},{6,10},{7,11},{10,8},{11,9},{1... | collective-permute-start | bytes 129032 | tf_op jit(solution)/shard_map/ppermute | solution.py:543
  20.8 5.7 %collective-permute-start.1 = (bf16[168,128]{1,0:T(8,128)(2,1)S(1)}, bf16[168,128]{1,0:T(8,128)(2,1)S(1)}, u32[]{:S(2)}, u32[]{:S(2)}) collective-permute-start(bf16[168,128]{1,0:T(8,128)(2,1)S(1)} %get-tuple-element.45.flux_ref), channel_id=1, source_target_pairs={{0,2},{1,3},{2,4},{3,5},{4,0},{5,1},{6,8},{7,9},{8,10},{9,11},{12,... | collective-permute-start | bytes 129032 | tf_op jit(solution)/shard_map/ppermute | solution.py:543
  26.5 4.6 %collective-permute-start.4 = (bf16[168,128]{1,0:T(8,128)(2,1)S(1)}, bf16[168,128]{1,0:T(8,128)(2,1)S(1)}, u32[]{:S(2)}, u32[]{:S(2)}) collective-permute-start(bf16[168,128]{1,0:T(8,128)(2,1)S(1)} %get-tuple-element.48), channel_id=1, source_target_pairs={{0,6},{1,7},{2,8},{3,9},{4,10},{5,11},{8,12},{9,13},{10,14},{11,15... | collective-permute-start | bytes 129032 | tf_op jit(solution)/shard_map/ppermute | solution.py:552
  29.8 2.4 %collective-permute-start.3 = (bf16[168,128]{1,0:T(8,128)(2,1)S(1)}, bf16[168,128]{1,0:T(8,128)(2,1)S(1)}, u32[]{:S(2)}, u32[]{:S(2)}) collective-permute-start(bf16[168,128]{1,0:T(8,128)(2,1)S(1)} %get-tuple-element.48), channel_id=1, source_target_pairs={{0,12},{1,13},{2,14},{3,15},{16,28},{17,29},{18,30},{19,31},{32,44... | collective-permute-start | bytes 129032 | tf_op jit(solution)/shard_map/ppermute | solution.py:552
  39.1 6.9 %collective-permute-start.6 = (bf16[168,128]{1,0:T(8,128)(2,1)S(1)}, bf16[168,128]{1,0:T(8,128)(2,1)S(1)}, u32[]{:S(2)}, u32[]{:S(2)}) collective-permute-start(bf16[168,128]{1,0:T(8,128)(2,1)S(1)} %get-tuple-element.54.flux_ref), channel_id=1, source_target_pairs={{0,4},{1,5},{2,0},{3,1},{4,2},{5,3},{6,10},{7,11},{10,8},{11,9},{1... | collective-permute-start | bytes 129032 | tf_op jit(solution)/shard_map/ppermute | solution.py:543
  44.1 5.7 %collective-permute-start.5 = (bf16[168,128]{1,0:T(8,128)(2,1)S(1)}, bf16[168,128]{1,0:T(8,128)(2,1)S(1)}, u32[]{:S(2)}, u32[]{:S(2)}) collective-permute-start(bf16[168,128]{1,0:T(8,128)(2,1)S(1)} %get-tuple-element.54.flux_ref), channel_id=1, source_target_pairs={{0,2},{1,3},{2,4},{3,5},{4,0},{5,1},{6,8},{7,9},{8,10},{9,11},{12,... | collective-permute-start | bytes 129032 | tf_op jit(solution)/shard_map/ppermute | solution.py:543
  49.8 5.5 %collective-permute-start.8 = (bf16[168,128]{1,0:T(8,128)(2,1)S(1)}, bf16[168,128]{1,0:T(8,128)(2,1)S(1)}, u32[]{:S(2)}, u32[]{:S(2)}) collective-permute-start(bf16[168,128]{1,0:T(8,128)(2,1)S(1)} %get-tuple-element.56), channel_id=1, source_target_pairs={{0,6},{1,7},{2,8},{3,9},{4,10},{5,11},{8,12},{9,13},{10,14},{11,15... | collective-permute-start | bytes 129032 | tf_op jit(solution)/shard_map/ppermute | solution.py:552
  54.0 2.4 %collective-permute-start.7 = (bf16[168,128]{1,0:T(8,128)(2,1)S(1)}, bf16[168,128]{1,0:T(8,128)(2,1)S(1)}, u32[]{:S(2)}, u32[]{:S(2)}) collective-permute-start(bf16[168,128]{1,0:T(8,128)(2,1)S(1)} %get-tuple-element.56), channel_id=1, source_target_pairs={{0,12},{1,13},{2,14},{3,15},{16,28},{17,29},{18,30},{19,31},{32,44... | collective-permute-start | bytes 129032 | tf_op jit(solution)/shard_map/ppermute | solution.py:552
  57.0 5.5 %collective-permute-start.9 = (bf16[2,33,8,384]{3,2,1,0:T(8,128)(2,1)S(1)}, bf16[2,33,8,384]{3,2,1,0:T(8,128)(2,1)S(1)}, u32[]{:S(2)}, u32[]{:S(2)}) collective-permute-start(bf16[2,33,8,384]{3,2,1,0:T(8,128)(2,1)S(1)} %tendencies_sent.1), channel_id=1, source_target_pairs={{0,1},{1,0},{2,3},{3,2},{4,5},{5,4},{6,7},{7,6},{8,9},{9,8},{10,11... | collective-permute-start | bytes 1216520 | tf_op jit(solution)/shard_map/ppermute | solution.py:582

commit v2 on v1

--- a/solution.py
+++ b/solution.py
@@ -134,10 +134,9 @@
             weight_ref[r - 1] = flat_of(w, w, w)
         w = jnp.where(fits, product(first + there + 1, first + size), 0.0)
         weight_ref[2 + r] = flat_of(w, w, w)
-    for back in range(1, GROUP):
-        start = first - GROUP * (back - 1)
-        w = jnp.where(first >= GROUP * back, product(jnp.maximum(start, 0), chip), 0.0)
-        weight_ref[4 + back] = flat_of(w, w, w)
+    for at, start in ((5, first), (6, GROUP)):
+        w = jnp.where(first >= GROUP, product(start, chip), 0.0)
+        weight_ref[at] = flat_of(w, w, w)
 
 
 def pack_weights(pair_ref, rime_ref, growth_ref, wide_ref, slim_ref, main_ref, rest_ref):
@@ -260,8 +259,9 @@
     flux_ref[...] = flat_of(a, b, packed).astype(BF16)
 
 
-def arrivals(prefix_ref, far_ref, near_ref, weight_ref):
-    flux = prefix_ref[...] + weight_ref[5] * near_ref[...].astype(F32) + weight_ref[6] * far_ref[...].astype(F32)
+def arrivals(prefix_ref, far_refs, near_ref, weight_ref):
+    far = sum(ref[...].astype(F32) for ref in far_refs)
+    flux = prefix_ref[...] + weight_ref[5] * near_ref[...].astype(F32) + weight_ref[6] * far
     pieces = from_flat(flux)
     middle = pieces[4]
     other = turned(middle)
@@ -366,7 +366,7 @@
         state_ref[u, l] = state
         round_ref[u, l] = state.astype(BF16).astype(F32)
 
-    with_arrivals(state_in, arrive_ref, arrivals(prefix_ref, far_ref, near_ref, weight_ref), put)
+    with_arrivals(state_in, arrive_ref, arrivals(prefix_ref, (far_ref,), near_ref, weight_ref), put)
     substep(round_ref, state_ref, state_ref, sat_ref, flag_ref, main_ref, rest_ref)
     settle(state_ref, courant_ref, inverse_ref, lower_ref, flux_ref)
 
@@ -379,13 +379,13 @@
 
 
 def last_kernel(
-    of_own, index_ref, state_ref, initial_ref, prefix_ref, far_ref, near_ref, weight_ref, arrive_ref,
+    of_own, index_ref, state_ref, initial_ref, prefix_ref, farther_ref, far_ref, near_ref, weight_ref, arrive_ref,
     part_ref,
     change_ref,
 ):
     core = index_ref[0] % 2
     slab = core if of_own else 1 - core
-    fluxes = arrivals(prefix_ref, far_ref, near_ref, weight_ref)
+    fluxes = arrivals(prefix_ref, (farther_ref, far_ref), near_ref, weight_ref)
     for k in range(3):
         u = 2 * k + slab if k < 2 else 4
         for l in range(SLAB):
@@ -529,18 +529,19 @@
     def between(pairs):
         return [(2 * a + c, 2 * b + c) for a, b in pairs for c in range(2)]
 
-    around = []
-    for r in range(1, GROUP):
+    def around(r, without):
         pairs = []
         for first in range(0, CHIPS, GROUP):
             size = min(GROUP, CHIPS - first)
             pairs += [(first + p, first + (p + r) % size) for p in range(size) if r < size]
-        around.append(between([(a, b) for a, b in pairs if b not in (3, 6)]))
-    near = between([(0, 3), (1, 4), (2, 5), (4, 6), (5, 7)])
-    far = between([(0, 6), (1, 7)])
-
-    def scan(flux):
-        got = [lax.ppermute(flux, "lat", pairs) for pairs in around]
+        return between([(a, b) for a, b in pairs if b not in without])
+
+    first_scan = (3, 6), ([(2, 4), (0, 6), (1, 7)], [(0, 3), (2, 5), (4, 6), (5, 7)])
+    last_scan = (0, 3, 6), ([(1, 6)], [(2, 4), (1, 7)], [(1, 3), (2, 5), (4, 6), (5, 7)])
+
+    def scan(flux, plan):
+        without, sums = plan
+        got = [lax.ppermute(flux, "lat", around(r, without)) for r in range(1, GROUP)]
         prefix, send = pl.pallas_call(
             group_kernel,
             in_specs=[VMEM] * 4,
@@ -549,7 +550,7 @@
             compiler_params=PARAMS,
             name="scan_group",
         )(flux, *got, weight)
-        return prefix, lax.ppermute(send, "lat", far), lax.ppermute(send, "lat", near)
+        return prefix, *(lax.ppermute(send, "lat", between(pairs)) for pairs in sums)
 
     state, flux = pl.pallas_call(
         second_kernel,
@@ -560,14 +561,14 @@
         compiler_params=PARAMS,
         cost_estimate=cost,
         name="second_substep",
-    )(state, *scan(flux), weight, sat, flags, main, rest, courant, inverse, arrive, lower)
-
-    arrived = scan(flux)
+    )(state, *scan(flux, first_scan), weight, sat, flags, main, rest, courant, inverse, arrive, lower)
+
+    arrived = scan(flux, last_scan)
 
     def tendencies(of_own, name):
         return pl.pallas_call(
             functools.partial(last_kernel, of_own),
-            in_specs=[SMEM] + [VMEM] * 7,
+            in_specs=[SMEM] + [VMEM] * 8,
             out_specs=VMEM,
             out_shape=shaped((2, BINS, SLAB, MINE), BF16),
             scratch_shapes=[pltpu.VMEM((3 * SLAB * ROWS, LANES), F32)],

time: 64 us -> 63.4 us (level)
  the two profiles are of different devices: /device:TPU:1 before, /device:TPU:183 now
where the time goes in v2:
time: 63.4 us; the launch traced here: 63.1 us
  starting transfers between devices  36.6 us (58%)
  Pallas kernels  19.6 us (31%)
  waiting for transfers between devices  6.73 us (11%)
    ppermute x5, starting transfers between devices, scan(): lax.ppermute(send, 'lat', between(pairs))  19.2 us
    ppermute x4, starting transfers between devices, scan(): lax.ppermute(flux, 'lat', around(r, without))  9.39 us
    pallas_call x1, Pallas kernels, local(): pl.pallas_call(first_kernel, in_specs=[SMEM] + [VMEM] * 8, out_specs=[VME...  7.17 us
    pallas_call x1, Pallas kernels, local(): pl.pallas_call(second_kernel, in_specs=[VMEM] * 13, out_specs=[VMEM] * 2,...  6.9 us
    ppermute x1, starting transfers between devices, local(): got = lax.ppermute(send, 'lat', swap)  5.43 us
    ppermute x4, waiting for transfers between devices, scan(): lax.ppermute(flux, 'lat', around(r, without))  3.47 us
    ppermute x1, starting transfers between devices, local(): other = lax.ppermute(sent, 'lat', swap)  2.58 us
    ppermute x5, waiting for transfers between devices, scan(): lax.ppermute(send, 'lat', between(pairs))  1.83 us
  transfers between devices with their start and end apart: 11, of which 6 were waited for; matrix products, arithmetic and copies ran while one was open for 0% of the time, Pallas kernels for 4%

profile of v2, /device:TPU:183, one launch (start us, length us, event | category | flops | bytes accessed | tf_op | source)
XLA Modules:
  0.0 63.1 jit_solution(1561897795047391006)
XLA Ops:
  0.0 1.5 %load_arguments.1 = (bf16[2,34,8,384]{3,2,1,0:T(8,128)(2,1)S(1)}, bf16[2,34,8,384]{3,2,1,0:T(8,128)(2,1)S(1)}, s32[5,128]{1,0:T(8,128)S(1)}, bf16[33,33,33]{2,1,...) custom-call(s32[1]{0:T(128)} %bitcast.index_ref, ...), custom_call_target="tpu_custom_call" | custom-call | tf_op jit(solution)/shard_map/load_arguments/pallas_call | solution.py:453
  1.5 2.6 %collective-permute-start = (bf16[2,34,8,384]{3,2,1,0:T(8,128)(2,1)S(1)}, bf16[2,34,8,384]{3,2,1,0:T(8,128)(2,1)S(1)}, u32[]{:S(2)}, u32[]{:S(2)}) collective-permute-start(bf16[2,34,8,384]{3,2,1,0:T(8,128)(2,1)S(1)} %get-tuple-element.33), channel_id=1, source_target_pairs={{0,1},{1,0},{2,3},{3,2},{4,5},{5,4},{6,7},{7,6},{8,9},{9,8},{10,11... | collective-permute-start | bytes 1253384 | tf_op jit(solution)/shard_map/ppermute | solution.py:474
  4.1 0.8 %tables.1 = (bf16[33,64,128]{2,1,0:T(8,128)(2,1)S(1)}, bf16[2,96,128]{2,1,0:T(8,128)(2,1)S(1)}, f32[24,80,128]{2,1,0:T(8,128)S(1)}, f32[24,80,128]{2,1,0:T(8,128)S(1)}, f32[9,80,128]{2,1,0:T(8,128)S(1)}) custom-call(s32[1]{0:T(128)} %bitcast.index_ref, bf16[33,33,33]{2,1,0:T(8,128)(2,1)S(1)} %get-tuple-element.34.pair_ref, ...), custom_call_target="tpu_custom_call" | custom-call | flops 1000000 | bytes 8000000 | tf_op jit(solution)/shard_map/tables/pallas_call | solution.py:482
  4.9 0.6 collective-permute-done.other_ref
  5.4 7.2 %first_substep.1 = (f32[5,8,80,128]{3,2,1,0:T(8,128)S(1)}, bf16[168,128]{1,0:T(8,128)(2,1)S(1)}, f32[3200,128]{1,0:T(8,128)S(1)}, f32[5,16,1,128]{3,2,1,0:T(1,128)S(1)}, f32[5,1,128]{2,1,0:T(1,128)S(1)}) custom-call(s32[1]{0:T(128)} %bitcast.index_ref, bf16[2,34,8,384]{3,2,1,0:T(8,128)(2,1)S(1)} %get-tuple-element.31.own_ref, ...), custom_call_target="tpu_custom_call" | custom-call | flops 1874329600 | bytes 4000000 | tf_op jit(solution)/shard_map/first_substep/pallas_call | solution.py:502
  12.6 1.9 %collective-permute-start.2 = (bf16[168,128]{1,0:T(8,128)(2,1)S(1)}, bf16[168,128]{1,0:T(8,128)(2,1)S(1)}, u32[]{:S(2)}, u32[]{:S(2)}) collective-permute-start(bf16[168,128]{1,0:T(8,128)(2,1)S(1)} %get-tuple-element.45.flux_ref), channel_id=1, source_target_pairs={{0,4},{1,5},{2,0},{3,1},{4,2},{5,3},{6,10},{7,11},{10,8},{11,9},{1... | collective-permute-start | bytes 129032 | tf_op jit(solution)/shard_map/ppermute | solution.py:544
  14.6 4.3 %collective-permute-start.1 = (bf16[168,128]{1,0:T(8,128)(2,1)S(1)}, bf16[168,128]{1,0:T(8,128)(2,1)S(1)}, u32[]{:S(2)}, u32[]{:S(2)}) collective-permute-start(bf16[168,128]{1,0:T(8,128)(2,1)S(1)} %get-tuple-element.45.flux_ref), channel_id=1, source_target_pairs={{0,2},{1,3},{2,4},{3,5},{4,0},{5,1},{6,8},{7,9},{8,10},{9,11},{12,... | collective-permute-start | bytes 129032 | tf_op jit(solution)/shard_map/ppermute | solution.py:544
  18.8 1.2 %scan_weights.1 = (f32[24,80,128]{2,1,0:T(8,128)S(1)}, f32[7,168,128]{2,1,0:T(8,128)S(1)}) custom-call(s32[1]{0:T(128)} %bitcast.index_ref, f32[2,33]{1,0:T(2,128)S(1)} %get-tuple-element.37.fall_ref, f32[1,128]{1,0:T(1,128)S(1)} %get-tuple-element.38.dens_ref, f32[24,80,128]{2,1,0:T(8,128)S(1)} %get-tuple-element.41.courant_ref, ...), custom_call_target="tpu_custom_call" | custom-call | flops 1000000 | bytes 8000000 | tf_op jit(solution)/shard_map/scan_weights/pallas_call | solution.py:518
  20.1 0.0 collective-permute-done.2.got2_ref
  20.1 0.0 collective-permute-done.1.got1_ref
  20.1 8.6 %collective-permute-start.4 = (bf16[168,128]{1,0:T(8,128)(2,1)S(1)}, bf16[168,128]{1,0:T(8,128)(2,1)S(1)}, u32[]{:S(2)}, u32[]{:S(2)}) collective-permute-start(bf16[168,128]{1,0:T(8,128)(2,1)S(1)} %get-tuple-element.48), channel_id=1, source_target_pairs={{0,6},{1,7},{4,10},{5,11},{8,12},{9,13},{10,14},{11,15},{16,22},{1... | collective-permute-start | bytes 129032 | tf_op jit(solution)/shard_map/ppermute | solution.py:553
  28.8 1.3 %collective-permute-start.3 = (bf16[168,128]{1,0:T(8,128)(2,1)S(1)}, bf16[168,128]{1,0:T(8,128)(2,1)S(1)}, u32[]{:S(2)}, u32[]{:S(2)}) collective-permute-start(bf16[168,128]{1,0:T(8,128)(2,1)S(1)} %get-tuple-element.48), channel_id=1, source_target_pairs={{4,8},{5,9},{0,12},{1,13},{2,14},{3,15},{20,24},{21,25},{16,28},{1... | collective-permute-start | bytes 129032 | tf_op jit(solution)/shard_map/ppermute | solution.py:553
  30.1 0.0 collective-permute-done.4.near_ref
  30.1 1.4 %collective-permute-done.3.far_ref = bf16[168,128]{1,0:T(8,128)(2,1)S(1)} collective-permute-done((bf16[168,128]{1,0:T(8,128)(2,1)S(1)}, bf16[168,128]{1,0:T(8,128)(2,1)S(1)}, u32[]{:S(2)}, u32[]{:S(2)}) %collective-permute-start.3) | collective-permute-done | bytes 43040 | tf_op jit(solution)/shard_map/ppermute | solution.py:553
  31.5 6.9 %second_substep.1 = (f32[5,8,80,128]{3,2,1,0:T(8,128)S(1)}, bf16[168,128]{1,0:T(8,128)(2,1)S(1)}) custom-call(f32[5,8,80,128]{3,2,1,0:T(8,128)S(1)} %get-tuple-element.44.state_in, f32[168,128]{1,0:T(8,128)S(1)} %get-tuple-element.47.prefix_ref, bf16[168,128]{1,0:T(8,128)(2,1)S(1)} %collective-permute-done.3.far_ref, ...), custom_call_target="tpu_custom_call" | custom-call | flops 1874329600 | bytes 4000000 | tf_op jit(solution)/shard_map/second_substep/pallas_call | solution.py:555
  38.4 1.9 %collective-permute-start.6 = (bf16[168,128]{1,0:T(8,128)(2,1)S(1)}, bf16[168,128]{1,0:T(8,128)(2,1)S(1)}, u32[]{:S(2)}, u32[]{:S(2)}) collective-permute-start(bf16[168,128]{1,0:T(8,128)(2,1)S(1)} %get-tuple-element.54.flux_ref), channel_id=1, source_target_pairs={{0,4},{1,5},{4,2},{5,3},{6,10},{7,11},{10,8},{11,9},{16,20},{17,21... | collective-permute-start | bytes 129032 | tf_op jit(solution)/shard_map/ppermute | solution.py:544
  40.3 1.3 %collective-permute-start.5 = (bf16[168,128]{1,0:T(8,128)(2,1)S(1)}, bf16[168,128]{1,0:T(8,128)(2,1)S(1)}, u32[]{:S(2)}, u32[]{:S(2)}) collective-permute-start(bf16[168,128]{1,0:T(8,128)(2,1)S(1)} %get-tuple-element.54.flux_ref), channel_id=1, source_target_pairs={{0,2},{1,3},{2,4},{3,5},{6,8},{7,9},{8,10},{9,11},{12,14},{13,15},... | collective-permute-start | bytes 129032 | tf_op jit(solution)/shard_map/ppermute | solution.py:544
  41.6 2.4 %collective-permute-done.6.got2_ref = bf16[168,128]{1,0:T(8,128)(2,1)S(1)} collective-permute-done((bf16[168,128]{1,0:T(8,128)(2,1)S(1)}, bf16[168,128]{1,0:T(8,128)(2,1)S(1)}, u32[]{:S(2)}, u32[]{:S(2)}) %collective-permute-start.6) | collective-permute-done | bytes 43040 | tf_op jit(solution)/shard_map/ppermute | solution.py:544
  44.1 1.0 %collective-permute-done.5.got1_ref = bf16[168,128]{1,0:T(8,128)(2,1)S(1)} collective-permute-done((bf16[168,128]{1,0:T(8,128)(2,1)S(1)}, bf16[168,128]{1,0:T(8,128)(2,1)S(1)}, u32[]{:S(2)}, u32[]{:S(2)}) %collective-permute-start.5) | collective-permute-done | bytes 43040 | tf_op jit(solution)/shard_map/ppermute | solution.py:544
  45.1 7.3 %collective-permute-start.9 = (bf16[168,128]{1,0:T(8,128)(2,1)S(1)}, bf16[168,128]{1,0:T(8,128)(2,1)S(1)}, u32[]{:S(2)}, u32[]{:S(2)}) collective-permute-start(bf16[168,128]{1,0:T(8,128)(2,1)S(1)} %get-tuple-element.56), channel_id=1, source_target_pairs={{2,6},{3,7},{4,10},{5,11},{8,12},{9,13},{10,14},{11,15},{18,22},{1... | collective-permute-start | bytes 129032 | tf_op jit(solution)/shard_map/ppermute | solution.py:553
  52.5 1.3 %collective-permute-start.8 = (bf16[168,128]{1,0:T(8,128)(2,1)S(1)}, bf16[168,128]{1,0:T(8,128)(2,1)S(1)}, u32[]{:S(2)}, u32[]{:S(2)}) collective-permute-start(bf16[168,128]{1,0:T(8,128)(2,1)S(1)} %get-tuple-element.56), channel_id=1, source_target_pairs={{4,8},{5,9},{2,14},{3,15},{20,24},{21,25},{18,30},{19,31},{36,40},... | collective-permute-start | bytes 129032 | tf_op jit(solution)/shard_map/ppermute | solution.py:553
  53.8 0.7 %collective-permute-start.7 = (bf16[168,128]{1,0:T(8,128)(2,1)S(1)}, bf16[168,128]{1,0:T(8,128)(2,1)S(1)}, u32[]{:S(2)}, u32[]{:S(2)}) collective-permute-start(bf16[168,128]{1,0:T(8,128)(2,1)S(1)} %get-tuple-element.56), channel_id=1, source_target_pairs={{2,12},{3,13},{18,28},{19,29},{34,44},{35,45},{50,60},{51,61},{66,... | collective-permute-start | bytes 129032 | tf_op jit(solution)/shard_map/ppermute | solution.py:553
  54.5 0.0 collective-permute-done.9.near_ref
  54.5 0.4 collective-permute-done.8.far_ref
  54.9 0.0 collective-permute-done.7.farther_ref
  54.9 0.6 tendencies_sent.1
  55.5 5.4 %collective-permute-start.10 = (bf16[2,33,8,384]{3,2,1,0:T(8,128)(2,1)S(1)}, bf16[2,33,8,384]{3,2,1,0:T(8,128)(2,1)S(1)}, u32[]{:S(2)}, u32[]{:S(2)}) collective-permute-start(bf16[2,33,8,384]{3,2,1,0:T(8,128)(2,1)S(1)} %tendencies_sent.1), channel_id=1, source_target_pairs={{0,1},{1,0},{2,3},{3,2},{4,5},{5,4},{6,7},{7,6},{8,9},{9,8},{10,11... | collective-permute-start | bytes 1216520 | tf_op jit(solution)/shard_map/ppermute | solution.py:583
  60.9 0.5 tendencies_kept.1.keep_ref
  61.4 0.9 %collective-permute-done.10.got_ref = bf16[2,33,8,384]{3,2,1,0:T(8,128)(2,1)S(1)} collective-permute-done((bf16[2,33,8,384]{3,2,1,0:T(8,128)(2,1)S(1)}, bf16[2,33,8,384]{3,2,1,0:T(8,128)(2,1)S(1)}, u32[]{:S(2)}, u32[]{:S(2)}) %collective-permute-start.10) | collective-permute-done | bytes 405536 | tf_op jit(solution)/shard_map/ppermute | solution.py:583
  62.2 0.9 %merge_slabs.1 = bf16[2,33,8,640]{3,2,1,0:T(8,128)(2,1)} custom-call(s32[1]{0:T(128)} %bitcast.index_ref, bf16[2,33,8,384]{3,2,1,0:T(8,128)(2,1)S(1)} %tendencies_kept.1.keep_ref, bf16[2,33,8,384]{3,2,1,0:T(8,128)(2,1)S(1)} %collective-permute-done.10.got_ref), custom_call_target="tpu_custom_call" | custom-call | flops 1000000 | bytes 8000000 | tf_op jit(solution)/shard_map/merge_slabs/pallas_call | solution.py:584
  (2 shorter events, 0.1 us)
Async XLA Ops:
  1.5 4.0 %collective-permute-start = (bf16[2,34,8,384]{3,2,1,0:T(8,128)(2,1)S(1)}, bf16[2,34,8,384]{3,2,1,0:T(8,128)(2,1)S(1)}, u32[]{:S(2)}, u32[]{:S(2)}) collective-permute-start(bf16[2,34,8,384]{3,2,1,0:T(8,128)(2,1)S(1)} %get-tuple-element.33), channel_id=1, source_target_pairs={{0,1},{1,0},{2,3},{3,2},{4,5},{5,4},{6,7},{7,6},{8,9},{9,8},{10,11... | collective-permute-start | bytes 1253384 | tf_op jit(solution)/shard_map/ppermute | solution.py:474
  12.6 7.4 %collective-permute-start.2 = (bf16[168,128]{1,0:T(8,128)(2,1)S(1)}, bf16[168,128]{1,0:T(8,128)(2,1)S(1)}, u32[]{:S(2)}, u32[]{:S(2)}) collective-permute-start(bf16[168,128]{1,0:T(8,128)(2,1)S(1)} %get-tuple-element.45.flux_ref), channel_id=1, source_target_pairs={{0,4},{1,5},{2,0},{3,1},{4,2},{5,3},{6,10},{7,11},{10,8},{11,9},{1... | collective-permute-start | bytes 129032 | tf_op jit(solution)/shard_map/ppermute | solution.py:544
  14.6 5.5 %collective-permute-start.1 = (bf16[168,128]{1,0:T(8,128)(2,1)S(1)}, bf16[168,128]{1,0:T(8,128)(2,1)S(1)}, u32[]{:S(2)}, u32[]{:S(2)}) collective-permute-start(bf16[168,128]{1,0:T(8,128)(2,1)S(1)} %get-tuple-element.45.flux_ref), channel_id=1, source_target_pairs={{0,2},{1,3},{2,4},{3,5},{4,0},{5,1},{6,8},{7,9},{8,10},{9,11},{12,... | collective-permute-start | bytes 129032 | tf_op jit(solution)/shard_map/ppermute | solution.py:544
  20.1 10.0 %collective-permute-start.4 = (bf16[168,128]{1,0:T(8,128)(2,1)S(1)}, bf16[168,128]{1,0:T(8,128)(2,1)S(1)}, u32[]{:S(2)}, u32[]{:S(2)}) collective-permute-start(bf16[168,128]{1,0:T(8,128)(2,1)S(1)} %get-tuple-element.48), channel_id=1, source_target_pairs={{0,6},{1,7},{4,10},{5,11},{8,12},{9,13},{10,14},{11,15},{16,22},{1... | collective-permute-start | bytes 129032 | tf_op jit(solution)/shard_map/ppermute | solution.py:553
  28.8 2.7 %collective-permute-start.3 = (bf16[168,128]{1,0:T(8,128)(2,1)S(1)}, bf16[168,128]{1,0:T(8,128)(2,1)S(1)}, u32[]{:S(2)}, u32[]{:S(2)}) collective-permute-start(bf16[168,128]{1,0:T(8,128)(2,1)S(1)} %get-tuple-element.48), channel_id=1, source_target_pairs={{4,8},{5,9},{0,12},{1,13},{2,14},{3,15},{20,24},{21,25},{16,28},{1... | collective-permute-start | bytes 129032 | tf_op jit(solution)/shard_map/ppermute | solution.py:553
  38.4 5.7 %collective-permute-start.6 = (bf16[168,128]{1,0:T(8,128)(2,1)S(1)}, bf16[168,128]{1,0:T(8,128)(2,1)S(1)}, u32[]{:S(2)}, u32[]{:S(2)}) collective-permute-start(bf16[168,128]{1,0:T(8,128)(2,1)S(1)} %get-tuple-element.54.flux_ref), channel_id=1, source_target_pairs={{0,4},{1,5},{4,2},{5,3},{6,10},{7,11},{10,8},{11,9},{16,20},{17,21... | collective-permute-start | bytes 129032 | tf_op jit(solution)/shard_map/ppermute | solution.py:544
  40.3 4.8 %collective-permute-start.5 = (bf16[168,128]{1,0:T(8,128)(2,1)S(1)}, bf16[168,128]{1,0:T(8,128)(2,1)S(1)}, u32[]{:S(2)}, u32[]{:S(2)}) collective-permute-start(bf16[168,128]{1,0:T(8,128)(2,1)S(1)} %get-tuple-element.54.flux_ref), channel_id=1, source_target_pairs={{0,2},{1,3},{2,4},{3,5},{6,8},{7,9},{8,10},{9,11},{12,14},{13,15},... | collective-permute-start | bytes 129032 | tf_op jit(solution)/shard_map/ppermute | solution.py:544
  45.1 9.3 %collective-permute-start.9 = (bf16[168,128]{1,0:T(8,128)(2,1)S(1)}, bf16[168,128]{1,0:T(8,128)(2,1)S(1)}, u32[]{:S(2)}, u32[]{:S(2)}) collective-permute-start(bf16[168,128]{1,0:T(8,128)(2,1)S(1)} %get-tuple-element.56), channel_id=1, source_target_pairs={{2,6},{3,7},{4,10},{5,11},{8,12},{9,13},{10,14},{11,15},{18,22},{1... | collective-permute-start | bytes 129032 | tf_op jit(solution)/shard_map/ppermute | solution.py:553
  52.5 2.4 %collective-permute-start.8 = (bf16[168,128]{1,0:T(8,128)(2,1)S(1)}, bf16[168,128]{1,0:T(8,128)(2,1)S(1)}, u32[]{:S(2)}, u32[]{:S(2)}) collective-permute-start(bf16[168,128]{1,0:T(8,128)(2,1)S(1)} %get-tuple-element.56), channel_id=1, source_target_pairs={{4,8},{5,9},{2,14},{3,15},{20,24},{21,25},{18,30},{19,31},{36,40},... | collective-permute-start | bytes 129032 | tf_op jit(solution)/shard_map/ppermute | solution.py:553
  53.8 1.1 %collective-permute-start.7 = (bf16[168,128]{1,0:T(8,128)(2,1)S(1)}, bf16[168,128]{1,0:T(8,128)(2,1)S(1)}, u32[]{:S(2)}, u32[]{:S(2)}) collective-permute-start(bf16[168,128]{1,0:T(8,128)(2,1)S(1)} %get-tuple-element.56), channel_id=1, source_target_pairs={{2,12},{3,13},{18,28},{19,29},{34,44},{35,45},{50,60},{51,61},{66,... | collective-permute-start | bytes 129032 | tf_op jit(solution)/shard_map/ppermute | solution.py:553
  55.5 6.8 %collective-permute-start.10 = (bf16[2,33,8,384]{3,2,1,0:T(8,128)(2,1)S(1)}, bf16[2,33,8,384]{3,2,1,0:T(8,128)(2,1)S(1)}, u32[]{:S(2)}, u32[]{:S(2)}) collective-permute-start(bf16[2,33,8,384]{3,2,1,0:T(8,128)(2,1)S(1)} %tendencies_sent.1), channel_id=1, source_target_pairs={{0,1},{1,0},{2,3},{3,2},{4,5},{5,4},{6,7},{7,6},{8,9},{9,8},{10,11... | collective-permute-start | bytes 1216520 | tf_op jit(solution)/shard_map/ppermute | solution.py:583

commit v3 on v2

--- a/solution.py
+++ b/solution.py
@@ -17,7 +17,16 @@
 SENT = BINS + 1
 UNITS = 5
 CHIPS = 8
-GROUP = 3
+GROUPS = ((0, 3), (3, 2), (5, 3))
+FIRST_SCAN = (
+    ([(0, 1), (1, 2), (2, 0), (3, 4), (4, 3), (5, 6), (6, 7)], [(0, 2), (1, 0), (2, 1), (5, 7)]),
+    ([(1, 3), (2, 4), (3, 5), (0, 6), (4, 7)], [(0, 5), (4, 6), (1, 7)]),
+)
+LAST_SCAN = (
+    ([(0, 1), (1, 2), (3, 4), (4, 3), (5, 6), (6, 7)], [(0, 2), (2, 1), (5, 7)]),
+    ([(1, 3), (2, 4), (3, 5), (4, 6)], [(1, 7), (2, 5)], [(2, 6), (4, 7)]),
+)
+SUMS = FIRST_SCAN[1] + LAST_SCAN[1]
 DEVS = 2 * CHIPS
 FLAT = 168
 DEPTH = 11
@@ -123,10 +132,11 @@
     def product(first, end):
         return lax.fori_loop(first, end, lambda e, w: w * factor_ref[e], one)
 
-    place = chip % GROUP
-    first = chip - place
-    size = jnp.minimum(GROUP, CHIPS - first)
-    for r in range(GROUP):
+    first, size = jnp.int32(GROUPS[0][0]), jnp.int32(GROUPS[0][1])
+    for start, count in GROUPS[1:]:
+        first, size = jnp.where(chip >= start, start, first), jnp.where(chip >= start, count, size)
+    place = chip - first
+    for r in range(3):
         there = jnp.where(place >= r, place - r, place - r + size)
         fits = there >= 0
         if r > 0:
@@ -134,9 +144,13 @@
             weight_ref[r - 1] = flat_of(w, w, w)
         w = jnp.where(fits, product(first + there + 1, first + size), 0.0)
         weight_ref[2 + r] = flat_of(w, w, w)
-    for at, start in ((5, first), (6, GROUP)):
-        w = jnp.where(first >= GROUP, product(start, chip), 0.0)
-        weight_ref[at] = flat_of(w, w, w)
+    into = []
+    for start, _ in GROUPS[1:]:
+        w = jnp.where(chip >= start, product(start, chip), 0.0)
+        into.append(flat_of(w, w, w))
+    for n, pairs in enumerate(SUMS):
+        of_first = functools.reduce(jnp.logical_or, [chip == b for a, b in pairs if a < GROUPS[1][0]], False)
+        weight_ref[5 + n] = jnp.where(of_first, into[0], into[1])
 
 
 def pack_weights(pair_ref, rime_ref, growth_ref, wide_ref, slim_ref, main_ref, rest_ref):
@@ -259,9 +273,10 @@
     flux_ref[...] = flat_of(a, b, packed).astype(BF16)
 
 
-def arrivals(prefix_ref, far_refs, near_ref, weight_ref):
-    far = sum(ref[...].astype(F32) for ref in far_refs)
-    flux = prefix_ref[...] + weight_ref[5] * near_ref[...].astype(F32) + weight_ref[6] * far
+def arrivals(prefix_ref, got_refs, weight_ref, at):
+    flux = prefix_ref[...]
+    for n, ref in enumerate(reversed(got_refs)):
+        flux = flux + weight_ref[at + n] * ref[...].astype(F32)
     pieces = from_flat(flux)
     middle = pieces[4]
     other = turned(middle)
@@ -366,7 +381,7 @@
         state_ref[u, l] = state
         round_ref[u, l] = state.astype(BF16).astype(F32)
 
-    with_arrivals(state_in, arrive_ref, arrivals(prefix_ref, (far_ref,), near_ref, weight_ref), put)
+    with_arrivals(state_in, arrive_ref, arrivals(prefix_ref, (far_ref, near_ref), weight_ref, 5), put)
     substep(round_ref, state_ref, state_ref, sat_ref, flag_ref, main_ref, rest_ref)
     settle(state_ref, courant_ref, inverse_ref, lower_ref, flux_ref)
 
@@ -385,7 +400,7 @@
 ):
     core = index_ref[0] % 2
     slab = core if of_own else 1 - core
-    fluxes = arrivals(prefix_ref, (farther_ref, far_ref), near_ref, weight_ref)
+    fluxes = arrivals(prefix_ref, (farther_ref, far_ref, near_ref), weight_ref, 5 + len(FIRST_SCAN[1]))
     for k in range(3):
         u = 2 * k + slab if k < 2 else 4
         for l in range(SLAB):
@@ -519,7 +534,7 @@
         weight_kernel,
         in_specs=[SMEM] + [VMEM] * 4 + [pl.BlockSpec(memory_space=pl.ANY)],
         out_specs=[VMEM] * 2,
-        out_shape=[level_shape, shaped((7, FLAT, LANES))],
+        out_shape=[level_shape, shaped((5 + len(SUMS), FLAT, LANES))],
         scratch_shapes=[pltpu.VMEM((CHIPS, ROWS, LANES), F32)],
         compiler_params=PARAMS,
         cost_estimate=light,
@@ -529,19 +544,9 @@
     def between(pairs):
         return [(2 * a + c, 2 * b + c) for a, b in pairs for c in range(2)]
 
-    def around(r, without):
-        pairs = []
-        for first in range(0, CHIPS, GROUP):
-            size = min(GROUP, CHIPS - first)
-            pairs += [(first + p, first + (p + r) % size) for p in range(size) if r < size]
-        return between([(a, b) for a, b in pairs if b not in without])
-
-    first_scan = (3, 6), ([(2, 4), (0, 6), (1, 7)], [(0, 3), (2, 5), (4, 6), (5, 7)])
-    last_scan = (0, 3, 6), ([(1, 6)], [(2, 4), (1, 7)], [(1, 3), (2, 5), (4, 6), (5, 7)])
-
     def scan(flux, plan):
-        without, sums = plan
-        got = [lax.ppermute(flux, "lat", around(r, without)) for r in range(1, GROUP)]
+        own, sums = plan
+        got = [lax.ppermute(flux, "lat", between(pairs)) for pairs in own]
         prefix, send = pl.pallas_call(
             group_kernel,
             in_specs=[VMEM] * 4,
@@ -550,7 +555,7 @@
             compiler_params=PARAMS,
             name="scan_group",
         )(flux, *got, weight)
-        return prefix, *(lax.ppermute(send, "lat", between(pairs)) for pairs in sums)
+        return prefix, *(lax.ppermute(send, "lat", between(pairs)) for pairs in reversed(sums))
 
     state, flux = pl.pallas_call(
         second_kernel,
@@ -561,9 +566,9 @@
         compiler_params=PARAMS,
         cost_estimate=cost,
         name="second_substep",
-    )(state, *scan(flux, first_scan), weight, sat, flags, main, rest, courant, inverse, arrive, lower)
-
-    arrived = scan(flux, last_scan)
+    )(state, *scan(flux, FIRST_SCAN), weight, sat, flags, main, rest, courant, inverse, arrive, lower)
+
+    arrived = scan(flux, LAST_SCAN)
 
     def tendencies(of_own, name):
         return pl.pallas_call(

time: 63.4 us -> 62.5 us (0.986)
  the two profiles are of different devices: /device:TPU:183 before, /device:TPU:173 now
where the time goes in v3:
time: 62.5 us; the launch traced here: 62.2 us
  starting transfers between devices  36.2 us (58%)
  Pallas kernels  19.5 us (31%)
  waiting for transfers between devices  6.4 us (10%)
    ppermute x5, starting transfers between devices, scan(): lax.ppermute(send, 'lat', between(pairs))  14.8 us
    ppermute x4, starting transfers between devices, scan(): got = [lax.ppermute(flux, 'lat', between(pairs)) for pairs in own]  13.1 us
    pallas_call x1, Pallas kernels, local(): pl.pallas_call(first_kernel, in_specs=[SMEM] + [VMEM] * 8, out_specs=[VME...  7.1 us
    pallas_call x1, Pallas kernels, local(): pl.pallas_call(second_kernel, in_specs=[VMEM] * 13, out_specs=[VMEM] * 2,...  6.91 us
    ppermute x1, starting transfers between devices, local(): got = lax.ppermute(send, 'lat', swap)  5.71 us
    ppermute x4, waiting for transfers between devices, scan(): got = [lax.ppermute(flux, 'lat', between(pairs)) for pairs in own]  3.47 us
    ppermute x1, starting transfers between devices, local(): other = lax.ppermute(sent, 'lat', swap)  2.58 us
    ppermute x5, waiting for transfers between devices, scan(): lax.ppermute(send, 'lat', between(pairs))  1.52 us
  transfers between devices with their start and end apart: 11, of which 5 were waited for; matrix products, arithmetic and copies ran while one was open for 0% of the time, Pallas kernels for 4%

profile of v3, /device:TPU:173, one launch (start us, length us, event | category | flops | bytes accessed | tf_op | source)
XLA Modules:
  0.0 62.2 jit_solution(12698223142853009674)
XLA Ops:
  0.0 1.5 %load_arguments.1 = (bf16[2,34,8,384]{3,2,1,0:T(8,128)(2,1)S(1)}, bf16[2,34,8,384]{3,2,1,0:T(8,128)(2,1)S(1)}, s32[5,128]{1,0:T(8,128)S(1)}, bf16[33,33,33]{2,1,...) custom-call(s32[1]{0:T(128)} %bitcast.index_ref, ...), custom_call_target="tpu_custom_call" | custom-call | tf_op jit(solution)/shard_map/load_arguments/pallas_call | solution.py:468
  1.5 2.6 %collective-permute-start = (bf16[2,34,8,384]{3,2,1,0:T(8,128)(2,1)S(1)}, bf16[2,34,8,384]{3,2,1,0:T(8,128)(2,1)S(1)}, u32[]{:S(2)}, u32[]{:S(2)}) collective-permute-start(bf16[2,34,8,384]{3,2,1,0:T(8,128)(2,1)S(1)} %get-tuple-element.33), channel_id=1, source_target_pairs={{0,1},{1,0},{2,3},{3,2},{4,5},{5,4},{6,7},{7,6},{8,9},{9,8},{10,11... | collective-permute-start | bytes 1253384 | tf_op jit(solution)/shard_map/ppermute | solution.py:489
  4.1 0.8 %tables.1 = (bf16[33,64,128]{2,1,0:T(8,128)(2,1)S(1)}, bf16[2,96,128]{2,1,0:T(8,128)(2,1)S(1)}, f32[24,80,128]{2,1,0:T(8,128)S(1)}, f32[24,80,128]{2,1,0:T(8,128)S(1)}, f32[9,80,128]{2,1,0:T(8,128)S(1)}) custom-call(s32[1]{0:T(128)} %bitcast.index_ref, bf16[33,33,33]{2,1,0:T(8,128)(2,1)S(1)} %get-tuple-element.34.pair_ref, ...), custom_call_target="tpu_custom_call" | custom-call | flops 1000000 | bytes 8000000 | tf_op jit(solution)/shard_map/tables/pallas_call | solution.py:497
  4.9 0.6 collective-permute-done.other_ref
  5.4 7.1 %first_substep.1 = (f32[5,8,80,128]{3,2,1,0:T(8,128)S(1)}, bf16[168,128]{1,0:T(8,128)(2,1)S(1)}, f32[3200,128]{1,0:T(8,128)S(1)}, f32[5,16,1,128]{3,2,1,0:T(1,128)S(1)}, f32[5,1,128]{2,1,0:T(1,128)S(1)}) custom-call(s32[1]{0:T(128)} %bitcast.index_ref, bf16[2,34,8,384]{3,2,1,0:T(8,128)(2,1)S(1)} %get-tuple-element.31.own_ref, ...), custom_call_target="tpu_custom_call" | custom-call | flops 1874329600 | bytes 4000000 | tf_op jit(solution)/shard_map/first_substep/pallas_call | solution.py:517
  12.6 1.9 %collective-permute-start.2 = (bf16[168,128]{1,0:T(8,128)(2,1)S(1)}, bf16[168,128]{1,0:T(8,128)(2,1)S(1)}, u32[]{:S(2)}, u32[]{:S(2)}) collective-permute-start(bf16[168,128]{1,0:T(8,128)(2,1)S(1)} %get-tuple-element.45.flux_ref), channel_id=1, source_target_pairs={{0,4},{1,5},{2,0},{3,1},{4,2},{5,3},{10,14},{11,15},{16,20},{17,21... | collective-permute-start | bytes 129032 | tf_op jit(solution)/shard_map/ppermute | solution.py:549
  14.5 4.3 %collective-permute-start.1 = (bf16[168,128]{1,0:T(8,128)(2,1)S(1)}, bf16[168,128]{1,0:T(8,128)(2,1)S(1)}, u32[]{:S(2)}, u32[]{:S(2)}) collective-permute-start(bf16[168,128]{1,0:T(8,128)(2,1)S(1)} %get-tuple-element.45.flux_ref), channel_id=1, source_target_pairs={{0,2},{1,3},{2,4},{3,5},{4,0},{5,1},{6,8},{7,9},{8,6},{9,7},{10,12... | collective-permute-start | bytes 129032 | tf_op jit(solution)/shard_map/ppermute | solution.py:549
  18.8 1.2 %scan_weights.1 = (f32[24,80,128]{2,1,0:T(8,128)S(1)}, f32[10,168,128]{2,1,0:T(8,128)S(1)}) custom-call(s32[1]{0:T(128)} %bitcast.index_ref, f32[2,33]{1,0:T(2,128)S(1)} %get-tuple-element.37.fall_ref, f32[1,128]{1,0:T(1,128)S(1)} %get-tuple-element.38.dens_ref, f32[24,80,128]{2,1,0:T(8,128)S(1)} %get-tuple-element.41.courant_ref, ...), custom_call_target="tpu_custom_call" | custom-call | flops 1000000 | bytes 8000000 | tf_op jit(solution)/shard_map/scan_weights/pallas_call | solution.py:533
  20.0 0.0 collective-permute-done.2.got2_ref
  20.0 0.0 collective-permute-done.1.got1_ref
  20.1 6.2 %collective-permute-start.4 = (bf16[168,128]{1,0:T(8,128)(2,1)S(1)}, bf16[168,128]{1,0:T(8,128)(2,1)S(1)}, u32[]{:S(2)}, u32[]{:S(2)}) collective-permute-start(bf16[168,128]{1,0:T(8,128)(2,1)S(1)} %get-tuple-element.48), channel_id=1, source_target_pairs={{2,6},{3,7},{4,8},{5,9},{6,10},{7,11},{0,12},{1,13},{8,14},{9,15},... | collective-permute-start | bytes 129032 | tf_op jit(solution)/shard_map/ppermute | solution.py:558
  26.3 0.7 %collective-permute-start.3 = (bf16[168,128]{1,0:T(8,128)(2,1)S(1)}, bf16[168,128]{1,0:T(8,128)(2,1)S(1)}, u32[]{:S(2)}, u32[]{:S(2)}) collective-permute-start(bf16[168,128]{1,0:T(8,128)(2,1)S(1)} %get-tuple-element.48), channel_id=1, source_target_pairs={{0,10},{1,11},{8,12},{9,13},{2,14},{3,15},{16,26},{17,27},{24,28},... | collective-permute-start | bytes 129032 | tf_op jit(solution)/shard_map/ppermute | solution.py:558
  27.0 0.4 collective-permute-done.4.near_ref
  27.4 0.0 collective-permute-done.3.far_ref
  27.4 6.9 %second_substep.1 = (f32[5,8,80,128]{3,2,1,0:T(8,128)S(1)}, bf16[168,128]{1,0:T(8,128)(2,1)S(1)}) custom-call(f32[5,8,80,128]{3,2,1,0:T(8,128)S(1)} %get-tuple-element.44.state_in, f32[168,128]{1,0:T(8,128)S(1)} %get-tuple-element.47.prefix_ref, bf16[168,128]{1,0:T(8,128)(2,1)S(1)} %collective-permute-done.3.far_ref, ...), custom_call_target="tpu_custom_call" | custom-call | flops 1874329600 | bytes 4000000 | tf_op jit(solution)/shard_map/second_substep/pallas_call | solution.py:560
  34.3 5.6 %collective-permute-start.6 = (bf16[168,128]{1,0:T(8,128)(2,1)S(1)}, bf16[168,128]{1,0:T(8,128)(2,1)S(1)}, u32[]{:S(2)}, u32[]{:S(2)}) collective-permute-start(bf16[168,128]{1,0:T(8,128)(2,1)S(1)} %get-tuple-element.54.flux_ref), channel_id=1, source_target_pairs={{0,4},{1,5},{4,2},{5,3},{10,14},{11,15},{16,20},{17,21},{20,18},{2... | collective-permute-start | bytes 129032 | tf_op jit(solution)/shard_map/ppermute | solution.py:549
  39.9 1.3 %collective-permute-start.5 = (bf16[168,128]{1,0:T(8,128)(2,1)S(1)}, bf16[168,128]{1,0:T(8,128)(2,1)S(1)}, u32[]{:S(2)}, u32[]{:S(2)}) collective-permute-start(bf16[168,128]{1,0:T(8,128)(2,1)S(1)} %get-tuple-element.54.flux_ref), channel_id=1, source_target_pairs={{0,2},{1,3},{2,4},{3,5},{6,8},{7,9},{8,6},{9,7},{10,12},{11,13},{1... | collective-permute-start | bytes 129032 | tf_op jit(solution)/shard_map/ppermute | solution.py:549
  41.2 0.0 collective-permute-done.6.got2_ref
  41.2 3.5 %collective-permute-done.5.got1_ref = bf16[168,128]{1,0:T(8,128)(2,1)S(1)} collective-permute-done((bf16[168,128]{1,0:T(8,128)(2,1)S(1)}, bf16[168,128]{1,0:T(8,128)(2,1)S(1)}, u32[]{:S(2)}, u32[]{:S(2)}) %collective-permute-start.5) | collective-permute-done | bytes 43040 | tf_op jit(solution)/shard_map/ppermute | solution.py:549
  44.8 3.5 %collective-permute-start.9 = (bf16[168,128]{1,0:T(8,128)(2,1)S(1)}, bf16[168,128]{1,0:T(8,128)(2,1)S(1)}, u32[]{:S(2)}, u32[]{:S(2)}) collective-permute-start(bf16[168,128]{1,0:T(8,128)(2,1)S(1)} %get-tuple-element.56), channel_id=1, source_target_pairs={{2,6},{3,7},{4,8},{5,9},{6,10},{7,11},{8,12},{9,13},{18,22},{19,23... | collective-permute-start | bytes 129032 | tf_op jit(solution)/shard_map/ppermute | solution.py:558
  48.3 2.2 %collective-permute-start.8 = (bf16[168,128]{1,0:T(8,128)(2,1)S(1)}, bf16[168,128]{1,0:T(8,128)(2,1)S(1)}, u32[]{:S(2)}, u32[]{:S(2)}) collective-permute-start(bf16[168,128]{1,0:T(8,128)(2,1)S(1)} %get-tuple-element.56), channel_id=1, source_target_pairs={{2,14},{3,15},{4,10},{5,11},{18,30},{19,31},{20,26},{21,27},{34,46... | collective-permute-start | bytes 129032 | tf_op jit(solution)/shard_map/ppermute | solution.py:558
  50.5 2.1 %collective-permute-start.7 = (bf16[168,128]{1,0:T(8,128)(2,1)S(1)}, bf16[168,128]{1,0:T(8,128)(2,1)S(1)}, u32[]{:S(2)}, u32[]{:S(2)}) collective-permute-start(bf16[168,128]{1,0:T(8,128)(2,1)S(1)} %get-tuple-element.56), channel_id=1, source_target_pairs={{4,12},{5,13},{8,14},{9,15},{20,28},{21,29},{24,30},{25,31},{36,44... | collective-permute-start | bytes 129032 | tf_op jit(solution)/shard_map/ppermute | solution.py:558
  52.6 0.0 collective-permute-done.9.near_ref
  52.7 0.0 collective-permute-done.8.far_ref
  52.7 1.1 %collective-permute-done.7.farther_ref = bf16[168,128]{1,0:T(8,128)(2,1)S(1)} collective-permute-done((bf16[168,128]{1,0:T(8,128)(2,1)S(1)}, bf16[168,128]{1,0:T(8,128)(2,1)S(1)}, u32[]{:S(2)}, u32[]{:S(2)}) %collective-permute-start.7) | collective-permute-done | bytes 43040 | tf_op jit(solution)/shard_map/ppermute | solution.py:558
  53.7 0.5 tendencies_sent.1
  54.3 5.7 %collective-permute-start.10 = (bf16[2,33,8,384]{3,2,1,0:T(8,128)(2,1)S(1)}, bf16[2,33,8,384]{3,2,1,0:T(8,128)(2,1)S(1)}, u32[]{:S(2)}, u32[]{:S(2)}) collective-permute-start(bf16[2,33,8,384]{3,2,1,0:T(8,128)(2,1)S(1)} %tendencies_sent.1), channel_id=1, source_target_pairs={{0,1},{1,0},{2,3},{3,2},{4,5},{5,4},{6,7},{7,6},{8,9},{9,8},{10,11... | collective-permute-start | bytes 1216520 | tf_op jit(solution)/shard_map/ppermute | solution.py:588
  60.0 0.5 tendencies_kept.1.keep_ref
  60.5 0.9 %collective-permute-done.10.got_ref = bf16[2,33,8,384]{3,2,1,0:T(8,128)(2,1)S(1)} collective-permute-done((bf16[2,33,8,384]{3,2,1,0:T(8,128)(2,1)S(1)}, bf16[2,33,8,384]{3,2,1,0:T(8,128)(2,1)S(1)}, u32[]{:S(2)}, u32[]{:S(2)}) %collective-permute-start.10) | collective-permute-done | bytes 405536 | tf_op jit(solution)/shard_map/ppermute | solution.py:588
  61.3 0.9 %merge_slabs.1 = bf16[2,33,8,640]{3,2,1,0:T(8,128)(2,1)} custom-call(s32[1]{0:T(128)} %bitcast.index_ref, bf16[2,33,8,384]{3,2,1,0:T(8,128)(2,1)S(1)} %tendencies_kept.1.keep_ref, bf16[2,33,8,384]{3,2,1,0:T(8,128)(2,1)S(1)} %collective-permute-done.10.got_ref), custom_call_target="tpu_custom_call" | custom-call | flops 1000000 | bytes 8000000 | tf_op jit(solution)/shard_map/merge_slabs/pallas_call | solution.py:589
  (2 shorter events, 0.1 us)
Async XLA Ops:
  1.5 4.0 %collective-permute-start = (bf16[2,34,8,384]{3,2,1,0:T(8,128)(2,1)S(1)}, bf16[2,34,8,384]{3,2,1,0:T(8,128)(2,1)S(1)}, u32[]{:S(2)}, u32[]{:S(2)}) collective-permute-start(bf16[2,34,8,384]{3,2,1,0:T(8,128)(2,1)S(1)} %get-tuple-element.33), channel_id=1, source_target_pairs={{0,1},{1,0},{2,3},{3,2},{4,5},{5,4},{6,7},{7,6},{8,9},{9,8},{10,11... | collective-permute-start | bytes 1253384 | tf_op jit(solution)/shard_map/ppermute | solution.py:489
  12.6 7.4 %collective-permute-start.2 = (bf16[168,128]{1,0:T(8,128)(2,1)S(1)}, bf16[168,128]{1,0:T(8,128)(2,1)S(1)}, u32[]{:S(2)}, u32[]{:S(2)}) collective-permute-start(bf16[168,128]{1,0:T(8,128)(2,1)S(1)} %get-tuple-element.45.flux_ref), channel_id=1, source_target_pairs={{0,4},{1,5},{2,0},{3,1},{4,2},{5,3},{10,14},{11,15},{16,20},{17,21... | collective-permute-start | bytes 129032 | tf_op jit(solution)/shard_map/ppermute | solution.py:549
  14.5 5.5 %collective-permute-start.1 = (bf16[168,128]{1,0:T(8,128)(2,1)S(1)}, bf16[168,128]{1,0:T(8,128)(2,1)S(1)}, u32[]{:S(2)}, u32[]{:S(2)}) collective-permute-start(bf16[168,128]{1,0:T(8,128)(2,1)S(1)} %get-tuple-element.45.flux_ref), channel_id=1, source_target_pairs={{0,2},{1,3},{2,4},{3,5},{4,0},{5,1},{6,8},{7,9},{8,6},{9,7},{10,12... | collective-permute-start | bytes 129032 | tf_op jit(solution)/shard_map/ppermute | solution.py:549
  20.1 7.3 %collective-permute-start.4 = (bf16[168,128]{1,0:T(8,128)(2,1)S(1)}, bf16[168,128]{1,0:T(8,128)(2,1)S(1)}, u32[]{:S(2)}, u32[]{:S(2)}) collective-permute-start(bf16[168,128]{1,0:T(8,128)(2,1)S(1)} %get-tuple-element.48), channel_id=1, source_target_pairs={{2,6},{3,7},{4,8},{5,9},{6,10},{7,11},{0,12},{1,13},{8,14},{9,15},... | collective-permute-start | bytes 129032 | tf_op jit(solution)/shard_map/ppermute | solution.py:558
  26.3 1.1 %collective-permute-start.3 = (bf16[168,128]{1,0:T(8,128)(2,1)S(1)}, bf16[168,128]{1,0:T(8,128)(2,1)S(1)}, u32[]{:S(2)}, u32[]{:S(2)}) collective-permute-start(bf16[168,128]{1,0:T(8,128)(2,1)S(1)} %get-tuple-element.48), channel_id=1, source_target_pairs={{0,10},{1,11},{8,12},{9,13},{2,14},{3,15},{16,26},{17,27},{24,28},... | collective-permute-start | bytes 129032 | tf_op jit(solution)/shard_map/ppermute | solution.py:558
  34.3 6.9 %collective-permute-start.6 = (bf16[168,128]{1,0:T(8,128)(2,1)S(1)}, bf16[168,128]{1,0:T(8,128)(2,1)S(1)}, u32[]{:S(2)}, u32[]{:S(2)}) collective-permute-start(bf16[168,128]{1,0:T(8,128)(2,1)S(1)} %get-tuple-element.54.flux_ref), channel_id=1, source_target_pairs={{0,4},{1,5},{4,2},{5,3},{10,14},{11,15},{16,20},{17,21},{20,18},{2... | collective-permute-start | bytes 129032 | tf_op jit(solution)/shard_map/ppermute | solution.py:549
  39.9 4.8 %collective-permute-start.5 = (bf16[168,128]{1,0:T(8,128)(2,1)S(1)}, bf16[168,128]{1,0:T(8,128)(2,1)S(1)}, u32[]{:S(2)}, u32[]{:S(2)}) collective-permute-start(bf16[168,128]{1,0:T(8,128)(2,1)S(1)} %get-tuple-element.54.flux_ref), channel_id=1, source_target_pairs={{0,2},{1,3},{2,4},{3,5},{6,8},{7,9},{8,6},{9,7},{10,12},{11,13},{1... | collective-permute-start | bytes 129032 | tf_op jit(solution)/shard_map/ppermute | solution.py:549
  44.8 7.9 %collective-permute-start.9 = (bf16[168,128]{1,0:T(8,128)(2,1)S(1)}, bf16[168,128]{1,0:T(8,128)(2,1)S(1)}, u32[]{:S(2)}, u32[]{:S(2)}) collective-permute-start(bf16[168,128]{1,0:T(8,128)(2,1)S(1)} %get-tuple-element.56), channel_id=1, source_target_pairs={{2,6},{3,7},{4,8},{5,9},{6,10},{7,11},{8,12},{9,13},{18,22},{19,23... | collective-permute-start | bytes 129032 | tf_op jit(solution)/shard_map/ppermute | solution.py:558
  48.3 4.4 %collective-permute-start.8 = (bf16[168,128]{1,0:T(8,128)(2,1)S(1)}, bf16[168,128]{1,0:T(8,128)(2,1)S(1)}, u32[]{:S(2)}, u32[]{:S(2)}) collective-permute-start(bf16[168,128]{1,0:T(8,128)(2,1)S(1)} %get-tuple-element.56), channel_id=1, source_target_pairs={{2,14},{3,15},{4,10},{5,11},{18,30},{19,31},{20,26},{21,27},{34,46... | collective-permute-start | bytes 129032 | tf_op jit(solution)/shard_map/ppermute | solution.py:558
  50.5 3.2 %collective-permute-start.7 = (bf16[168,128]{1,0:T(8,128)(2,1)S(1)}, bf16[168,128]{1,0:T(8,128)(2,1)S(1)}, u32[]{:S(2)}, u32[]{:S(2)}) collective-permute-start(bf16[168,128]{1,0:T(8,128)(2,1)S(1)} %get-tuple-element.56), channel_id=1, source_target_pairs={{4,12},{5,13},{8,14},{9,15},{20,28},{21,29},{24,30},{25,31},{36,44... | collective-permute-start | bytes 129032 | tf_op jit(solution)/shard_map/ppermute | solution.py:558
  54.3 7.1 %collective-permute-start.10 = (bf16[2,33,8,384]{3,2,1,0:T(8,128)(2,1)S(1)}, bf16[2,33,8,384]{3,2,1,0:T(8,128)(2,1)S(1)}, u32[]{:S(2)}, u32[]{:S(2)}) collective-permute-start(bf16[2,33,8,384]{3,2,1,0:T(8,128)(2,1)S(1)} %tendencies_sent.1), channel_id=1, source_target_pairs={{0,1},{1,0},{2,3},{3,2},{4,5},{5,4},{6,7},{7,6},{8,9},{9,8},{10,11... | collective-permute-start | bytes 1216520 | tf_op jit(solution)/shard_map/ppermute | solution.py:588

commit v4 on v3

--- a/solution.py
+++ b/solution.py
@@ -29,7 +29,12 @@
 SUMS = FIRST_SCAN[1] + LAST_SCAN[1]
 DEVS = 2 * CHIPS
 FLAT = 168
-DEPTH = 11
+DEPTH = 10
+SQUARE = tuple(range(24, 32))
+SINGLES = tuple(i for i in range(BINS) if i not in SQUARE)
+PAIRS = tuple(zip(SQUARE[::2], SQUARE[1::2]))
+BLOCKS = len(SINGLES) + len(PAIRS) + 1
+PRODUCTS = 48
 F32 = jnp.float32
 BF16 = jnp.bfloat16
 
@@ -156,11 +161,34 @@
 def pack_weights(pair_ref, rime_ref, growth_ref, wide_ref, slim_ref, main_ref, rest_ref):
     for k in range(BINS):
         slim_ref[2 * k : 2 * k + 2, :] = padded(growth_ref[k].astype(F32), 2, LANES)
+    low, size = SQUARE[0], len(SQUARE)
+    lane = lax.broadcasted_iota(jnp.int32, (1, LANES), 1)
+    in_square = (lane >= low) & (lane < low + size)
     for at, source in ((0, pair_ref), (1, rime_ref)):
         for k in range(BINS - 1):
             wide_ref[HALF * k : HALF * (k + 1), :] = padded(source[k].astype(F32), HALF, LANES)
-        for i in range(BINS):
-            main_ref[i, 32 * at : 32 * (at + 1), :] = wide_ref[pl.ds(i, 32, stride=HALF), :].astype(BF16)
+        if at == 0:
+            products = jnp.zeros((32, LANES), F32)
+            for i in range(size):
+                rows = wide_ref[pl.ds(low + i, 32, stride=HALF), :]
+                products = products + pltpu.roll(jnp.where(in_square, rows, 0.0), PRODUCTS + size * i - low, 1)
+            main_ref[BLOCKS - 1, :32, :] = products.astype(BF16)
+            main_ref[BLOCKS - 1, 32:, :] = jnp.zeros((32, LANES), BF16)
+            for first in range(0, BINS - 1, LANES // size):
+                ks = range(first, min(first + LANES // size, BINS - 1))
+                turn = jnp.concatenate([wide_ref[HALF * k + low : HALF * k + low + size, :] for k in ks], axis=0).T
+                for n, k in enumerate(ks):
+                    shift = (low - size * n) % LANES
+                    extra = pltpu.roll(turn[:HALF], shift, 1) if shift else turn[:HALF]
+                    rows = slice(HALF * k, HALF * (k + 1))
+                    wide_ref[rows, :] = wide_ref[rows, :] + jnp.where(in_square, extra, 0.0)
+            for j, i in enumerate(SINGLES):
+                main_ref[j, :32, :] = wide_ref[pl.ds(i, 32, stride=HALF), :].astype(BF16)
+        else:
+            places = [(j, 32, i) for j, i in enumerate(SINGLES)]
+            places += [(len(SINGLES) + n, 32 * half, i) for n, pair in enumerate(PAIRS) for half, i in enumerate(pair)]
+            for j, row, i in places:
+                main_ref[j, row : row + 32, :] = wide_ref[pl.ds(i, 32, stride=HALF), :].astype(BF16)
         rest_ref[0, 48 * at : 48 * (at + 1), :] = padded(source[BINS - 1].astype(F32), 48, LANES).astype(BF16)
         grow = slim_ref[pl.ds(at, BINS, stride=2), :]
         rest_ref[1, 48 * at : 48 * (at + 1), :] = padded(grow, 48, LANES).astype(BF16)
@@ -190,49 +218,69 @@
         return jnp.concatenate([ref[block, l, rows, :] for l in levels[m]], axis=1)
 
     def scoped(*accs):
-        accs = (accs[: DEPTH + 2], accs[DEPTH + 2 :])
+        accs = (accs[: DEPTH + 3], accs[DEPTH + 3 :])
 
         def push(spot):
             empty = jnp.zeros((LANES - 48, 2 * LANES), BF16)
             for m in range(2):
                 liquid = padded(wide(round_ref, spot, slice(0, HALF), m), 48, 2 * LANES).astype(BF16)
+                square = wide(round_ref, spot, slice(SQUARE[0], SQUARE[-1] + 1), m)
+                products = [square * wide(round_ref, spot, slice(i, i + 1), m) for i in SQUARE]
+                products = padded(jnp.concatenate(products, axis=0), LANES - PRODUCTS, 2 * LANES).astype(BF16)
                 frozen = padded(wide(round_ref, spot, slice(HALF, ROWS), m), 48, 2 * LANES).astype(BF16)
-                pltpu.matmul_push_rhs(jnp.concatenate([liquid, empty, frozen, empty], axis=0), 0, m)
+                pltpu.matmul_push_rhs(jnp.concatenate([liquid, products, frozen, empty], axis=0), 0, m)
 
         def issue(j):
-            lhs = two_sided(main_ref[j] if j < BINS else rest_ref[j - BINS])
+            if j >= BLOCKS:
+                lhs = two_sided(rest_ref[j - BLOCKS])
+            elif j < len(SINGLES):
+                lhs = two_sided(main_ref[j])
+            elif j < BLOCKS - 1:
+                lhs = jnp.concatenate([jnp.zeros((64, LANES), BF16), main_ref[j]], axis=1)
+            else:
+                lhs = jnp.concatenate([main_ref[j, :32, :], jnp.zeros((32, LANES), BF16)], axis=1)
             for m in range(2):
-                acc = accs[m][j % DEPTH] if j < BINS else accs[m][DEPTH + j - BINS]
-                pltpu.matmul_acc_lhs(acc, lhs, load_staged_rhs=0 if j == 0 else None)
+                pltpu.matmul_acc_lhs(place_of(m, j), lhs, load_staged_rhs=0 if j == 0 else None)
+
+        def place_of(m, j):
+            return accs[m][j % DEPTH if j < BLOCKS - 1 else DEPTH + j - (BLOCKS - 1)]
 
         def body(step, carry):
             spot = place(step)
             block, levels = spot
             after = place(jnp.minimum(step + 1, steps - 1))
-            sums = [jnp.zeros((64, 2 * LANES), F32) for m in range(2)]
-            for i in range(BINS):
+            sums = [[jnp.zeros((32, 2 * LANES), F32) for s in range(2)] for m in range(2)]
+            for i in range(BLOCKS):
                 if i == DEPTH - 1:
                     push(after)
                 for m in range(2):
-                    term = pltpu.matmul_pop(accs[m][i % DEPTH])
-                    sums[m] = sums[m] + term * wide(round_ref, spot, slice(i, i + 1), m)
-                if i + DEPTH < BINS:
+                    term = pltpu.matmul_pop(place_of(m, i))
+                    if i < len(SINGLES):
+                        by = wide(round_ref, spot, slice(SINGLES[i], SINGLES[i] + 1), m)
+                        sums[m] = [sums[m][s] + term[32 * s : 32 * (s + 1)] * by for s in range(2)]
+                    elif i < BLOCKS - 1:
+                        for half, at in enumerate(PAIRS[i - len(SINGLES)]):
+                            by = wide(round_ref, spot, slice(at, at + 1), m)
+                            sums[m][1] = sums[m][1] + term[32 * half : 32 * (half + 1)] * by
+                    else:
+                        sums[m][0] = sums[m][0] + term
+                if i + DEPTH < BLOCKS:
                     issue(i + DEPTH)
                 else:
-                    if i + DEPTH == BINS:
-                        issue(BINS)
-                        issue(BINS + 1)
-                    issue(i + DEPTH - BINS)
+                    if i + DEPTH == BLOCKS:
+                        issue(BLOCKS)
+                        issue(BLOCKS + 1)
+                    issue(i + DEPTH - BLOCKS)
             flag = flag_ref[block]
             flag = jnp.concatenate([flag, flag], axis=1)
             for m in range(2):
-                last = pltpu.matmul_pop(accs[m][DEPTH])
-                grow = pltpu.matmul_pop(accs[m][DEPTH + 1])
+                last = pltpu.matmul_pop(place_of(m, BLOCKS))
+                grow = pltpu.matmul_pop(place_of(m, BLOCKS + 1))
                 liquid = wide(round_ref, spot, slice(0, HALF), m)
                 for s in range(2):
                     tail = jnp.sum(last[48 * s : 48 * s + HALF] * liquid, axis=0, keepdims=True)
                     tail = padded(tail, 8, 2 * LANES)
-                    gain = jnp.concatenate([sums[m][32 * s : 32 * (s + 1)], tail], axis=0) * flag
+                    gain = jnp.concatenate([sums[m][s], tail], axis=0) * flag
                     sat = jnp.concatenate([sat_ref[block, s * SLAB + l] for l in levels[m]], axis=1)
                     gain = gain + grow[48 * s : 48 * s + HALF] * sat
                     for half, l in enumerate(levels[m]):
@@ -451,7 +499,7 @@
 def accumulators():
     kinds = []
     for m in range(2):
-        kinds += [pltpu.ACC(m)((rows, 2 * LANES), F32) for rows in (64,) * DEPTH + (96, 96)]
+        kinds += [pltpu.ACC(m)((rows, 2 * LANES), F32) for rows in (64,) * DEPTH + (32, 96, 96)]
     return kinds
 
 
@@ -499,7 +547,7 @@
         in_specs=[SMEM] + [VMEM] * 5,
         out_specs=[VMEM] * 5,
         out_shape=[
-            shaped((BINS, 64, LANES), BF16),
+            shaped((BLOCKS, 64, LANES), BF16),
             shaped((2, 96, LANES), BF16),
             level_shape,
             level_shape,

time: 62.5 us -> 61.3 us (0.981)
  the two profiles are of different devices: /device:TPU:173 before, /device:TPU:137 now
where the time goes in v4:
time: 61.3 us; the launch traced here: 61 us
  starting transfers between devices  36.2 us (59%)
  Pallas kernels  18.4 us (30%)
  waiting for transfers between devices  6.31 us (10%)
    ppermute x5, starting transfers between devices, scan(): lax.ppermute(send, 'lat', between(pairs))  14.8 us
    ppermute x4, starting transfers between devices, scan(): got = [lax.ppermute(flux, 'lat', between(pairs)) for pairs in own]  13.1 us
    pallas_call x1, Pallas kernels, local(): pl.pallas_call(first_kernel, in_specs=[SMEM] + [VMEM] * 8, out_specs=[VME...  6.53 us
    pallas_call x1, Pallas kernels, local(): pl.pallas_call(second_kernel, in_specs=[VMEM] * 13, out_specs=[VMEM] * 2,...  6.3 us
    ppermute x1, starting transfers between devices, local(): got = lax.ppermute(send, 'lat', swap)  5.7 us
    ppermute x4, waiting for transfers between devices, scan(): got = [lax.ppermute(flux, 'lat', between(pairs)) for pairs in own]  3.47 us
    ppermute x1, starting transfers between devices, local(): other = lax.ppermute(sent, 'lat', swap)  2.58 us
    ppermute x5, waiting for transfers between devices, scan(): lax.ppermute(send, 'lat', between(pairs))  1.52 us
  transfers between devices with their start and end apart: 11, of which 5 were waited for; matrix products, arithmetic and copies ran while one was open for 0% of the time, Pallas kernels for 4%

profile of v4, /device:TPU:137, one launch (start us, length us, event | category | flops | bytes accessed | tf_op | source)
XLA Modules:
  0.0 61.0 jit_solution(16386707269790077254)
XLA Ops:
  0.0 1.5 %load_arguments.1 = (bf16[2,34,8,384]{3,2,1,0:T(8,128)(2,1)S(1)}, bf16[2,34,8,384]{3,2,1,0:T(8,128)(2,1)S(1)}, s32[5,128]{1,0:T(8,128)S(1)}, bf16[33,33,33]{2,1,...) custom-call(s32[1]{0:T(128)} %bitcast.index_ref, ...), custom_call_target="tpu_custom_call" | custom-call | tf_op jit(solution)/shard_map/load_arguments/pallas_call | solution.py:516
  1.5 2.6 %collective-permute-start = (bf16[2,34,8,384]{3,2,1,0:T(8,128)(2,1)S(1)}, bf16[2,34,8,384]{3,2,1,0:T(8,128)(2,1)S(1)}, u32[]{:S(2)}, u32[]{:S(2)}) collective-permute-start(bf16[2,34,8,384]{3,2,1,0:T(8,128)(2,1)S(1)} %get-tuple-element.33), channel_id=1, source_target_pairs={{0,1},{1,0},{2,3},{3,2},{4,5},{5,4},{6,7},{7,6},{8,9},{9,8},{10,11... | collective-permute-start | bytes 1253384 | tf_op jit(solution)/shard_map/ppermute | solution.py:537
  4.1 0.9 %tables.1 = (bf16[30,64,128]{2,1,0:T(8,128)(2,1)S(1)}, bf16[2,96,128]{2,1,0:T(8,128)(2,1)S(1)}, f32[24,80,128]{2,1,0:T(8,128)S(1)}, f32[24,80,128]{2,1,0:T(8,128)S(1)}, f32[9,80,128]{2,1,0:T(8,128)S(1)}) custom-call(s32[1]{0:T(128)} %bitcast.index_ref, bf16[33,33,33]{2,1,0:T(8,128)(2,1)S(1)} %get-tuple-element.34.pair_ref, ...), custom_call_target="tpu_custom_call" | custom-call | flops 1000000 | bytes 8000000 | tf_op jit(solution)/shard_map/tables/pallas_call | solution.py:545
  5.0 0.5 collective-permute-done.other_ref
  5.4 6.5 %first_substep.1 = (f32[5,8,80,128]{3,2,1,0:T(8,128)S(1)}, bf16[168,128]{1,0:T(8,128)(2,1)S(1)}, f32[3200,128]{1,0:T(8,128)S(1)}, f32[5,16,1,128]{3,2,1,0:T(1,128)S(1)}, f32[5,1,128]{2,1,0:T(1,128)S(1)}) custom-call(s32[1]{0:T(128)} %bitcast.index_ref, bf16[2,34,8,384]{3,2,1,0:T(8,128)(2,1)S(1)} %get-tuple-element.31.own_ref, ...), custom_call_target="tpu_custom_call" | custom-call | flops 1874329600 | bytes 4000000 | tf_op jit(solution)/shard_map/first_substep/pallas_call | solution.py:565
  12.0 1.9 %collective-permute-start.2 = (bf16[168,128]{1,0:T(8,128)(2,1)S(1)}, bf16[168,128]{1,0:T(8,128)(2,1)S(1)}, u32[]{:S(2)}, u32[]{:S(2)}) collective-permute-start(bf16[168,128]{1,0:T(8,128)(2,1)S(1)} %get-tuple-element.45.flux_ref), channel_id=1, source_target_pairs={{0,4},{1,5},{2,0},{3,1},{4,2},{5,3},{10,14},{11,15},{16,20},{17,21... | collective-permute-start | bytes 129032 | tf_op jit(solution)/shard_map/ppermute | solution.py:597
  13.9 4.3 %collective-permute-start.1 = (bf16[168,128]{1,0:T(8,128)(2,1)S(1)}, bf16[168,128]{1,0:T(8,128)(2,1)S(1)}, u32[]{:S(2)}, u32[]{:S(2)}) collective-permute-start(bf16[168,128]{1,0:T(8,128)(2,1)S(1)} %get-tuple-element.45.flux_ref), channel_id=1, source_target_pairs={{0,2},{1,3},{2,4},{3,5},{4,0},{5,1},{6,8},{7,9},{8,6},{9,7},{10,12... | collective-permute-start | bytes 129032 | tf_op jit(solution)/shard_map/ppermute | solution.py:597
  18.2 1.2 %scan_weights.1 = (f32[24,80,128]{2,1,0:T(8,128)S(1)}, f32[10,168,128]{2,1,0:T(8,128)S(1)}) custom-call(s32[1]{0:T(128)} %bitcast.index_ref, f32[2,33]{1,0:T(2,128)S(1)} %get-tuple-element.37.fall_ref, f32[1,128]{1,0:T(1,128)S(1)} %get-tuple-element.38.dens_ref, f32[24,80,128]{2,1,0:T(8,128)S(1)} %get-tuple-element.41.courant_ref, ...), custom_call_target="tpu_custom_call" | custom-call | flops 1000000 | bytes 8000000 | tf_op jit(solution)/shard_map/scan_weights/pallas_call | solution.py:581
  19.4 0.0 collective-permute-done.2.got2_ref
  19.4 0.0 collective-permute-done.1.got1_ref
  19.5 6.2 %collective-permute-start.4 = (bf16[168,128]{1,0:T(8,128)(2,1)S(1)}, bf16[168,128]{1,0:T(8,128)(2,1)S(1)}, u32[]{:S(2)}, u32[]{:S(2)}) collective-permute-start(bf16[168,128]{1,0:T(8,128)(2,1)S(1)} %get-tuple-element.48), channel_id=1, source_target_pairs={{2,6},{3,7},{4,8},{5,9},{6,10},{7,11},{0,12},{1,13},{8,14},{9,15},... | collective-permute-start | bytes 129032 | tf_op jit(solution)/shard_map/ppermute | solution.py:606
  25.7 0.7 %collective-permute-start.3 = (bf16[168,128]{1,0:T(8,128)(2,1)S(1)}, bf16[168,128]{1,0:T(8,128)(2,1)S(1)}, u32[]{:S(2)}, u32[]{:S(2)}) collective-permute-start(bf16[168,128]{1,0:T(8,128)(2,1)S(1)} %get-tuple-element.48), channel_id=1, source_target_pairs={{0,10},{1,11},{8,12},{9,13},{2,14},{3,15},{16,26},{17,27},{24,28},... | collective-permute-start | bytes 129032 | tf_op jit(solution)/shard_map/ppermute | solution.py:606
  26.4 0.4 collective-permute-done.4.near_ref
  26.8 0.0 collective-permute-done.3.far_ref
  26.8 6.3 %second_substep.1 = (f32[5,8,80,128]{3,2,1,0:T(8,128)S(1)}, bf16[168,128]{1,0:T(8,128)(2,1)S(1)}) custom-call(f32[5,8,80,128]{3,2,1,0:T(8,128)S(1)} %get-tuple-element.44.state_in, f32[168,128]{1,0:T(8,128)S(1)} %get-tuple-element.47.prefix_ref, bf16[168,128]{1,0:T(8,128)(2,1)S(1)} %collective-permute-done.3.far_ref, ...), custom_call_target="tpu_custom_call" | custom-call | flops 1874329600 | bytes 4000000 | tf_op jit(solution)/shard_map/second_substep/pallas_call | solution.py:608
  33.1 5.6 %collective-permute-start.6 = (bf16[168,128]{1,0:T(8,128)(2,1)S(1)}, bf16[168,128]{1,0:T(8,128)(2,1)S(1)}, u32[]{:S(2)}, u32[]{:S(2)}) collective-permute-start(bf16[168,128]{1,0:T(8,128)(2,1)S(1)} %get-tuple-element.54.flux_ref), channel_id=1, source_target_pairs={{0,4},{1,5},{4,2},{5,3},{10,14},{11,15},{16,20},{17,21},{20,18},{2... | collective-permute-start | bytes 129032 | tf_op jit(solution)/shard_map/ppermute | solution.py:597
  38.8 1.3 %collective-permute-start.5 = (bf16[168,128]{1,0:T(8,128)(2,1)S(1)}, bf16[168,128]{1,0:T(8,128)(2,1)S(1)}, u32[]{:S(2)}, u32[]{:S(2)}) collective-permute-start(bf16[168,128]{1,0:T(8,128)(2,1)S(1)} %get-tuple-element.54.flux_ref), channel_id=1, source_target_pairs={{0,2},{1,3},{2,4},{3,5},{6,8},{7,9},{8,6},{9,7},{10,12},{11,13},{1... | collective-permute-start | bytes 129032 | tf_op jit(solution)/shard_map/ppermute | solution.py:597
  40.1 0.0 collective-permute-done.6.got2_ref
  40.1 3.5 %collective-permute-done.5.got1_ref = bf16[168,128]{1,0:T(8,128)(2,1)S(1)} collective-permute-done((bf16[168,128]{1,0:T(8,128)(2,1)S(1)}, bf16[168,128]{1,0:T(8,128)(2,1)S(1)}, u32[]{:S(2)}, u32[]{:S(2)}) %collective-permute-start.5) | collective-permute-done | bytes 43040 | tf_op jit(solution)/shard_map/ppermute | solution.py:597
  43.6 3.5 %collective-permute-start.9 = (bf16[168,128]{1,0:T(8,128)(2,1)S(1)}, bf16[168,128]{1,0:T(8,128)(2,1)S(1)}, u32[]{:S(2)}, u32[]{:S(2)}) collective-permute-start(bf16[168,128]{1,0:T(8,128)(2,1)S(1)} %get-tuple-element.56), channel_id=1, source_target_pairs={{2,6},{3,7},{4,8},{5,9},{6,10},{7,11},{8,12},{9,13},{18,22},{19,23... | collective-permute-start | bytes 129032 | tf_op jit(solution)/shard_map/ppermute | solution.py:606
  47.1 2.2 %collective-permute-start.8 = (bf16[168,128]{1,0:T(8,128)(2,1)S(1)}, bf16[168,128]{1,0:T(8,128)(2,1)S(1)}, u32[]{:S(2)}, u32[]{:S(2)}) collective-permute-start(bf16[168,128]{1,0:T(8,128)(2,1)S(1)} %get-tuple-element.56), channel_id=1, source_target_pairs={{2,14},{3,15},{4,10},{5,11},{18,30},{19,31},{20,26},{21,27},{34,46... | collective-permute-start | bytes 129032 | tf_op jit(solution)/shard_map/ppermute | solution.py:606
  49.3 2.1 %collective-permute-start.7 = (bf16[168,128]{1,0:T(8,128)(2,1)S(1)}, bf16[168,128]{1,0:T(8,128)(2,1)S(1)}, u32[]{:S(2)}, u32[]{:S(2)}) collective-permute-start(bf16[168,128]{1,0:T(8,128)(2,1)S(1)} %get-tuple-element.56), channel_id=1, source_target_pairs={{4,12},{5,13},{8,14},{9,15},{20,28},{21,29},{24,30},{25,31},{36,44... | collective-permute-start | bytes 129032 | tf_op jit(solution)/shard_map/ppermute | solution.py:606
  51.5 0.0 collective-permute-done.9.near_ref
  51.5 0.0 collective-permute-done.8.far_ref
  51.5 1.1 %collective-permute-done.7.farther_ref = bf16[168,128]{1,0:T(8,128)(2,1)S(1)} collective-permute-done((bf16[168,128]{1,0:T(8,128)(2,1)S(1)}, bf16[168,128]{1,0:T(8,128)(2,1)S(1)}, u32[]{:S(2)}, u32[]{:S(2)}) %collective-permute-start.7) | collective-permute-done | bytes 43040 | tf_op jit(solution)/shard_map/ppermute | solution.py:606
  52.6 0.5 tendencies_sent.1
  53.1 5.7 %collective-permute-start.10 = (bf16[2,33,8,384]{3,2,1,0:T(8,128)(2,1)S(1)}, bf16[2,33,8,384]{3,2,1,0:T(8,128)(2,1)S(1)}, u32[]{:S(2)}, u32[]{:S(2)}) collective-permute-start(bf16[2,33,8,384]{3,2,1,0:T(8,128)(2,1)S(1)} %tendencies_sent.1), channel_id=1, source_target_pairs={{0,1},{1,0},{2,3},{3,2},{4,5},{5,4},{6,7},{7,6},{8,9},{9,8},{10,11... | collective-permute-start | bytes 1216520 | tf_op jit(solution)/shard_map/ppermute | solution.py:636
  58.8 0.5 tendencies_kept.1.keep_ref
  59.3 0.9 %collective-permute-done.10.got_ref = bf16[2,33,8,384]{3,2,1,0:T(8,128)(2,1)S(1)} collective-permute-done((bf16[2,33,8,384]{3,2,1,0:T(8,128)(2,1)S(1)}, bf16[2,33,8,384]{3,2,1,0:T(8,128)(2,1)S(1)}, u32[]{:S(2)}, u32[]{:S(2)}) %collective-permute-start.10) | collective-permute-done | bytes 405536 | tf_op jit(solution)/shard_map/ppermute | solution.py:636
  60.2 0.9 %merge_slabs.1 = bf16[2,33,8,640]{3,2,1,0:T(8,128)(2,1)} custom-call(s32[1]{0:T(128)} %bitcast.index_ref, bf16[2,33,8,384]{3,2,1,0:T(8,128)(2,1)S(1)} %tendencies_kept.1.keep_ref, bf16[2,33,8,384]{3,2,1,0:T(8,128)(2,1)S(1)} %collective-permute-done.10.got_ref), custom_call_target="tpu_custom_call" | custom-call | flops 1000000 | bytes 8000000 | tf_op jit(solution)/shard_map/merge_slabs/pallas_call | solution.py:637
  (2 shorter events, 0.1 us)
Async XLA Ops:
  1.5 4.0 %collective-permute-start = (bf16[2,34,8,384]{3,2,1,0:T(8,128)(2,1)S(1)}, bf16[2,34,8,384]{3,2,1,0:T(8,128)(2,1)S(1)}, u32[]{:S(2)}, u32[]{:S(2)}) collective-permute-start(bf16[2,34,8,384]{3,2,1,0:T(8,128)(2,1)S(1)} %get-tuple-element.33), channel_id=1, source_target_pairs={{0,1},{1,0},{2,3},{3,2},{4,5},{5,4},{6,7},{7,6},{8,9},{9,8},{10,11... | collective-permute-start | bytes 1253384 | tf_op jit(solution)/shard_map/ppermute | solution.py:537
  12.0 7.4 %collective-permute-start.2 = (bf16[168,128]{1,0:T(8,128)(2,1)S(1)}, bf16[168,128]{1,0:T(8,128)(2,1)S(1)}, u32[]{:S(2)}, u32[]{:S(2)}) collective-permute-start(bf16[168,128]{1,0:T(8,128)(2,1)S(1)} %get-tuple-element.45.flux_ref), channel_id=1, source_target_pairs={{0,4},{1,5},{2,0},{3,1},{4,2},{5,3},{10,14},{11,15},{16,20},{17,21... | collective-permute-start | bytes 129032 | tf_op jit(solution)/shard_map/ppermute | solution.py:597
  13.9 5.5 %collective-permute-start.1 = (bf16[168,128]{1,0:T(8,128)(2,1)S(1)}, bf16[168,128]{1,0:T(8,128)(2,1)S(1)}, u32[]{:S(2)}, u32[]{:S(2)}) collective-permute-start(bf16[168,128]{1,0:T(8,128)(2,1)S(1)} %get-tuple-element.45.flux_ref), channel_id=1, source_target_pairs={{0,2},{1,3},{2,4},{3,5},{4,0},{5,1},{6,8},{7,9},{8,6},{9,7},{10,12... | collective-permute-start | bytes 129032 | tf_op jit(solution)/shard_map/ppermute | solution.py:597
  19.5 7.3 %collective-permute-start.4 = (bf16[168,128]{1,0:T(8,128)(2,1)S(1)}, bf16[168,128]{1,0:T(8,128)(2,1)S(1)}, u32[]{:S(2)}, u32[]{:S(2)}) collective-permute-start(bf16[168,128]{1,0:T(8,128)(2,1)S(1)} %get-tuple-element.48), channel_id=1, source_target_pairs={{2,6},{3,7},{4,8},{5,9},{6,10},{7,11},{0,12},{1,13},{8,14},{9,15},... | collective-permute-start | bytes 129032 | tf_op jit(solution)/shard_map/ppermute | solution.py:606
  25.7 1.1 %collective-permute-start.3 = (bf16[168,128]{1,0:T(8,128)(2,1)S(1)}, bf16[168,128]{1,0:T(8,128)(2,1)S(1)}, u32[]{:S(2)}, u32[]{:S(2)}) collective-permute-start(bf16[168,128]{1,0:T(8,128)(2,1)S(1)} %get-tuple-element.48), channel_id=1, source_target_pairs={{0,10},{1,11},{8,12},{9,13},{2,14},{3,15},{16,26},{17,27},{24,28},... | collective-permute-start | bytes 129032 | tf_op jit(solution)/shard_map/ppermute | solution.py:606
  33.1 6.9 %collective-permute-start.6 = (bf16[168,128]{1,0:T(8,128)(2,1)S(1)}, bf16[168,128]{1,0:T(8,128)(2,1)S(1)}, u32[]{:S(2)}, u32[]{:S(2)}) collective-permute-start(bf16[168,128]{1,0:T(8,128)(2,1)S(1)} %get-tuple-element.54.flux_ref), channel_id=1, source_target_pairs={{0,4},{1,5},{4,2},{5,3},{10,14},{11,15},{16,20},{17,21},{20,18},{2... | collective-permute-start | bytes 129032 | tf_op jit(solution)/shard_map/ppermute | solution.py:597
  38.8 4.8 %collective-permute-start.5 = (bf16[168,128]{1,0:T(8,128)(2,1)S(1)}, bf16[168,128]{1,0:T(8,128)(2,1)S(1)}, u32[]{:S(2)}, u32[]{:S(2)}) collective-permute-start(bf16[168,128]{1,0:T(8,128)(2,1)S(1)} %get-tuple-element.54.flux_ref), channel_id=1, source_target_pairs={{0,2},{1,3},{2,4},{3,5},{6,8},{7,9},{8,6},{9,7},{10,12},{11,13},{1... | collective-permute-start | bytes 129032 | tf_op jit(solution)/shard_map/ppermute | solution.py:597
  43.6 7.9 %collective-permute-start.9 = (bf16[168,128]{1,0:T(8,128)(2,1)S(1)}, bf16[168,128]{1,0:T(8,128)(2,1)S(1)}, u32[]{:S(2)}, u32[]{:S(2)}) collective-permute-start(bf16[168,128]{1,0:T(8,128)(2,1)S(1)} %get-tuple-element.56), channel_id=1, source_target_pairs={{2,6},{3,7},{4,8},{5,9},{6,10},{7,11},{8,12},{9,13},{18,22},{19,23... | collective-permute-start | bytes 129032 | tf_op jit(solution)/shard_map/ppermute | solution.py:606
  47.1 4.4 %collective-permute-start.8 = (bf16[168,128]{1,0:T(8,128)(2,1)S(1)}, bf16[168,128]{1,0:T(8,128)(2,1)S(1)}, u32[]{:S(2)}, u32[]{:S(2)}) collective-permute-start(bf16[168,128]{1,0:T(8,128)(2,1)S(1)} %get-tuple-element.56), channel_id=1, source_target_pairs={{2,14},{3,15},{4,10},{5,11},{18,30},{19,31},{20,26},{21,27},{34,46... | collective-permute-start | bytes 129032 | tf_op jit(solution)/shard_map/ppermute | solution.py:606
  49.3 3.2 %collective-permute-start.7 = (bf16[168,128]{1,0:T(8,128)(2,1)S(1)}, bf16[168,128]{1,0:T(8,128)(2,1)S(1)}, u32[]{:S(2)}, u32[]{:S(2)}) collective-permute-start(bf16[168,128]{1,0:T(8,128)(2,1)S(1)} %get-tuple-element.56), channel_id=1, source_target_pairs={{4,12},{5,13},{8,14},{9,15},{20,28},{21,29},{24,30},{25,31},{36,44... | collective-permute-start | bytes 129032 | tf_op jit(solution)/shard_map/ppermute | solution.py:606
  53.1 7.0 %collective-permute-start.10 = (bf16[2,33,8,384]{3,2,1,0:T(8,128)(2,1)S(1)}, bf16[2,33,8,384]{3,2,1,0:T(8,128)(2,1)S(1)}, u32[]{:S(2)}, u32[]{:S(2)}) collective-permute-start(bf16[2,33,8,384]{3,2,1,0:T(8,128)(2,1)S(1)} %tendencies_sent.1), channel_id=1, source_target_pairs={{0,1},{1,0},{2,3},{3,2},{4,5},{5,4},{6,7},{7,6},{8,9},{9,8},{10,11... | collective-permute-start | bytes 1216520 | tf_op jit(solution)/shard_map/ppermute | solution.py:636

commit v5 on v4

--- a/solution.py
+++ b/solution.py
@@ -29,12 +29,13 @@
 SUMS = FIRST_SCAN[1] + LAST_SCAN[1]
 DEVS = 2 * CHIPS
 FLAT = 168
-DEPTH = 10
-SQUARE = tuple(range(24, 32))
+DEPTH = 13
+SQUARE = tuple(range(16, 32))
 SINGLES = tuple(i for i in range(BINS) if i not in SQUARE)
 PAIRS = tuple(zip(SQUARE[::2], SQUARE[1::2]))
 BLOCKS = len(SINGLES) + len(PAIRS) + 1
 PRODUCTS = 48
+TURNS = (0, 1, 2, 3, 4), (5, 6, 7, 8)
 F32 = jnp.float32
 BF16 = jnp.bfloat16
 
@@ -168,12 +169,6 @@
         for k in range(BINS - 1):
             wide_ref[HALF * k : HALF * (k + 1), :] = padded(source[k].astype(F32), HALF, LANES)
         if at == 0:
-            products = jnp.zeros((32, LANES), F32)
-            for i in range(size):
-                rows = wide_ref[pl.ds(low + i, 32, stride=HALF), :]
-                products = products + pltpu.roll(jnp.where(in_square, rows, 0.0), PRODUCTS + size * i - low, 1)
-            main_ref[BLOCKS - 1, :32, :] = products.astype(BF16)
-            main_ref[BLOCKS - 1, 32:, :] = jnp.zeros((32, LANES), BF16)
             for first in range(0, BINS - 1, LANES // size):
                 ks = range(first, min(first + LANES // size, BINS - 1))
                 turn = jnp.concatenate([wide_ref[HALF * k + low : HALF * k + low + size, :] for k in ks], axis=0).T
@@ -182,6 +177,16 @@
                     extra = pltpu.roll(turn[:HALF], shift, 1) if shift else turn[:HALF]
                     rows = slice(HALF * k, HALF * (k + 1))
                     wide_ref[rows, :] = wide_ref[rows, :] + jnp.where(in_square, extra, 0.0)
+            for half, turns in enumerate(TURNS):
+                products = jnp.zeros((32, LANES), F32)
+                for i in range(size):
+                    rows = wide_ref[pl.ds(low + i, 32, stride=HALF), :]
+                    for n, r in enumerate(turns):
+                        if 2 * r < size or i < size // 2:
+                            to, there = PRODUCTS + size * n + i, low + (i + r) % size
+                            moved = pltpu.roll(rows, (to - there) % LANES, 1) if to != there else rows
+                            products = jnp.where(lane == to, moved * (0.5 if r == 0 else 1.0), products)
+                main_ref[BLOCKS - 1, 32 * half : 32 * (half + 1), :] = products.astype(BF16)
             for j, i in enumerate(SINGLES):
                 main_ref[j, :32, :] = wide_ref[pl.ds(i, 32, stride=HALF), :].astype(BF16)
         else:
@@ -189,9 +194,10 @@
             places += [(len(SINGLES) + n, 32 * half, i) for n, pair in enumerate(PAIRS) for half, i in enumerate(pair)]
             for j, row, i in places:
                 main_ref[j, row : row + 32, :] = wide_ref[pl.ds(i, 32, stride=HALF), :].astype(BF16)
-        rest_ref[0, 48 * at : 48 * (at + 1), :] = padded(source[BINS - 1].astype(F32), 48, LANES).astype(BF16)
-        grow = slim_ref[pl.ds(at, BINS, stride=2), :]
-        rest_ref[1, 48 * at : 48 * (at + 1), :] = padded(grow, 48, LANES).astype(BF16)
+    tails = [padded(source[BINS - 1].astype(F32), HALF, LANES) for source in (pair_ref, rime_ref)]
+    grow = [padded(slim_ref[pl.ds(at, BINS, stride=2), :], HALF, LANES) for at in range(2)]
+    for at, halves in enumerate((tails, grow)):
+        rest_ref[at] = two_sided(jnp.concatenate(halves, axis=0)).astype(BF16)
 
 
 def two_sided(block):
@@ -221,24 +227,27 @@
         accs = (accs[: DEPTH + 3], accs[DEPTH + 3 :])
 
         def push(spot):
-            empty = jnp.zeros((LANES - 48, 2 * LANES), BF16)
             for m in range(2):
-                liquid = padded(wide(round_ref, spot, slice(0, HALF), m), 48, 2 * LANES).astype(BF16)
                 square = wide(round_ref, spot, slice(SQUARE[0], SQUARE[-1] + 1), m)
-                products = [square * wide(round_ref, spot, slice(i, i + 1), m) for i in SQUARE]
-                products = padded(jnp.concatenate(products, axis=0), LANES - PRODUCTS, 2 * LANES).astype(BF16)
-                frozen = padded(wide(round_ref, spot, slice(HALF, ROWS), m), 48, 2 * LANES).astype(BF16)
-                pltpu.matmul_push_rhs(jnp.concatenate([liquid, products, frozen, empty], axis=0), 0, m)
+                operand = []
+                for half, turns in enumerate(TURNS):
+                    linear = wide(round_ref, spot, slice(HALF * half, HALF * (half + 1)), m)
+                    pieces = [padded(linear, PRODUCTS, 2 * LANES)]
+                    for r in turns:
+                        other = pltpu.roll(square, len(SQUARE) - r, 0) if r else square
+                        pieces.append((square * other)[: len(SQUARE) if 2 * r < len(SQUARE) else len(SQUARE) // 2])
+                    operand.append(padded(jnp.concatenate(pieces, axis=0), LANES, 2 * LANES).astype(BF16))
+                pltpu.matmul_push_rhs(jnp.concatenate(operand, axis=0), 0, m)
 
         def issue(j):
             if j >= BLOCKS:
-                lhs = two_sided(rest_ref[j - BLOCKS])
+                lhs = rest_ref[j - BLOCKS]
             elif j < len(SINGLES):
                 lhs = two_sided(main_ref[j])
             elif j < BLOCKS - 1:
                 lhs = jnp.concatenate([jnp.zeros((64, LANES), BF16), main_ref[j]], axis=1)
             else:
-                lhs = jnp.concatenate([main_ref[j, :32, :], jnp.zeros((32, LANES), BF16)], axis=1)
+                lhs = jnp.concatenate([main_ref[j, :32, :], main_ref[j, 32:, :]], axis=1)
             for m in range(2):
                 pltpu.matmul_acc_lhs(place_of(m, j), lhs, load_staged_rhs=0 if j == 0 else None)
 
@@ -278,11 +287,11 @@
                 grow = pltpu.matmul_pop(place_of(m, BLOCKS + 1))
                 liquid = wide(round_ref, spot, slice(0, HALF), m)
                 for s in range(2):
-                    tail = jnp.sum(last[48 * s : 48 * s + HALF] * liquid, axis=0, keepdims=True)
+                    tail = jnp.sum(last[HALF * s : HALF * (s + 1)] * liquid, axis=0, keepdims=True)
                     tail = padded(tail, 8, 2 * LANES)
                     gain = jnp.concatenate([sums[m][s], tail], axis=0) * flag
                     sat = jnp.concatenate([sat_ref[block, s * SLAB + l] for l in levels[m]], axis=1)
-                    gain = gain + grow[48 * s : 48 * s + HALF] * sat
+                    gain = gain + grow[HALF * s : HALF * (s + 1)] * sat
                     for half, l in enumerate(levels[m]):
                         rows = slice(HALF * s, HALF * (s + 1))
                         part = gain[:, half * LANES : (half + 1) * LANES]
@@ -499,7 +508,7 @@
 def accumulators():
     kinds = []
     for m in range(2):
-        kinds += [pltpu.ACC(m)((rows, 2 * LANES), F32) for rows in (64,) * DEPTH + (32, 96, 96)]
+        kinds += [pltpu.ACC(m)((rows, 2 * LANES), F32) for rows in (64,) * DEPTH + (32, ROWS, ROWS)]
     return kinds
 
 
@@ -548,7 +557,7 @@
         out_specs=[VMEM] * 5,
         out_shape=[
             shaped((BLOCKS, 64, LANES), BF16),
-            shaped((2, 96, LANES), BF16),
+            shaped((2, ROWS, 2 * LANES), BF16),
             level_shape,
             level_shape,
             shaped((SLAB + 1, ROWS, LANES)),

time: 61.3 us -> 60.4 us (0.985)
  the two profiles are of different devices: /device:TPU:137 before, /device:TPU:145 now
where the time goes in v5:
time: 60.4 us; the launch traced here: 60 us
  starting transfers between devices  36.1 us (60%)
  Pallas kernels  17.8 us (29%)
  waiting for transfers between devices  5.91 us (10%)
    ppermute x5, starting transfers between devices, scan(): lax.ppermute(send, 'lat', between(pairs))  14.8 us
    ppermute x4, starting transfers between devices, scan(): got = [lax.ppermute(flux, 'lat', between(pairs)) for pairs in own]  13.1 us
    pallas_call x1, Pallas kernels, local(): pl.pallas_call(first_kernel, in_specs=[SMEM] + [VMEM] * 8, out_specs=[VME...  6.02 us
    pallas_call x1, Pallas kernels, local(): pl.pallas_call(second_kernel, in_specs=[VMEM] * 13, out_specs=[VMEM] * 2,...  5.82 us
    ppermute x1, starting transfers between devices, local(): got = lax.ppermute(send, 'lat', swap)  5.72 us
    ppermute x4, waiting for transfers between devices, scan(): got = [lax.ppermute(flux, 'lat', between(pairs)) for pairs in own]  3.47 us
    ppermute x1, starting transfers between devices, local(): other = lax.ppermute(sent, 'lat', swap)  2.58 us
    ppermute x5, waiting for transfers between devices, scan(): lax.ppermute(send, 'lat', between(pairs))  1.52 us
  transfers between devices with their start and end apart: 11, of which 5 were waited for; matrix products, arithmetic and copies ran while one was open for 0% of the time, Pallas kernels for 5%

profile of v5, /device:TPU:145, one launch (start us, length us, event | category | flops | bytes accessed | tf_op | source)
XLA Modules:
  0.0 60.0 jit_solution(5723769590704755784)
XLA Ops:
  0.0 1.5 %load_arguments.1 = (bf16[2,34,8,384]{3,2,1,0:T(8,128)(2,1)S(1)}, bf16[2,34,8,384]{3,2,1,0:T(8,128)(2,1)S(1)}, s32[5,128]{1,0:T(8,128)S(1)}, bf16[33,33,33]{2,1,...) custom-call(s32[1]{0:T(128)} %bitcast.index_ref, ...), custom_call_target="tpu_custom_call" | custom-call | tf_op jit(solution)/shard_map/load_arguments/pallas_call | solution.py:525
  1.5 2.6 %collective-permute-start = (bf16[2,34,8,384]{3,2,1,0:T(8,128)(2,1)S(1)}, bf16[2,34,8,384]{3,2,1,0:T(8,128)(2,1)S(1)}, u32[]{:S(2)}, u32[]{:S(2)}) collective-permute-start(bf16[2,34,8,384]{3,2,1,0:T(8,128)(2,1)S(1)} %get-tuple-element.33), channel_id=1, source_target_pairs={{0,1},{1,0},{2,3},{3,2},{4,5},{5,4},{6,7},{7,6},{8,9},{9,8},{10,11... | collective-permute-start | bytes 1253384 | tf_op jit(solution)/shard_map/ppermute | solution.py:546
  4.1 1.3 %tables.1 = (bf16[26,64,128]{2,1,0:T(8,128)(2,1)S(1)}, bf16[2,80,256]{2,1,0:T(8,128)(2,1)S(1)}, f32[24,80,128]{2,1,0:T(8,128)S(1)}, f32[24,80,128]{2,1,0:T(8,128)S(1)}, f32[9,80,128]{2,1,0:T(8,128)S(1)}) custom-call(s32[1]{0:T(128)} %bitcast.index_ref, bf16[33,33,33]{2,1,0:T(8,128)(2,1)S(1)} %get-tuple-element.34.pair_ref, ...), custom_call_target="tpu_custom_call" | custom-call | flops 1000000 | bytes 8000000 | tf_op jit(solution)/shard_map/tables/pallas_call | solution.py:554
  5.4 0.1 collective-permute-done.other_ref
  5.4 6.0 %first_substep.1 = (f32[5,8,80,128]{3,2,1,0:T(8,128)S(1)}, bf16[168,128]{1,0:T(8,128)(2,1)S(1)}, f32[3200,128]{1,0:T(8,128)S(1)}, f32[5,16,1,128]{3,2,1,0:T(1,128)S(1)}, f32[5,1,128]{2,1,0:T(1,128)S(1)}) custom-call(s32[1]{0:T(128)} %bitcast.index_ref, bf16[2,34,8,384]{3,2,1,0:T(8,128)(2,1)S(1)} %get-tuple-element.31.own_ref, ...), custom_call_target="tpu_custom_call" | custom-call | flops 1874329600 | bytes 4000000 | tf_op jit(solution)/shard_map/first_substep/pallas_call | solution.py:574
  11.5 1.9 %collective-permute-start.2 = (bf16[168,128]{1,0:T(8,128)(2,1)S(1)}, bf16[168,128]{1,0:T(8,128)(2,1)S(1)}, u32[]{:S(2)}, u32[]{:S(2)}) collective-permute-start(bf16[168,128]{1,0:T(8,128)(2,1)S(1)} %get-tuple-element.45.flux_ref), channel_id=1, source_target_pairs={{0,4},{1,5},{2,0},{3,1},{4,2},{5,3},{10,14},{11,15},{16,20},{17,21... | collective-permute-start | bytes 129032 | tf_op jit(solution)/shard_map/ppermute | solution.py:606
  13.4 4.3 %collective-permute-start.1 = (bf16[168,128]{1,0:T(8,128)(2,1)S(1)}, bf16[168,128]{1,0:T(8,128)(2,1)S(1)}, u32[]{:S(2)}, u32[]{:S(2)}) collective-permute-start(bf16[168,128]{1,0:T(8,128)(2,1)S(1)} %get-tuple-element.45.flux_ref), channel_id=1, source_target_pairs={{0,2},{1,3},{2,4},{3,5},{4,0},{5,1},{6,8},{7,9},{8,6},{9,7},{10,12... | collective-permute-start | bytes 129032 | tf_op jit(solution)/shard_map/ppermute | solution.py:606
  17.7 1.2 %scan_weights.1 = (f32[24,80,128]{2,1,0:T(8,128)S(1)}, f32[10,168,128]{2,1,0:T(8,128)S(1)}) custom-call(s32[1]{0:T(128)} %bitcast.index_ref, f32[2,33]{1,0:T(2,128)S(1)} %get-tuple-element.37.fall_ref, f32[1,128]{1,0:T(1,128)S(1)} %get-tuple-element.38.dens_ref, f32[24,80,128]{2,1,0:T(8,128)S(1)} %get-tuple-element.41.courant_ref, ...), custom_call_target="tpu_custom_call" | custom-call | flops 1000000 | bytes 8000000 | tf_op jit(solution)/shard_map/scan_weights/pallas_call | solution.py:590
  18.9 0.0 collective-permute-done.2.got2_ref
  18.9 0.0 collective-permute-done.1.got1_ref
  19.0 6.2 %collective-permute-start.4 = (bf16[168,128]{1,0:T(8,128)(2,1)S(1)}, bf16[168,128]{1,0:T(8,128)(2,1)S(1)}, u32[]{:S(2)}, u32[]{:S(2)}) collective-permute-start(bf16[168,128]{1,0:T(8,128)(2,1)S(1)} %get-tuple-element.48), channel_id=1, source_target_pairs={{2,6},{3,7},{4,8},{5,9},{6,10},{7,11},{0,12},{1,13},{8,14},{9,15},... | collective-permute-start | bytes 129032 | tf_op jit(solution)/shard_map/ppermute | solution.py:615
  25.2 0.7 %collective-permute-start.3 = (bf16[168,128]{1,0:T(8,128)(2,1)S(1)}, bf16[168,128]{1,0:T(8,128)(2,1)S(1)}, u32[]{:S(2)}, u32[]{:S(2)}) collective-permute-start(bf16[168,128]{1,0:T(8,128)(2,1)S(1)} %get-tuple-element.48), channel_id=1, source_target_pairs={{0,10},{1,11},{8,12},{9,13},{2,14},{3,15},{16,26},{17,27},{24,28},... | collective-permute-start | bytes 129032 | tf_op jit(solution)/shard_map/ppermute | solution.py:615
  25.9 0.4 collective-permute-done.4.near_ref
  26.3 0.0 collective-permute-done.3.far_ref
  26.3 5.8 %second_substep.1 = (f32[5,8,80,128]{3,2,1,0:T(8,128)S(1)}, bf16[168,128]{1,0:T(8,128)(2,1)S(1)}) custom-call(f32[5,8,80,128]{3,2,1,0:T(8,128)S(1)} %get-tuple-element.44.state_in, f32[168,128]{1,0:T(8,128)S(1)} %get-tuple-element.47.prefix_ref, bf16[168,128]{1,0:T(8,128)(2,1)S(1)} %collective-permute-done.3.far_ref, ...), custom_call_target="tpu_custom_call" | custom-call | flops 1874329600 | bytes 4000000 | tf_op jit(solution)/shard_map/second_substep/pallas_call | solution.py:617
  32.1 5.6 %collective-permute-start.6 = (bf16[168,128]{1,0:T(8,128)(2,1)S(1)}, bf16[168,128]{1,0:T(8,128)(2,1)S(1)}, u32[]{:S(2)}, u32[]{:S(2)}) collective-permute-start(bf16[168,128]{1,0:T(8,128)(2,1)S(1)} %get-tuple-element.54.flux_ref), channel_id=1, source_target_pairs={{0,4},{1,5},{4,2},{5,3},{10,14},{11,15},{16,20},{17,21},{20,18},{2... | collective-permute-start | bytes 129032 | tf_op jit(solution)/shard_map/ppermute | solution.py:606
  37.8 1.3 %collective-permute-start.5 = (bf16[168,128]{1,0:T(8,128)(2,1)S(1)}, bf16[168,128]{1,0:T(8,128)(2,1)S(1)}, u32[]{:S(2)}, u32[]{:S(2)}) collective-permute-start(bf16[168,128]{1,0:T(8,128)(2,1)S(1)} %get-tuple-element.54.flux_ref), channel_id=1, source_target_pairs={{0,2},{1,3},{2,4},{3,5},{6,8},{7,9},{8,6},{9,7},{10,12},{11,13},{1... | collective-permute-start | bytes 129032 | tf_op jit(solution)/shard_map/ppermute | solution.py:606
  39.1 0.0 collective-permute-done.6.got2_ref
  39.1 3.5 %collective-permute-done.5.got1_ref = bf16[168,128]{1,0:T(8,128)(2,1)S(1)} collective-permute-done((bf16[168,128]{1,0:T(8,128)(2,1)S(1)}, bf16[168,128]{1,0:T(8,128)(2,1)S(1)}, u32[]{:S(2)}, u32[]{:S(2)}) %collective-permute-start.5) | collective-permute-done | bytes 43040 | tf_op jit(solution)/shard_map/ppermute | solution.py:606
  42.6 3.5 %collective-permute-start.9 = (bf16[168,128]{1,0:T(8,128)(2,1)S(1)}, bf16[168,128]{1,0:T(8,128)(2,1)S(1)}, u32[]{:S(2)}, u32[]{:S(2)}) collective-permute-start(bf16[168,128]{1,0:T(8,128)(2,1)S(1)} %get-tuple-element.56), channel_id=1, source_target_pairs={{2,6},{3,7},{4,8},{5,9},{6,10},{7,11},{8,12},{9,13},{18,22},{19,23... | collective-permute-start | bytes 129032 | tf_op jit(solution)/shard_map/ppermute | solution.py:615
  46.1 2.2 %collective-permute-start.8 = (bf16[168,128]{1,0:T(8,128)(2,1)S(1)}, bf16[168,128]{1,0:T(8,128)(2,1)S(1)}, u32[]{:S(2)}, u32[]{:S(2)}) collective-permute-start(bf16[168,128]{1,0:T(8,128)(2,1)S(1)} %get-tuple-element.56), channel_id=1, source_target_pairs={{2,14},{3,15},{4,10},{5,11},{18,30},{19,31},{20,26},{21,27},{34,46... | collective-permute-start | bytes 129032 | tf_op jit(solution)/shard_map/ppermute | solution.py:615
  48.3 2.1 %collective-permute-start.7 = (bf16[168,128]{1,0:T(8,128)(2,1)S(1)}, bf16[168,128]{1,0:T(8,128)(2,1)S(1)}, u32[]{:S(2)}, u32[]{:S(2)}) collective-permute-start(bf16[168,128]{1,0:T(8,128)(2,1)S(1)} %get-tuple-element.56), channel_id=1, source_target_pairs={{4,12},{5,13},{8,14},{9,15},{20,28},{21,29},{24,30},{25,31},{36,44... | collective-permute-start | bytes 129032 | tf_op jit(solution)/shard_map/ppermute | solution.py:615
  50.5 0.0 collective-permute-done.9.near_ref
  50.5 0.0 collective-permute-done.8.far_ref
  50.5 1.1 %collective-permute-done.7.farther_ref = bf16[168,128]{1,0:T(8,128)(2,1)S(1)} collective-permute-done((bf16[168,128]{1,0:T(8,128)(2,1)S(1)}, bf16[168,128]{1,0:T(8,128)(2,1)S(1)}, u32[]{:S(2)}, u32[]{:S(2)}) %collective-permute-start.7) | collective-permute-done | bytes 43040 | tf_op jit(solution)/shard_map/ppermute | solution.py:615
  51.6 0.5 tendencies_sent.1
  52.1 5.7 %collective-permute-start.10 = (bf16[2,33,8,384]{3,2,1,0:T(8,128)(2,1)S(1)}, bf16[2,33,8,384]{3,2,1,0:T(8,128)(2,1)S(1)}, u32[]{:S(2)}, u32[]{:S(2)}) collective-permute-start(bf16[2,33,8,384]{3,2,1,0:T(8,128)(2,1)S(1)} %tendencies_sent.1), channel_id=1, source_target_pairs={{0,1},{1,0},{2,3},{3,2},{4,5},{5,4},{6,7},{7,6},{8,9},{9,8},{10,11... | collective-permute-start | bytes 1216520 | tf_op jit(solution)/shard_map/ppermute | solution.py:645
  57.8 0.5 tendencies_kept.1.keep_ref
  58.3 0.9 %collective-permute-done.10.got_ref = bf16[2,33,8,384]{3,2,1,0:T(8,128)(2,1)S(1)} collective-permute-done((bf16[2,33,8,384]{3,2,1,0:T(8,128)(2,1)S(1)}, bf16[2,33,8,384]{3,2,1,0:T(8,128)(2,1)S(1)}, u32[]{:S(2)}, u32[]{:S(2)}) %collective-permute-start.10) | collective-permute-done | bytes 405536 | tf_op jit(solution)/shard_map/ppermute | solution.py:645
  59.2 0.9 %merge_slabs.1 = bf16[2,33,8,640]{3,2,1,0:T(8,128)(2,1)} custom-call(s32[1]{0:T(128)} %bitcast.index_ref, bf16[2,33,8,384]{3,2,1,0:T(8,128)(2,1)S(1)} %tendencies_kept.1.keep_ref, bf16[2,33,8,384]{3,2,1,0:T(8,128)(2,1)S(1)} %collective-permute-done.10.got_ref), custom_call_target="tpu_custom_call" | custom-call | flops 1000000 | bytes 8000000 | tf_op jit(solution)/shard_map/merge_slabs/pallas_call | solution.py:646
  (2 shorter events, 0.1 us)
Async XLA Ops:
  1.5 4.0 %collective-permute-start = (bf16[2,34,8,384]{3,2,1,0:T(8,128)(2,1)S(1)}, bf16[2,34,8,384]{3,2,1,0:T(8,128)(2,1)S(1)}, u32[]{:S(2)}, u32[]{:S(2)}) collective-permute-start(bf16[2,34,8,384]{3,2,1,0:T(8,128)(2,1)S(1)} %get-tuple-element.33), channel_id=1, source_target_pairs={{0,1},{1,0},{2,3},{3,2},{4,5},{5,4},{6,7},{7,6},{8,9},{9,8},{10,11... | collective-permute-start | bytes 1253384 | tf_op jit(solution)/shard_map/ppermute | solution.py:546
  11.5 7.4 %collective-permute-start.2 = (bf16[168,128]{1,0:T(8,128)(2,1)S(1)}, bf16[168,128]{1,0:T(8,128)(2,1)S(1)}, u32[]{:S(2)}, u32[]{:S(2)}) collective-permute-start(bf16[168,128]{1,0:T(8,128)(2,1)S(1)} %get-tuple-element.45.flux_ref), channel_id=1, source_target_pairs={{0,4},{1,5},{2,0},{3,1},{4,2},{5,3},{10,14},{11,15},{16,20},{17,21... | collective-permute-start | bytes 129032 | tf_op jit(solution)/shard_map/ppermute | solution.py:606
  13.4 5.5 %collective-permute-start.1 = (bf16[168,128]{1,0:T(8,128)(2,1)S(1)}, bf16[168,128]{1,0:T(8,128)(2,1)S(1)}, u32[]{:S(2)}, u32[]{:S(2)}) collective-permute-start(bf16[168,128]{1,0:T(8,128)(2,1)S(1)} %get-tuple-element.45.flux_ref), channel_id=1, source_target_pairs={{0,2},{1,3},{2,4},{3,5},{4,0},{5,1},{6,8},{7,9},{8,6},{9,7},{10,12... | collective-permute-start | bytes 129032 | tf_op jit(solution)/shard_map/ppermute | solution.py:606
  19.0 7.3 %collective-permute-start.4 = (bf16[168,128]{1,0:T(8,128)(2,1)S(1)}, bf16[168,128]{1,0:T(8,128)(2,1)S(1)}, u32[]{:S(2)}, u32[]{:S(2)}) collective-permute-start(bf16[168,128]{1,0:T(8,128)(2,1)S(1)} %get-tuple-element.48), channel_id=1, source_target_pairs={{2,6},{3,7},{4,8},{5,9},{6,10},{7,11},{0,12},{1,13},{8,14},{9,15},... | collective-permute-start | bytes 129032 | tf_op jit(solution)/shard_map/ppermute | solution.py:615
  25.2 1.1 %collective-permute-start.3 = (bf16[168,128]{1,0:T(8,128)(2,1)S(1)}, bf16[168,128]{1,0:T(8,128)(2,1)S(1)}, u32[]{:S(2)}, u32[]{:S(2)}) collective-permute-start(bf16[168,128]{1,0:T(8,128)(2,1)S(1)} %get-tuple-element.48), channel_id=1, source_target_pairs={{0,10},{1,11},{8,12},{9,13},{2,14},{3,15},{16,26},{17,27},{24,28},... | collective-permute-start | bytes 129032 | tf_op jit(solution)/shard_map/ppermute | solution.py:615
  32.1 6.9 %collective-permute-start.6 = (bf16[168,128]{1,0:T(8,128)(2,1)S(1)}, bf16[168,128]{1,0:T(8,128)(2,1)S(1)}, u32[]{:S(2)}, u32[]{:S(2)}) collective-permute-start(bf16[168,128]{1,0:T(8,128)(2,1)S(1)} %get-tuple-element.54.flux_ref), channel_id=1, source_target_pairs={{0,4},{1,5},{4,2},{5,3},{10,14},{11,15},{16,20},{17,21},{20,18},{2... | collective-permute-start | bytes 129032 | tf_op jit(solution)/shard_map/ppermute | solution.py:606
  37.8 4.8 %collective-permute-start.5 = (bf16[168,128]{1,0:T(8,128)(2,1)S(1)}, bf16[168,128]{1,0:T(8,128)(2,1)S(1)}, u32[]{:S(2)}, u32[]{:S(2)}) collective-permute-start(bf16[168,128]{1,0:T(8,128)(2,1)S(1)} %get-tuple-element.54.flux_ref), channel_id=1, source_target_pairs={{0,2},{1,3},{2,4},{3,5},{6,8},{7,9},{8,6},{9,7},{10,12},{11,13},{1... | collective-permute-start | bytes 129032 | tf_op jit(solution)/shard_map/ppermute | solution.py:606
  42.6 7.9 %collective-permute-start.9 = (bf16[168,128]{1,0:T(8,128)(2,1)S(1)}, bf16[168,128]{1,0:T(8,128)(2,1)S(1)}, u32[]{:S(2)}, u32[]{:S(2)}) collective-permute-start(bf16[168,128]{1,0:T(8,128)(2,1)S(1)} %get-tuple-element.56), channel_id=1, source_target_pairs={{2,6},{3,7},{4,8},{5,9},{6,10},{7,11},{8,12},{9,13},{18,22},{19,23... | collective-permute-start | bytes 129032 | tf_op jit(solution)/shard_map/ppermute | solution.py:615
  46.1 4.3 %collective-permute-start.8 = (bf16[168,128]{1,0:T(8,128)(2,1)S(1)}, bf16[168,128]{1,0:T(8,128)(2,1)S(1)}, u32[]{:S(2)}, u32[]{:S(2)}) collective-permute-start(bf16[168,128]{1,0:T(8,128)(2,1)S(1)} %get-tuple-element.56), channel_id=1, source_target_pairs={{2,14},{3,15},{4,10},{5,11},{18,30},{19,31},{20,26},{21,27},{34,46... | collective-permute-start | bytes 129032 | tf_op jit(solution)/shard_map/ppermute | solution.py:615
  48.3 3.2 %collective-permute-start.7 = (bf16[168,128]{1,0:T(8,128)(2,1)S(1)}, bf16[168,128]{1,0:T(8,128)(2,1)S(1)}, u32[]{:S(2)}, u32[]{:S(2)}) collective-permute-start(bf16[168,128]{1,0:T(8,128)(2,1)S(1)} %get-tuple-element.56), channel_id=1, source_target_pairs={{4,12},{5,13},{8,14},{9,15},{20,28},{21,29},{24,30},{25,31},{36,44... | collective-permute-start | bytes 129032 | tf_op jit(solution)/shard_map/ppermute | solution.py:615
  52.1 7.1 %collective-permute-start.10 = (bf16[2,33,8,384]{3,2,1,0:T(8,128)(2,1)S(1)}, bf16[2,33,8,384]{3,2,1,0:T(8,128)(2,1)S(1)}, u32[]{:S(2)}, u32[]{:S(2)}) collective-permute-start(bf16[2,33,8,384]{3,2,1,0:T(8,128)(2,1)S(1)} %tendencies_sent.1), channel_id=1, source_target_pairs={{0,1},{1,0},{2,3},{3,2},{4,5},{5,4},{6,7},{7,6},{8,9},{9,8},{10,11... | collective-permute-start | bytes 1216520 | tf_op jit(solution)/shard_map/ppermute | solution.py:645

commit v6 on v5

--- a/solution.py
+++ b/solution.py
@@ -212,26 +212,26 @@
     )
 
 
-def substep(round_ref, base_ref, state_ref, sat_ref, flag_ref, main_ref, rest_ref):
+def substep(base_ref, state_ref, sat_ref, flag_ref, main_ref, rest_ref):
     steps = 2 * UNITS
 
     def place(step):
         block, first = step // 2, (step % 2) * 4
         return block, [(first + 2 * m, first + 2 * m + 1) for m in range(2)]
 
-    def wide(ref, spot, rows, m):
+    def wide(spot, rows, m):
         block, levels = spot
-        return jnp.concatenate([ref[block, l, rows, :] for l in levels[m]], axis=1)
+        return jnp.concatenate([base_ref[block, l, rows, :] for l in levels[m]], axis=1).astype(BF16).astype(F32)
 
     def scoped(*accs):
         accs = (accs[: DEPTH + 3], accs[DEPTH + 3 :])
 
         def push(spot):
             for m in range(2):
-                square = wide(round_ref, spot, slice(SQUARE[0], SQUARE[-1] + 1), m)
+                square = wide(spot, slice(SQUARE[0], SQUARE[-1] + 1), m)
                 operand = []
                 for half, turns in enumerate(TURNS):
-                    linear = wide(round_ref, spot, slice(HALF * half, HALF * (half + 1)), m)
+                    linear = wide(spot, slice(HALF * half, HALF * (half + 1)), m)
                     pieces = [padded(linear, PRODUCTS, 2 * LANES)]
                     for r in turns:
                         other = pltpu.roll(square, len(SQUARE) - r, 0) if r else square
@@ -265,11 +265,11 @@
                 for m in range(2):
                     term = pltpu.matmul_pop(place_of(m, i))
                     if i < len(SINGLES):
-                        by = wide(round_ref, spot, slice(SINGLES[i], SINGLES[i] + 1), m)
+                        by = wide(spot, slice(SINGLES[i], SINGLES[i] + 1), m)
                         sums[m] = [sums[m][s] + term[32 * s : 32 * (s + 1)] * by for s in range(2)]
                     elif i < BLOCKS - 1:
                         for half, at in enumerate(PAIRS[i - len(SINGLES)]):
-                            by = wide(round_ref, spot, slice(at, at + 1), m)
+                            by = wide(spot, slice(at, at + 1), m)
                             sums[m][1] = sums[m][1] + term[32 * half : 32 * (half + 1)] * by
                     else:
                         sums[m][0] = sums[m][0] + term
@@ -285,7 +285,7 @@
             for m in range(2):
                 last = pltpu.matmul_pop(place_of(m, BLOCKS))
                 grow = pltpu.matmul_pop(place_of(m, BLOCKS + 1))
-                liquid = wide(round_ref, spot, slice(0, HALF), m)
+                liquid = wide(spot, slice(0, HALF), m)
                 for s in range(2):
                     tail = jnp.sum(last[HALF * s : HALF * (s + 1)] * liquid, axis=0, keepdims=True)
                     tail = padded(tail, 8, 2 * LANES)
@@ -424,7 +424,7 @@
             for u in range(UNITS):
                 initial_ref[pl.ds(u * SLAB * ROWS + HALF * s + n, SLAB, stride=ROWS), :] = units[u]
     initial = initial_ref.reshape(UNITS, SLAB, ROWS, LANES)
-    substep(initial, initial, state_ref, sat_ref, flag_ref, main_ref, rest_ref)
+    substep(initial, state_ref, sat_ref, flag_ref, main_ref, rest_ref)
     settle(state_ref, courant_ref, inverse_ref, lower_ref, flux_ref)
 
 
@@ -432,14 +432,12 @@
     state_in, prefix_ref, far_ref, near_ref, weight_ref, sat_ref, flag_ref, main_ref, rest_ref,
     courant_ref, inverse_ref, arrive_ref, lower_ref,
     state_ref, flux_ref,
-    round_ref,
 ):
     def put(u, l, state):
         state_ref[u, l] = state
-        round_ref[u, l] = state.astype(BF16).astype(F32)
 
     with_arrivals(state_in, arrive_ref, arrivals(prefix_ref, (far_ref, near_ref), weight_ref, 5), put)
-    substep(round_ref, state_ref, state_ref, sat_ref, flag_ref, main_ref, rest_ref)
+    substep(state_ref, state_ref, sat_ref, flag_ref, main_ref, rest_ref)
     settle(state_ref, courant_ref, inverse_ref, lower_ref, flux_ref)
 
 
@@ -619,7 +617,6 @@
         in_specs=[VMEM] * 13,
         out_specs=[VMEM] * 2,
         out_shape=[state_shape, flux_shape],
-        scratch_shapes=[pltpu.VMEM((UNITS, SLAB, ROWS, LANES), F32)],
         compiler_params=PARAMS,
         cost_estimate=cost,
         name="second_substep",

time: 60.4 us -> 61.6 us (1.020)
  the two profiles are of different devices: /device:TPU:145 before, /device:TPU:179 now
where the time goes in v6:
time: 61.6 us; the launch traced here: 61.2 us
  starting transfers between devices  36.2 us (59%)
  Pallas kernels  19 us (31%)
  waiting for transfers between devices  5.91 us (10%)
    ppermute x5, starting transfers between devices, scan(): lax.ppermute(send, 'lat', between(pairs))  14.8 us
    ppermute x4, starting transfers between devices, scan(): got = [lax.ppermute(flux, 'lat', between(pairs)) for pairs in own]  13.1 us
    pallas_call x1, Pallas kernels, local(): pl.pallas_call(first_kernel, in_specs=[SMEM] + [VMEM] * 8, out_specs=[VME...  6.58 us
    pallas_call x1, Pallas kernels, local(): pl.pallas_call(second_kernel, in_specs=[VMEM] * 13, out_specs=[VMEM] * 2,...  6.45 us
    ppermute x1, starting transfers between devices, local(): got = lax.ppermute(send, 'lat', swap)  5.72 us
    ppermute x4, waiting for transfers between devices, scan(): got = [lax.ppermute(flux, 'lat', between(pairs)) for pairs in own]  3.47 us
    ppermute x1, starting transfers between devices, local(): other = lax.ppermute(sent, 'lat', swap)  2.58 us
    ppermute x5, waiting for transfers between devices, scan(): lax.ppermute(send, 'lat', between(pairs))  1.52 us
  transfers between devices with their start and end apart: 11, of which 5 were waited for; matrix products, arithmetic and copies ran while one was open for 0% of the time, Pallas kernels for 5%

profile of v6, /device:TPU:179, one launch (start us, length us, event | category | flops | bytes accessed | tf_op | source)
XLA Modules:
  0.0 61.2 jit_solution(2850632634789877552)
XLA Ops:
  0.0 1.5 %load_arguments.1 = (bf16[2,34,8,384]{3,2,1,0:T(8,128)(2,1)S(1)}, bf16[2,34,8,384]{3,2,1,0:T(8,128)(2,1)S(1)}, s32[5,128]{1,0:T(8,128)S(1)}, bf16[33,33,33]{2,1,...) custom-call(s32[1]{0:T(128)} %bitcast.index_ref, ...), custom_call_target="tpu_custom_call" | custom-call | tf_op jit(solution)/shard_map/load_arguments/pallas_call | solution.py:523
  1.5 2.6 %collective-permute-start = (bf16[2,34,8,384]{3,2,1,0:T(8,128)(2,1)S(1)}, bf16[2,34,8,384]{3,2,1,0:T(8,128)(2,1)S(1)}, u32[]{:S(2)}, u32[]{:S(2)}) collective-permute-start(bf16[2,34,8,384]{3,2,1,0:T(8,128)(2,1)S(1)} %get-tuple-element.33), channel_id=1, source_target_pairs={{0,1},{1,0},{2,3},{3,2},{4,5},{5,4},{6,7},{7,6},{8,9},{9,8},{10,11... | collective-permute-start | bytes 1253384 | tf_op jit(solution)/shard_map/ppermute | solution.py:544
  4.1 1.3 %tables.1 = (bf16[26,64,128]{2,1,0:T(8,128)(2,1)S(1)}, bf16[2,80,256]{2,1,0:T(8,128)(2,1)S(1)}, f32[24,80,128]{2,1,0:T(8,128)S(1)}, f32[24,80,128]{2,1,0:T(8,128)S(1)}, f32[9,80,128]{2,1,0:T(8,128)S(1)}) custom-call(s32[1]{0:T(128)} %bitcast.index_ref, bf16[33,33,33]{2,1,0:T(8,128)(2,1)S(1)} %get-tuple-element.34.pair_ref, ...), custom_call_target="tpu_custom_call" | custom-call | flops 1000000 | bytes 8000000 | tf_op jit(solution)/shard_map/tables/pallas_call | solution.py:552
  5.4 0.1 collective-permute-done.other_ref
  5.4 6.6 %first_substep.1 = (f32[5,8,80,128]{3,2,1,0:T(8,128)S(1)}, bf16[168,128]{1,0:T(8,128)(2,1)S(1)}, f32[3200,128]{1,0:T(8,128)S(1)}, f32[5,16,1,128]{3,2,1,0:T(1,128)S(1)}, f32[5,1,128]{2,1,0:T(1,128)S(1)}) custom-call(s32[1]{0:T(128)} %bitcast.index_ref, bf16[2,34,8,384]{3,2,1,0:T(8,128)(2,1)S(1)} %get-tuple-element.31.own_ref, ...), custom_call_target="tpu_custom_call" | custom-call | flops 1874329600 | bytes 4000000 | tf_op jit(solution)/shard_map/first_substep/pallas_call | solution.py:572
  12.0 1.9 %collective-permute-start.2 = (bf16[168,128]{1,0:T(8,128)(2,1)S(1)}, bf16[168,128]{1,0:T(8,128)(2,1)S(1)}, u32[]{:S(2)}, u32[]{:S(2)}) collective-permute-start(bf16[168,128]{1,0:T(8,128)(2,1)S(1)} %get-tuple-element.45.flux_ref), channel_id=1, source_target_pairs={{0,4},{1,5},{2,0},{3,1},{4,2},{5,3},{10,14},{11,15},{16,20},{17,21... | collective-permute-start | bytes 129032 | tf_op jit(solution)/shard_map/ppermute | solution.py:604
  14.0 4.3 %collective-permute-start.1 = (bf16[168,128]{1,0:T(8,128)(2,1)S(1)}, bf16[168,128]{1,0:T(8,128)(2,1)S(1)}, u32[]{:S(2)}, u32[]{:S(2)}) collective-permute-start(bf16[168,128]{1,0:T(8,128)(2,1)S(1)} %get-tuple-element.45.flux_ref), channel_id=1, source_target_pairs={{0,2},{1,3},{2,4},{3,5},{4,0},{5,1},{6,8},{7,9},{8,6},{9,7},{10,12... | collective-permute-start | bytes 129032 | tf_op jit(solution)/shard_map/ppermute | solution.py:604
  18.2 1.2 %scan_weights.1 = (f32[24,80,128]{2,1,0:T(8,128)S(1)}, f32[10,168,128]{2,1,0:T(8,128)S(1)}) custom-call(s32[1]{0:T(128)} %bitcast.index_ref, f32[2,33]{1,0:T(2,128)S(1)} %get-tuple-element.37.fall_ref, f32[1,128]{1,0:T(1,128)S(1)} %get-tuple-element.38.dens_ref, f32[24,80,128]{2,1,0:T(8,128)S(1)} %get-tuple-element.41.courant_ref, ...), custom_call_target="tpu_custom_call" | custom-call | flops 1000000 | bytes 8000000 | tf_op jit(solution)/shard_map/scan_weights/pallas_call | solution.py:588
  19.5 0.0 collective-permute-done.2.got2_ref
  19.5 0.0 collective-permute-done.1.got1_ref
  19.5 6.2 %collective-permute-start.4 = (bf16[168,128]{1,0:T(8,128)(2,1)S(1)}, bf16[168,128]{1,0:T(8,128)(2,1)S(1)}, u32[]{:S(2)}, u32[]{:S(2)}) collective-permute-start(bf16[168,128]{1,0:T(8,128)(2,1)S(1)} %get-tuple-element.48), channel_id=1, source_target_pairs={{2,6},{3,7},{4,8},{5,9},{6,10},{7,11},{0,12},{1,13},{8,14},{9,15},... | collective-permute-start | bytes 129032 | tf_op jit(solution)/shard_map/ppermute | solution.py:613
  25.8 0.7 %collective-permute-start.3 = (bf16[168,128]{1,0:T(8,128)(2,1)S(1)}, bf16[168,128]{1,0:T(8,128)(2,1)S(1)}, u32[]{:S(2)}, u32[]{:S(2)}) collective-permute-start(bf16[168,128]{1,0:T(8,128)(2,1)S(1)} %get-tuple-element.48), channel_id=1, source_target_pairs={{0,10},{1,11},{8,12},{9,13},{2,14},{3,15},{16,26},{17,27},{24,28},... | collective-permute-start | bytes 129032 | tf_op jit(solution)/shard_map/ppermute | solution.py:613
  26.4 0.4 collective-permute-done.4.near_ref
  26.9 0.0 collective-permute-done.3.far_ref
  26.9 6.4 %second_substep.1 = (f32[5,8,80,128]{3,2,1,0:T(8,128)S(1)}, bf16[168,128]{1,0:T(8,128)(2,1)S(1)}) custom-call(f32[5,8,80,128]{3,2,1,0:T(8,128)S(1)} %get-tuple-element.44.state_in, f32[168,128]{1,0:T(8,128)S(1)} %get-tuple-element.47.prefix_ref, bf16[168,128]{1,0:T(8,128)(2,1)S(1)} %collective-permute-done.3.far_ref, ...), custom_call_target="tpu_custom_call" | custom-call | flops 1874329600 | bytes 4000000 | tf_op jit(solution)/shard_map/second_substep/pallas_call | solution.py:615
  33.3 5.6 %collective-permute-start.6 = (bf16[168,128]{1,0:T(8,128)(2,1)S(1)}, bf16[168,128]{1,0:T(8,128)(2,1)S(1)}, u32[]{:S(2)}, u32[]{:S(2)}) collective-permute-start(bf16[168,128]{1,0:T(8,128)(2,1)S(1)} %get-tuple-element.54.flux_ref), channel_id=1, source_target_pairs={{0,4},{1,5},{4,2},{5,3},{10,14},{11,15},{16,20},{17,21},{20,18},{2... | collective-permute-start | bytes 129032 | tf_op jit(solution)/shard_map/ppermute | solution.py:604
  39.0 1.3 %collective-permute-start.5 = (bf16[168,128]{1,0:T(8,128)(2,1)S(1)}, bf16[168,128]{1,0:T(8,128)(2,1)S(1)}, u32[]{:S(2)}, u32[]{:S(2)}) collective-permute-start(bf16[168,128]{1,0:T(8,128)(2,1)S(1)} %get-tuple-element.54.flux_ref), channel_id=1, source_target_pairs={{0,2},{1,3},{2,4},{3,5},{6,8},{7,9},{8,6},{9,7},{10,12},{11,13},{1... | collective-permute-start | bytes 129032 | tf_op jit(solution)/shard_map/ppermute | solution.py:604
  40.3 0.0 collective-permute-done.6.got2_ref
  40.3 3.5 %collective-permute-done.5.got1_ref = bf16[168,128]{1,0:T(8,128)(2,1)S(1)} collective-permute-done((bf16[168,128]{1,0:T(8,128)(2,1)S(1)}, bf16[168,128]{1,0:T(8,128)(2,1)S(1)}, u32[]{:S(2)}, u32[]{:S(2)}) %collective-permute-start.5) | collective-permute-done | bytes 43040 | tf_op jit(solution)/shard_map/ppermute | solution.py:604
  43.8 3.5 %collective-permute-start.9 = (bf16[168,128]{1,0:T(8,128)(2,1)S(1)}, bf16[168,128]{1,0:T(8,128)(2,1)S(1)}, u32[]{:S(2)}, u32[]{:S(2)}) collective-permute-start(bf16[168,128]{1,0:T(8,128)(2,1)S(1)} %get-tuple-element.56), channel_id=1, source_target_pairs={{2,6},{3,7},{4,8},{5,9},{6,10},{7,11},{8,12},{9,13},{18,22},{19,23... | collective-permute-start | bytes 129032 | tf_op jit(solution)/shard_map/ppermute | solution.py:613
  47.3 2.2 %collective-permute-start.8 = (bf16[168,128]{1,0:T(8,128)(2,1)S(1)}, bf16[168,128]{1,0:T(8,128)(2,1)S(1)}, u32[]{:S(2)}, u32[]{:S(2)}) collective-permute-start(bf16[168,128]{1,0:T(8,128)(2,1)S(1)} %get-tuple-element.56), channel_id=1, source_target_pairs={{2,14},{3,15},{4,10},{5,11},{18,30},{19,31},{20,26},{21,27},{34,46... | collective-permute-start | bytes 129032 | tf_op jit(solution)/shard_map/ppermute | solution.py:613
  49.5 2.1 %collective-permute-start.7 = (bf16[168,128]{1,0:T(8,128)(2,1)S(1)}, bf16[168,128]{1,0:T(8,128)(2,1)S(1)}, u32[]{:S(2)}, u32[]{:S(2)}) collective-permute-start(bf16[168,128]{1,0:T(8,128)(2,1)S(1)} %get-tuple-element.56), channel_id=1, source_target_pairs={{4,12},{5,13},{8,14},{9,15},{20,28},{21,29},{24,30},{25,31},{36,44... | collective-permute-start | bytes 129032 | tf_op jit(solution)/shard_map/ppermute | solution.py:613
  51.7 0.0 collective-permute-done.9.near_ref
  51.7 0.0 collective-permute-done.8.far_ref
  51.7 1.1 %collective-permute-done.7.farther_ref = bf16[168,128]{1,0:T(8,128)(2,1)S(1)} collective-permute-done((bf16[168,128]{1,0:T(8,128)(2,1)S(1)}, bf16[168,128]{1,0:T(8,128)(2,1)S(1)}, u32[]{:S(2)}, u32[]{:S(2)}) %collective-permute-start.7) | collective-permute-done | bytes 43040 | tf_op jit(solution)/shard_map/ppermute | solution.py:613
  52.8 0.5 tendencies_sent.1
  53.3 5.7 %collective-permute-start.10 = (bf16[2,33,8,384]{3,2,1,0:T(8,128)(2,1)S(1)}, bf16[2,33,8,384]{3,2,1,0:T(8,128)(2,1)S(1)}, u32[]{:S(2)}, u32[]{:S(2)}) collective-permute-start(bf16[2,33,8,384]{3,2,1,0:T(8,128)(2,1)S(1)} %tendencies_sent.1), channel_id=1, source_target_pairs={{0,1},{1,0},{2,3},{3,2},{4,5},{5,4},{6,7},{7,6},{8,9},{9,8},{10,11... | collective-permute-start | bytes 1216520 | tf_op jit(solution)/shard_map/ppermute | solution.py:642
  59.0 0.5 tendencies_kept.1.keep_ref
  59.5 0.9 %collective-permute-done.10.got_ref = bf16[2,33,8,384]{3,2,1,0:T(8,128)(2,1)S(1)} collective-permute-done((bf16[2,33,8,384]{3,2,1,0:T(8,128)(2,1)S(1)}, bf16[2,33,8,384]{3,2,1,0:T(8,128)(2,1)S(1)}, u32[]{:S(2)}, u32[]{:S(2)}) %collective-permute-start.10) | collective-permute-done | bytes 405536 | tf_op jit(solution)/shard_map/ppermute | solution.py:642
  60.4 0.9 %merge_slabs.1 = bf16[2,33,8,640]{3,2,1,0:T(8,128)(2,1)} custom-call(s32[1]{0:T(128)} %bitcast.index_ref, bf16[2,33,8,384]{3,2,1,0:T(8,128)(2,1)S(1)} %tendencies_kept.1.keep_ref, bf16[2,33,8,384]{3,2,1,0:T(8,128)(2,1)S(1)} %collective-permute-done.10.got_ref), custom_call_target="tpu_custom_call" | custom-call | flops 1000000 | bytes 8000000 | tf_op jit(solution)/shard_map/merge_slabs/pallas_call | solution.py:643
  (2 shorter events, 0.1 us)
Async XLA Ops:
  1.5 4.0 %collective-permute-start = (bf16[2,34,8,384]{3,2,1,0:T(8,128)(2,1)S(1)}, bf16[2,34,8,384]{3,2,1,0:T(8,128)(2,1)S(1)}, u32[]{:S(2)}, u32[]{:S(2)}) collective-permute-start(bf16[2,34,8,384]{3,2,1,0:T(8,128)(2,1)S(1)} %get-tuple-element.33), channel_id=1, source_target_pairs={{0,1},{1,0},{2,3},{3,2},{4,5},{5,4},{6,7},{7,6},{8,9},{9,8},{10,11... | collective-permute-start | bytes 1253384 | tf_op jit(solution)/shard_map/ppermute | solution.py:544
  12.0 7.4 %collective-permute-start.2 = (bf16[168,128]{1,0:T(8,128)(2,1)S(1)}, bf16[168,128]{1,0:T(8,128)(2,1)S(1)}, u32[]{:S(2)}, u32[]{:S(2)}) collective-permute-start(bf16[168,128]{1,0:T(8,128)(2,1)S(1)} %get-tuple-element.45.flux_ref), channel_id=1, source_target_pairs={{0,4},{1,5},{2,0},{3,1},{4,2},{5,3},{10,14},{11,15},{16,20},{17,21... | collective-permute-start | bytes 129032 | tf_op jit(solution)/shard_map/ppermute | solution.py:604
  14.0 5.5 %collective-permute-start.1 = (bf16[168,128]{1,0:T(8,128)(2,1)S(1)}, bf16[168,128]{1,0:T(8,128)(2,1)S(1)}, u32[]{:S(2)}, u32[]{:S(2)}) collective-permute-start(bf16[168,128]{1,0:T(8,128)(2,1)S(1)} %get-tuple-element.45.flux_ref), channel_id=1, source_target_pairs={{0,2},{1,3},{2,4},{3,5},{4,0},{5,1},{6,8},{7,9},{8,6},{9,7},{10,12... | collective-permute-start | bytes 129032 | tf_op jit(solution)/shard_map/ppermute | solution.py:604
  19.5 7.3 %collective-permute-start.4 = (bf16[168,128]{1,0:T(8,128)(2,1)S(1)}, bf16[168,128]{1,0:T(8,128)(2,1)S(1)}, u32[]{:S(2)}, u32[]{:S(2)}) collective-permute-start(bf16[168,128]{1,0:T(8,128)(2,1)S(1)} %get-tuple-element.48), channel_id=1, source_target_pairs={{2,6},{3,7},{4,8},{5,9},{6,10},{7,11},{0,12},{1,13},{8,14},{9,15},... | collective-permute-start | bytes 129032 | tf_op jit(solution)/shard_map/ppermute | solution.py:613
  25.8 1.1 %collective-permute-start.3 = (bf16[168,128]{1,0:T(8,128)(2,1)S(1)}, bf16[168,128]{1,0:T(8,128)(2,1)S(1)}, u32[]{:S(2)}, u32[]{:S(2)}) collective-permute-start(bf16[168,128]{1,0:T(8,128)(2,1)S(1)} %get-tuple-element.48), channel_id=1, source_target_pairs={{0,10},{1,11},{8,12},{9,13},{2,14},{3,15},{16,26},{17,27},{24,28},... | collective-permute-start | bytes 129032 | tf_op jit(solution)/shard_map/ppermute | solution.py:613
  33.3 6.9 %collective-permute-start.6 = (bf16[168,128]{1,0:T(8,128)(2,1)S(1)}, bf16[168,128]{1,0:T(8,128)(2,1)S(1)}, u32[]{:S(2)}, u32[]{:S(2)}) collective-permute-start(bf16[168,128]{1,0:T(8,128)(2,1)S(1)} %get-tuple-element.54.flux_ref), channel_id=1, source_target_pairs={{0,4},{1,5},{4,2},{5,3},{10,14},{11,15},{16,20},{17,21},{20,18},{2... | collective-permute-start | bytes 129032 | tf_op jit(solution)/shard_map/ppermute | solution.py:604
  39.0 4.8 %collective-permute-start.5 = (bf16[168,128]{1,0:T(8,128)(2,1)S(1)}, bf16[168,128]{1,0:T(8,128)(2,1)S(1)}, u32[]{:S(2)}, u32[]{:S(2)}) collective-permute-start(bf16[168,128]{1,0:T(8,128)(2,1)S(1)} %get-tuple-element.54.flux_ref), channel_id=1, source_target_pairs={{0,2},{1,3},{2,4},{3,5},{6,8},{7,9},{8,6},{9,7},{10,12},{11,13},{1... | collective-permute-start | bytes 129032 | tf_op jit(solution)/shard_map/ppermute | solution.py:604
  43.8 7.9 %collective-permute-start.9 = (bf16[168,128]{1,0:T(8,128)(2,1)S(1)}, bf16[168,128]{1,0:T(8,128)(2,1)S(1)}, u32[]{:S(2)}, u32[]{:S(2)}) collective-permute-start(bf16[168,128]{1,0:T(8,128)(2,1)S(1)} %get-tuple-element.56), channel_id=1, source_target_pairs={{2,6},{3,7},{4,8},{5,9},{6,10},{7,11},{8,12},{9,13},{18,22},{19,23... | collective-permute-start | bytes 129032 | tf_op jit(solution)/shard_map/ppermute | solution.py:613
  47.3 4.3 %collective-permute-start.8 = (bf16[168,128]{1,0:T(8,128)(2,1)S(1)}, bf16[168,128]{1,0:T(8,128)(2,1)S(1)}, u32[]{:S(2)}, u32[]{:S(2)}) collective-permute-start(bf16[168,128]{1,0:T(8,128)(2,1)S(1)} %get-tuple-element.56), channel_id=1, source_target_pairs={{2,14},{3,15},{4,10},{5,11},{18,30},{19,31},{20,26},{21,27},{34,46... | collective-permute-start | bytes 129032 | tf_op jit(solution)/shard_map/ppermute | solution.py:613
  49.5 3.2 %collective-permute-start.7 = (bf16[168,128]{1,0:T(8,128)(2,1)S(1)}, bf16[168,128]{1,0:T(8,128)(2,1)S(1)}, u32[]{:S(2)}, u32[]{:S(2)}) collective-permute-start(bf16[168,128]{1,0:T(8,128)(2,1)S(1)} %get-tuple-element.56), channel_id=1, source_target_pairs={{4,12},{5,13},{8,14},{9,15},{20,28},{21,29},{24,30},{25,31},{36,44... | collective-permute-start | bytes 129032 | tf_op jit(solution)/shard_map/ppermute | solution.py:613
  53.3 7.1 %collective-permute-start.10 = (bf16[2,33,8,384]{3,2,1,0:T(8,128)(2,1)S(1)}, bf16[2,33,8,384]{3,2,1,0:T(8,128)(2,1)S(1)}, u32[]{:S(2)}, u32[]{:S(2)}) collective-permute-start(bf16[2,33,8,384]{3,2,1,0:T(8,128)(2,1)S(1)} %tendencies_sent.1), channel_id=1, source_target_pairs={{0,1},{1,0},{2,3},{3,2},{4,5},{5,4},{6,7},{7,6},{8,9},{9,8},{10,11... | collective-permute-start | bytes 1216520 | tf_op jit(solution)/shard_map/ppermute | solution.py:642
